TPU v7x, 32 devices: a whole 2x2x4 slice. The times are simulated.
32 devices in a mesh: row: 4 (over x, core), col: 8 (over z, y).
Axes of the slice: x: 2, y: 2, z: 4, core: 2. Of those that a mesh axis runs over, the one named last changes fastest.
Arguments:
- density_factor: bfloat16 [131072, 256], P(('row', 'col'))
- onsite: float32 [131072], P(('row', 'col')), may hold values from -4 to 4
- neighbour_ids: int32 [256, 8], P(('row', 'col')), may hold values from 0 to 255, as said below
- neighbour_count: int32 [256], P(('row', 'col')), may hold values from 1 to 8, as said below
- coupling_type: int32 [256, 8], P(('row', 'col')), may hold values from 0 to 3
- coupling_blocks: bfloat16 [4, 512, 512], replicated, may hold values from -0.25 to 0.25
- bath_pattern: int32 [256], P(('row', 'col')), may hold values from 0 to 3
- bath_blocks: bfloat16 [4, 512, 512], replicated, may hold values from -0.25 to 0.25
Outputs:
- new_factor: bfloat16 [131072, 256], P(('row', 'col'))
Inputs may be any that keep to these rules, and one draw needn't show every extreme that they name: `neighbour_ids`: every neighbour of block b lies among the 64 blocks that share b's index of row, at most half of 64 blocks from b when that group is taken as a loop, and is never b itself; some block has a neighbour exactly half of 64 blocks away. Only the first neighbour_count[b] slots of block b's lists are used; some block uses all 8.
All inputs are finite; a program needn't handle non-finite values.
Results may differ from a plain program's by a relative error of at most 0.0056.
Values may be sent and summed in bfloat16 or wider, within the bound.
No kernel may reach another device: no remote copies, remote signals or barrier semaphores. Data moves between devices by JAX's collectives and lax.ppermute only.
A program may use at most 192 MiB of HBM per device.

v0:
```python
import jax
import jax.numpy as jnp
from jax import lax
from jax.experimental import pallas as pl
from jax.experimental.pallas import tpu as pltpu
from jax.sharding import PartitionSpec as P

time_step = 0.25
PANEL = 64
SMALLEST_PIVOT = 1 / 64
HIGHEST = lax.Precision.HIGHEST


def bath_kernel(pattern_ref, bath_ref, own_ref, bathed_ref, gram_ref):
    bathed = jnp.dot(bath_ref[0], own_ref[...], preferred_element_type=jnp.float32).astype(jnp.bfloat16)
    bathed_ref[...] = bathed
    part = lax.dot_general(
        bathed, bathed, (((0,), (0,)), ((), ())), preferred_element_type=jnp.float32
    )

    @pl.when(pl.program_id(0) == 0)
    def _():
        gram_ref[...] = part

    @pl.when(pl.program_id(0) > 0)
    def _():
        gram_ref[...] += part


def bath_part(own, bath_pattern, bath_blocks):
    blocks = bath_pattern.shape[0]
    block_rows = bath_blocks.shape[1]
    rows, rank = own.shape
    tile = pl.BlockSpec((block_rows, rank), lambda b, kind: (b, 0))
    return pl.pallas_call(
        bath_kernel,
        grid_spec=pltpu.PrefetchScalarGridSpec(
            num_scalar_prefetch=1,
            grid=(blocks,),
            in_specs=[
                pl.BlockSpec((1, block_rows, block_rows), lambda b, kind: (kind[b], 0, 0)),
                tile,
            ],
            out_specs=[tile, pl.BlockSpec((rank, rank), lambda b, kind: (0, 0))],
        ),
        out_shape=[
            jax.ShapeDtypeStruct((rows, rank), jnp.bfloat16),
            jax.ShapeDtypeStruct((rank, rank), jnp.float32),
        ],
        compiler_params=pltpu.CompilerParams(vmem_limit_bytes=7 * 2**20),
        name="bath",
    )(bath_pattern, bath_blocks, own)


def gather_products(origin_ref, offset_ref, first_ref, count_ref, kind_ref, sources, coupling_ref, held, sems, total):
    blocks, slots = origin_ref.shape
    block_rows = held.shape[2]
    b = pl.program_id(0)
    group = 1
    while group * group < len(sources):
        group += 1

    def copy(source, block, slot):
        start = pl.multiple_of(offset_ref[block, slot] * block_rows, block_rows)
        return pltpu.make_async_copy(
            source.at[pl.ds(start, block_rows), :],
            held.at[lax.rem(block, 2), slot],
            sems.at[lax.rem(block, 2), slot],
        )

    def fetch(block):
        def one(slot, carry):
            origin = origin_ref[block, slot]
            for low in range(0, len(sources), group):
                high = min(low + group, len(sources))

                @pl.when((origin >= low) & (origin < high))
                def _():
                    for place in range(low, high):
                        @pl.when(origin == place)
                        def _():
                            copy(sources[place], block, slot).start()
            return carry

        lax.fori_loop(first_ref[block], first_ref[block] + count_ref[block], one, 0)

    @pl.when(b == 0)
    def _():
        fetch(0)

    @pl.when(b + 1 < blocks)
    def _():
        fetch(b + 1)

    def product(slot):
        copy(sources[0], b, slot).wait()
        return jnp.dot(
            coupling_ref[kind_ref[b, slot]],
            held[lax.rem(b, 2), slot],
            preferred_element_type=jnp.float32,
        )

    first, count = first_ref[b], count_ref[b]

    def add_two(pair, carry):
        slot = first + 2 * pair
        total[...] -= time_step * (product(slot) + product(slot + 1))
        return carry

    lax.fori_loop(0, count // 2, add_two, 0)

    @pl.when(lax.rem(count, 2) == 1)
    def _():
        total[...] -= time_step * product(first + count - 1)


def early_kernel(origin_ref, offset_ref, first_ref, count_ref, kind_ref, *refs):
    sources = refs[:-8]
    coupling_hbm, own_ref, energy_ref, total_ref, coupling, held, sems, coupling_sem = refs[-8:]
    block_rows = own_ref.shape[0]
    load = pltpu.make_async_copy(coupling_hbm, coupling, coupling_sem)

    @pl.when(pl.program_id(0) == 0)
    def _():
        load.start()

    row = energy_ref[pl.ds(pl.program_id(0), 1), :]
    energy = jnp.broadcast_to(row, (8, block_rows)).T[:, :1]
    wide = own_ref[...].astype(jnp.float32)
    total_ref[...] = wide - time_step * (energy * wide)

    @pl.when(pl.program_id(0) == 0)
    def _():
        load.wait()

    gather_products(
        origin_ref, offset_ref, first_ref, count_ref, kind_ref, sources, coupling, held, sems, total_ref
    )


def middle_kernel(origin_ref, offset_ref, first_ref, count_ref, kind_ref, *refs):
    sources = refs[:-5]
    coupling_ref, base_ref, total_ref, held, sems = refs[-5:]
    total_ref[...] = base_ref[...]
    gather_products(
        origin_ref, offset_ref, first_ref, count_ref, kind_ref, sources, coupling_ref, held, sems, total_ref
    )


def late_kernel(origin_ref, offset_ref, first_ref, count_ref, kind_ref, *refs):
    sources = refs[:-8]
    coupling_ref, base_ref, bathed_ref, moved_ref, gram_ref, total, held, sems = refs[-8:]
    b = pl.program_id(0)
    total[...] = base_ref[...]
    gather_products(
        origin_ref, offset_ref, first_ref, count_ref, kind_ref, sources, coupling_ref, held, sems, total
    )
    moved = total[...].astype(jnp.bfloat16)
    moved_ref[...] = moved
    both = jnp.concatenate([moved, bathed_ref[...]], axis=1)
    part = lax.dot_general(
        moved, both, (((0,), (0,)), ((), ())), preferred_element_type=jnp.float32
    )

    @pl.when(b == 0)
    def _():
        gram_ref[...] = part

    @pl.when(b > 0)
    def _():
        gram_ref[...] += part


def early_part(lists, sources, coupling_blocks, own, energy):
    blocks, slots = lists[0].shape
    kinds, block_rows, _ = coupling_blocks.shape
    rows, rank = own.shape
    tile = pl.BlockSpec((block_rows, rank), lambda b, *_: (b, 0))
    return pl.pallas_call(
        early_kernel,
        grid_spec=pltpu.PrefetchScalarGridSpec(
            num_scalar_prefetch=5,
            grid=(blocks,),
            in_specs=[
                *[pl.BlockSpec(memory_space=pltpu.HBM) for _ in sources],
                pl.BlockSpec(memory_space=pltpu.HBM),
                tile,
                pl.BlockSpec((blocks, block_rows), lambda b, *_: (0, 0)),
            ],
            out_specs=tile,
            scratch_shapes=[
                pltpu.VMEM((kinds, block_rows, block_rows), jnp.bfloat16),
                pltpu.VMEM((2, slots, block_rows, rank), jnp.bfloat16),
                pltpu.SemaphoreType.DMA((2, slots)),
                pltpu.SemaphoreType.DMA,
            ],
        ),
        out_shape=jax.ShapeDtypeStruct((rows, rank), jnp.float32),
        compiler_params=pltpu.CompilerParams(vmem_limit_bytes=12 * 2**20),
        cost_estimate=pl.CostEstimate(
            flops=blocks * slots * block_rows * block_rows * rank,
            bytes_accessed=blocks * slots * block_rows * rank * 2,
            transcendentals=0,
        ),
        name="couple_early",
    )(*lists, *sources, coupling_blocks, own, energy)


def middle_part(lists, sources, coupling_blocks, base):
    blocks, slots = lists[0].shape
    kinds, block_rows, _ = coupling_blocks.shape
    rows, rank = base.shape
    tile = pl.BlockSpec((block_rows, rank), lambda b, *_: (b, 0))
    return pl.pallas_call(
        middle_kernel,
        grid_spec=pltpu.PrefetchScalarGridSpec(
            num_scalar_prefetch=5,
            grid=(blocks,),
            in_specs=[
                *[pl.BlockSpec(memory_space=pl.ANY) for _ in sources],
                pl.BlockSpec((kinds, block_rows, block_rows), lambda b, *_: (0, 0, 0)),
                tile,
            ],
            out_specs=tile,
            scratch_shapes=[
                pltpu.VMEM((2, slots, block_rows, rank), jnp.bfloat16),
                pltpu.SemaphoreType.DMA((2, slots)),
            ],
        ),
        out_shape=jax.ShapeDtypeStruct((rows, rank), jnp.float32),
        compiler_params=pltpu.CompilerParams(vmem_limit_bytes=14 * 2**20),
        cost_estimate=pl.CostEstimate(
            flops=blocks * slots * block_rows * block_rows * rank,
            bytes_accessed=blocks * slots * block_rows * rank * 2,
            transcendentals=0,
        ),
        name="couple_middle",
    )(*lists, *sources, coupling_blocks, base)


def late_part(lists, sources, coupling_blocks, base, bathed):
    blocks, slots = lists[0].shape
    kinds, block_rows, _ = coupling_blocks.shape
    rows, rank = base.shape
    tile = pl.BlockSpec((block_rows, rank), lambda b, *_: (b, 0))
    return pl.pallas_call(
        late_kernel,
        grid_spec=pltpu.PrefetchScalarGridSpec(
            num_scalar_prefetch=5,
            grid=(blocks,),
            in_specs=[
                *[pl.BlockSpec(memory_space=pl.ANY) for _ in sources],
                pl.BlockSpec((kinds, block_rows, block_rows), lambda b, *_: (0, 0, 0)),
                tile,
                tile,
            ],
            out_specs=[tile, pl.BlockSpec((rank, 2 * rank), lambda b, *_: (0, 0))],
            scratch_shapes=[
                pltpu.VMEM((block_rows, rank), jnp.float32),
                pltpu.VMEM((2, slots, block_rows, rank), jnp.bfloat16),
                pltpu.SemaphoreType.DMA((2, slots)),
            ],
        ),
        out_shape=[
            jax.ShapeDtypeStruct((rows, rank), jnp.bfloat16),
            jax.ShapeDtypeStruct((rank, 2 * rank), jnp.float32),
        ],
        compiler_params=pltpu.CompilerParams(vmem_limit_bytes=14 * 2**20),
        name="couple_late",
    )(*lists, *sources, coupling_blocks, base, bathed)


def inverse_factor(square, start, lowest):
    n = square.shape[0]
    eye = (
        lax.broadcasted_iota(jnp.int32, (n, n), 0) == lax.broadcasted_iota(jnp.int32, (n, n), 1)
    ).astype(jnp.float32)
    work = jnp.concatenate([square, eye], axis=1)
    bands = [work[8 * i : 8 * i + 8, :] for i in range(n // 8)]
    sublane = lax.broadcasted_iota(jnp.int32, (8, 2 * n), 0)
    def spread(band, g):
        return [jnp.broadcast_to(band[:, 8 * g + r : 8 * g + r + 1], (8, 2 * n)) for r in range(8)]

    out = []
    for g in range(n // 8):
        band = bands[g]
        pivots = spread(band, g)
        diagonal = jnp.zeros((8, 2 * n), jnp.float32)
        scales = []
        for r in range(8):
            scales.append(pl.reciprocal(pivots[r][r : r + 1, :], approx=True))
            diagonal = jnp.where(sublane == r, pivots[r], diagonal)
            share = jnp.where(sublane > r, pivots[r] * scales[r], 0.0)
            for q in range(r + 1, 8):
                pivots[q] = pivots[q] - share * pivots[q][r : r + 1, :]
            band = band - share * band[r : r + 1, :]
        out.append(band[:, n:] * lax.rsqrt(diagonal)[:, n:])
        lowest[...] = jnp.minimum(lowest[...], diagonal / start[8 * g : 8 * g + 8, :])
        for i in range(g + 1, n // 8):
            columns = spread(bands[i], g)
            below = bands[i]
            for r in range(8):
                share = columns[r] * scales[r]
                for q in range(r + 1, 8):
                    columns[q] = columns[q] - share * pivots[q][r : r + 1, :]
                below = below - share * band[r : r + 1, :]
            bands[i] = below
    return jnp.concatenate(out, axis=0)


def eliminate(inner, image, start, lowest):
    rank = inner.shape[0]
    diagonal = lax.broadcasted_iota(jnp.int32, (rank, rank), 0) == lax.broadcasted_iota(jnp.int32, (rank, rank), 1)
    start[...] = jnp.broadcast_to(
        jnp.sum(jnp.where(diagonal, inner[...], 0.0), axis=1, keepdims=True), start.shape
    )
    lowest[...] = jnp.ones_like(lowest)

    def product(left, right, contract):
        return lax.dot_general(
            left, right, ((contract, (0,)), ((), ())),
            precision=HIGHEST, preferred_element_type=jnp.float32,
        )

    for low in range(0, rank, PANEL):
        high = low + PANEL
        here, first = low // 128 * 128, high // 128 * 128
        inverse = inverse_factor(inner[low:high, low:high], start[low:high, :], lowest)
        panel = product(inverse, inner[low:high, here:], (1,))
        inner[low:high, here:] = panel
        share = panel[:, high - here :]
        if high < rank:
            inner[high:, first:] -= product(share, panel[:, first - here :], (0,))
        side = product(inverse, image[low:high, :], (1,))
        image[low:high, :] = side
        if high < rank:
            image[high:, :] -= product(share, side, (0,))


def finish_kernel(
    order_ref, chunks_ref, moved_hbm, bathed_hbm, out_hbm,
    gram, inner, image, start, lowest, moved, bathed, out, in_sems, out_sems,
):
    rank = chunks_ref.shape[0]
    load_moved = pltpu.make_async_copy(moved_hbm, moved, in_sems.at[0])
    load_bathed = pltpu.make_async_copy(bathed_hbm, bathed, in_sems.at[1])
    load_moved.start()
    load_bathed.start()

    chunks = order_ref.shape[0]
    size = rank // chunks
    half = rank // 2
    for i in range(chunks):
        rows = pl.ds(pl.multiple_of(order_ref[i] * size, size), size)
        below = pl.ds(pl.multiple_of(rank + order_ref[i] * size, size), size)
        chunk = chunks_ref[i * size : (i + 1) * size, :]

        @pl.when(order_ref[i] < chunks // 2)
        def _():
            gram[rows, :] = chunk[:, : 2 * rank]
            gram[below, rank : rank + half] = chunk[:, 2 * rank :]

        @pl.when(order_ref[i] >= chunks // 2)
        def _():
            gram[rows, half:] = chunk[:, : rank + half]
            gram[below, rank:] = chunk[:, rank + half :]

    gram[half:rank, :half] = gram[:half, half:rank].T
    gram[rank : rank + half, rank + half :] = gram[rank + half :, rank : rank + half].T
    gram[rank:, :rank] = gram[:rank, rank:].T
    largest = jnp.max(jnp.max(jnp.abs(gram[...]), axis=0, keepdims=True), axis=1, keepdims=True)
    gram[...] = gram[...] * (1.0 / largest)
    product = jnp.dot(gram[:rank, :], gram[...], precision=HIGHEST, preferred_element_type=jnp.float32)

    def inner_product():
        rows = image[...]
        inner[...] = lax.dot_general(
            rows, rows, (((1,), (1,)), ((), ())),
            precision=HIGHEST, preferred_element_type=jnp.float32,
        )

    image[...] = product
    inner_product()
    eliminate(inner, image, start, lowest)
    safe = jnp.min(lowest[...]) >= SMALLEST_PIVOT

    @pl.when(jnp.logical_not(safe))
    def _():
        later = jnp.dot(gram[:rank, :], gram[...], precision=HIGHEST, preferred_element_type=jnp.float32)
        inner[...] = later[:, :rank]
        image[:, rank:] = later[:, rank:]
        eliminate(inner, image.at[:, rank:], start, lowest)
        upper = lax.broadcasted_iota(jnp.int32, (rank, rank), 0) <= lax.broadcasted_iota(jnp.int32, (rank, rank), 1)
        image[:, :rank] = jnp.where(upper, inner[...], 0.0)
        inner_product()
        eliminate(inner, image, start, lowest)

    rotation = image[...].T.astype(jnp.bfloat16)
    load_moved.wait()
    load_bathed.wait()
    pieces = out_sems.shape[0]
    size = moved.shape[0] // pieces

    def store(piece):
        rows = pl.ds(pl.multiple_of(piece * size, size), size)
        return pltpu.make_async_copy(out.at[rows, :], out_hbm.at[rows, :], out_sems.at[piece])

    def one(piece, carry):
        rows = pl.ds(pl.multiple_of(piece * size, size), size)
        stacked = jnp.concatenate([moved[rows, :], bathed[rows, :]], axis=1)
        value = jnp.dot(stacked, rotation, preferred_element_type=jnp.float32)
        out[rows, :] = value.astype(jnp.bfloat16)
        store(piece).start()
        return carry

    lax.fori_loop(0, pieces, one, 0)

    def drain(piece, carry):
        store(piece).wait()
        return carry

    lax.fori_loop(0, pieces, drain, 0)


def finish_part(order, chunks, moved, bathed):
    rows, rank = moved.shape
    return pl.pallas_call(
        finish_kernel,
        in_specs=[
            pl.BlockSpec(memory_space=pltpu.SMEM),
            pl.BlockSpec(memory_space=pltpu.VMEM),
            pl.BlockSpec(memory_space=pltpu.HBM),
            pl.BlockSpec(memory_space=pltpu.HBM),
        ],
        out_specs=pl.BlockSpec(memory_space=pl.ANY),
        out_shape=jax.ShapeDtypeStruct((rows, rank), jnp.bfloat16),
        scratch_shapes=[
            pltpu.VMEM((2 * rank, 2 * rank), jnp.float32),
            pltpu.VMEM((rank, rank), jnp.float32),
            pltpu.VMEM((rank, 2 * rank), jnp.float32),
            pltpu.VMEM((rank, 2 * PANEL), jnp.float32),
            pltpu.VMEM((8, 2 * PANEL), jnp.float32),
            pltpu.VMEM((rows, rank), jnp.bfloat16),
            pltpu.VMEM((rows, rank), jnp.bfloat16),
            pltpu.VMEM((rows, rank), jnp.bfloat16),
            pltpu.SemaphoreType.DMA((2,)),
            pltpu.SemaphoreType.DMA((8,)),
        ],
        compiler_params=pltpu.CompilerParams(vmem_limit_bytes=14 * 2**20),
        name="finish",
    )(order, chunks, moved, bathed)


def ring_order(count):
    wide = 2
    while 4 * wide * wide <= count:
        wide *= 2
    tall = count // wide
    walk = [0]
    for r in range(tall):
        across = range(1, wide)
        walk += [r * wide + c for c in (across if r % 2 == 0 else reversed(across))]
    return walk + [r * wide for r in range(tall - 1, 0, -1)]


PIECES = 4


def tie(one, other):
    return lax.optimization_barrier((one, other))


def early_steps():
    return lax.axis_size("col") // 2 - 1


def ring_gather(own, side, stages, small, early):
    order = ring_order(lax.axis_size("col"))
    following = order[1:] + order[:1]
    forward = list(zip(order, following))
    back = list(zip(following, order))
    size = own.shape[0] // PIECES
    pieces = [own[i * size : (i + 1) * size] for i in range(PIECES)]
    stages = list(stages)
    steps = []
    total = None
    for step in range(1, len(order)):
        if step > 1:
            pieces[-1], side = tie(pieces[-1], side)
        if step == 3:
            pieces[-1], small = tie(pieces[-1], small)
        if step == early_steps() + 3:
            total = early(small, [piece for done in steps[: early_steps()] for piece in done])
            pieces[-1], total = tie(pieces[-1], total)
        pieces = [
            lax.ppermute(piece, "col", forward if i < PIECES // 2 else back)
            for i, piece in enumerate(pieces)
        ]
        if step > 1 and stages:
            side = stages.pop(0)(side)
        steps.append(list(pieces))
    return steps, side, small, total


def slot_lists(ids, counts, kinds):
    blocks, slots = ids.shape
    count = lax.axis_size("col")
    order = ring_order(count)
    place = jnp.asarray([order.index(c) for c in range(count)], jnp.int32)
    col = jnp.arange(count, dtype=jnp.int32)
    mine = jnp.sum(jnp.where(col == lax.axis_index("col"), place, 0))
    owner, within = ids // blocks, ids % blocks
    theirs = jnp.sum(jnp.where(owner[..., None] == col, place, 0), axis=-1)
    in_piece = blocks // PIECES
    piece = within // in_piece
    step = jnp.where(piece >= PIECES // 2, theirs - mine, mine - theirs) % count
    before = early_steps()
    part = (step > before).astype(jnp.int32) + (step == count - 1).astype(jnp.int32)
    origin = jnp.where(
        part == 0,
        jnp.where(step == 0, 0, 1 + (step - 1) * PIECES + piece),
        jnp.where(part == 1, (step - before - 1) * PIECES + piece, piece),
    )
    offset = jnp.where(step == 0, within, within % in_piece)
    slot = jnp.arange(slots, dtype=jnp.int32)
    used = slot[None, :] < counts[:, None]
    key = jnp.where(used, part, 3) * slots + slot
    rank = jnp.sum((key[:, None, :] < key[:, :, None]).astype(jnp.int32), axis=-1)
    at = rank[:, :, None] == slot

    def arrange(values):
        return jnp.sum(jnp.where(at, values[:, :, None], 0), axis=1)

    origin, offset, kinds = arrange(origin), arrange(offset), arrange(kinds)
    parts = []
    first = jnp.zeros_like(counts)
    for i in range(3):
        number = jnp.sum((used & (part == i)).astype(jnp.int32), axis=1)
        parts.append((origin, offset, first, number, kinds))
        first = first + number
    return parts


def swap(value, axis, stride):
    count = lax.axis_size(axis)
    return lax.ppermute(value, axis, [(i, i ^ stride) for i in range(count)])


def strides(axis):
    return [1 << i for i in range(lax.axis_size(axis).bit_length() - 1)]


def halvings():
    return [("row", stride) for stride in strides("row")] + [("col", 1)]


def side_of(axis, stride):
    return (lax.axis_index(axis) >> (stride.bit_length() - 1)) & 1


def halve(value, swapped, lower):
    half = value.shape[0] // 2
    keep = jnp.where(lower, value[:half], value[half:])
    give = jnp.where(lower, value[half:], value[:half])
    return keep + swap(give, *swapped)


def sum_relative(value, lower):
    value = halve(value, ("col", 1), lower)
    for stride in strides("col")[1:]:
        value = value + swap(value, "col", stride)
    for axis, stride in reversed(halvings()):
        value = jnp.concatenate([value, swap(value, axis, stride)], axis=0)
    return value


def pack(upper, corner, lower):
    half = corner.shape[1] // 2
    return jnp.where(
        lower,
        jnp.concatenate([upper, corner[:, :half]], axis=1),
        jnp.concatenate([upper[:, half:], corner], axis=1),
    )


def chunk_order():
    swaps = halvings()
    relative = jnp.arange(1 << len(swaps), dtype=jnp.int32)
    mine = jnp.zeros_like(relative)
    for i, (axis, stride) in enumerate(swaps):
        mine = mine + (side_of(axis, stride) << (len(swaps) - 1 - i))
    return relative ^ mine


def shards(
    density_factor,
    onsite,
    neighbour_ids,
    neighbour_count,
    coupling_type,
    coupling_blocks,
    bath_pattern,
    bath_blocks,
):
    blocks, slots = neighbour_ids.shape
    group_blocks = lax.axis_size("col") * blocks
    in_group = neighbour_ids - lax.axis_index("row") * group_blocks
    lists = slot_lists(in_group, neighbour_count, coupling_type)
    bathed, corner = bath_part(density_factor, bath_pattern, bath_blocks)
    energy = onsite.reshape(blocks, -1)
    swaps = halvings()
    lower = [side_of(axis, stride) == 0 for axis, stride in swaps]

    def over_row(value, lower):
        for swapped, chosen in zip(swaps[:-1], lower):
            value = halve(value, swapped, chosen)
        return value

    def early(small, pieces):
        lists, energy, _, _ = small
        return early_part(lists[0], [density_factor] + pieces, coupling_blocks, density_factor, energy)

    steps, corner, small, total = ring_gather(
        density_factor,
        corner,
        [lambda value: over_row(value, lower)],
        (lists, energy, chunk_order(), lower),
        early,
    )
    lists, _, order, lower = small
    between = [piece for step in steps[early_steps() : -1] for piece in step]
    total = middle_part(lists[1], between, coupling_blocks, total)
    moved, upper = late_part(lists[2], steps[-1], coupling_blocks, total, bathed)
    gram = pack(over_row(upper, lower), corner, lower[0])
    return finish_part(order, sum_relative(gram, lower[-1]), moved, bathed)


def solution(mesh):
    placed = (
        P(("row", "col"), None),
        P(("row", "col")),
        P(("row", "col"), None),
        P(("row", "col")),
        P(("row", "col"), None),
        P(),
        P(("row", "col")),
        P(),
    )
    return jax.shard_map(
        shards, mesh=mesh, in_specs=placed, out_specs=P(("row", "col"), None), check_vma=False
    )
```

profile of v0, /device:TPU:0, one launch (start us, length us, event | category | flops | bytes accessed | tf_op | source)
XLA Modules:
  0.0 224.3 jit_solution(8174835561642670361)
XLA Ops:
  0.0 3.0 %fusion.13 = (bf16[1024,256]{1,0:T(8,128)(2,1)}, bf16[1024,256]{1,0:T(8,128)(2,1)}, bf16[1024,256]{1,0:T(8,128)(2,1)}, bf16[1024,256]{1,0:T(8,128)(2,1)}) fusion(bf16[4096,256]{1,0:T(8,128)(2,1)} %refs_14_.1), kind=kLoop, calls=%fused_computation.62 | loop fusion | bytes 4194304 | tf_op jit(solution)/shard_map/slice | solution.py:483
  3.0 3.0 %collective-permute-start = (bf16[1024,256]{1,0:T(8,128)(2,1)}, bf16[1024,256]{1,0:T(8,128)(2,1)S(1)}, u32[]{:S(2)}, u32[]{:S(2)}) collective-permute-start(bf16[1024,256]{1,0:T(8,128)(2,1)} %get-tuple-element.95), channel_id=1, source_target_pairs={{1,0},{3,1},{5,3},{7,5},{6,7},{4,6},{2,4},{0,2},{9,8},{11,9},{13,1... | collective-permute-start | bytes 1572872 | tf_op jit(solution)/shard_map/ppermute | solution.py:496
  11.6 5.5 %bath.1 = (bf16[4096,256]{1,0:T(8,128)(2,1)S(1)}, f32[256,256]{1,0:T(8,128)S(1)}) custom-call(s32[8]{0:T(128)S(1)} %copy-done.6, bf16[4,512,512]{2,1,0:T(8,128)(2,1)S(1)} %copy-done.5, bf16[4096,256]{1,0:T(8,128)(2,1)S(1)} %copy-done), custom_call_target="tpu_custom_call" | custom-call | tf_op jit(solution)/shard_map/bath/pallas_call | solution.py:35
  20.1 2.2 collective-permute-start.1
  22.3 8.0 %collective-permute-done.18.refs_3_ = bf16[1024,256]{1,0:T(8,128)(2,1)} collective-permute-done((bf16[1024,256]{1,0:T(8,128)(2,1)}, bf16[1024,256]{1,0:T(8,128)(2,1)}, u32[]{:S(2)}, u32[]{:S(2)}) %collective-permute-start.18) | collective-permute-done | bytes 524320 | tf_op jit(solution)/shard_map/ppermute | solution.py:496
  35.4 2.3 %collective-permute-done.3 = f32[64,256]{1,0:T(8,128)S(1)} collective-permute-done((f32[64,256]{1,0:T(8,128)S(1)}, f32[64,256]{1,0:T(8,128)S(1)}, u32[]{:S(2)}, u32[]{:S(2)}) %collective-permute-start.3) | collective-permute-done | bytes 65568 | tf_op jit(solution)/shard_map/ppermute | solution.py:546
  37.8 3.7 %collective-permute-done.1.refs_8_ = bf16[1024,256]{1,0:T(8,128)(2,1)S(1)} collective-permute-done((bf16[1024,256]{1,0:T(8,128)(2,1)S(1)}, bf16[1024,256]{1,0:T(8,128)(2,1)S(1)}, u32[]{:S(2)}, u32[]{:S(2)}) %collective-permute-start.1) | collective-permute-done | bytes 524320 | tf_op jit(solution)/shard_map/ppermute | solution.py:496
  41.5 2.1 collective-permute-start.25
  43.6 9.8 %collective-permute-done.5.refs_5_ = bf16[1024,256]{1,0:T(8,128)(2,1)S(1)} collective-permute-done((bf16[1024,256]{1,0:T(8,128)(2,1)}, bf16[1024,256]{1,0:T(8,128)(2,1)S(1)}, u32[]{:S(2)}, u32[]{:S(2)}) %collective-permute-start.5) | collective-permute-done | bytes 524320 | tf_op jit(solution)/shard_map/ppermute | solution.py:496
  55.7 8.2 %collective-permute-done.25.refs_12_ = bf16[1024,256]{1,0:T(8,128)(2,1)S(1)} collective-permute-done((bf16[1024,256]{1,0:T(8,128)(2,1)S(1)}, bf16[1024,256]{1,0:T(8,128)(2,1)S(1)}, u32[]{:S(2)}, u32[]{:S(2)}) %collective-permute-start.25) | collective-permute-done | bytes 524320 | tf_op jit(solution)/shard_map/ppermute | solution.py:496
  66.0 2.2 collective-permute-done.6.refs_9_
  68.5 11.0 %collective-permute-done.13.refs_10_ = bf16[1024,256]{1,0:T(8,128)(2,1)S(1)} collective-permute-done((bf16[1024,256]{1,0:T(8,128)(2,1)S(1)}, bf16[1024,256]{1,0:T(8,128)(2,1)S(1)}, u32[]{:S(2)}, u32[]{:S(2)}) %collective-permute-start.13) | collective-permute-done | bytes 524320 | tf_op jit(solution)/shard_map/ppermute | solution.py:496
  81.5 4.9 %collective-permute-done.26.refs_3_ = bf16[1024,256]{1,0:T(8,128)(2,1)S(1)} collective-permute-done((bf16[1024,256]{1,0:T(8,128)(2,1)S(1)}, bf16[1024,256]{1,0:T(8,128)(2,1)S(1)}, u32[]{:S(2)}, u32[]{:S(2)}) %collective-permute-start.26) | collective-permute-done | bytes 524320 | tf_op jit(solution)/shard_map/ppermute | solution.py:496
  88.5 2.2 collective-permute-done.7.refs_0_
  91.0 11.0 %collective-permute-done.14.refs_1_ = bf16[1024,256]{1,0:T(8,128)(2,1)S(1)} collective-permute-done((bf16[1024,256]{1,0:T(8,128)(2,1)S(1)}, bf16[1024,256]{1,0:T(8,128)(2,1)S(1)}, u32[]{:S(2)}, u32[]{:S(2)}) %collective-permute-start.14) | collective-permute-done | bytes 524320 | tf_op jit(solution)/shard_map/ppermute | solution.py:496
  105.6 10.6 %couple_early.1.refs_13_ = f32[4096,256]{1,0:T(8,128)S(1)} custom-call(s32[8,8]{1,0:T(8,128)S(1)} %get-tuple-element.73.origin_ref, s32[8,8]{1,0:T(8,128)S(1)} %get-tuple-element.74.offset_ref, s32[8]{0:T(128)S(1)} %broadcast_in_dim.52.first_ref, s32[8]{0:T(128)S(1)} %get-tuple-element.75.count_ref.first_ref, s32[8,8]{1,0:T(8,128)S(1)} %get-tuple-element.77.kind_ref, ...), custom_call_target="tpu_custom_call" | custom-call | flops 4294967296 | bytes 16777216 | tf_op jit(solution)/shard_map/couple_early/pallas_call | solution.py:179
  118.3 6.1 %collective-permute-done.15.refs_5_ = bf16[1024,256]{1,0:T(8,128)(2,1)S(1)} collective-permute-done((bf16[1024,256]{1,0:T(8,128)(2,1)S(1)}, bf16[1024,256]{1,0:T(8,128)(2,1)S(1)}, u32[]{:S(2)}, u32[]{:S(2)}) %collective-permute-start.15) | collective-permute-done | bytes 524320 | tf_op jit(solution)/shard_map/ppermute | solution.py:496
  126.5 4.9 %collective-permute-done.28.refs_11_ = bf16[1024,256]{1,0:T(8,128)(2,1)S(1)} collective-permute-done((bf16[1024,256]{1,0:T(8,128)(2,1)S(1)}, bf16[1024,256]{1,0:T(8,128)(2,1)S(1)}, u32[]{:S(2)}, u32[]{:S(2)}) %collective-permute-start.28) | collective-permute-done | bytes 524320 | tf_op jit(solution)/shard_map/ppermute | solution.py:496
  133.5 2.2 collective-permute-done.9.refs_8_
  135.9 11.0 %collective-permute-done.16.refs_9_ = bf16[1024,256]{1,0:T(8,128)(2,1)S(1)} collective-permute-done((bf16[1024,256]{1,0:T(8,128)(2,1)S(1)}, bf16[1024,256]{1,0:T(8,128)(2,1)S(1)}, u32[]{:S(2)}, u32[]{:S(2)}) %collective-permute-start.16) | collective-permute-done | bytes 524320 | tf_op jit(solution)/shard_map/ppermute | solution.py:496
  148.9 8.0 %couple_middle.1.refs_5_ = f32[4096,256]{1,0:T(8,128)S(1)} custom-call(s32[8,8]{1,0:T(8,128)S(1)} %get-tuple-element.73.origin_ref, s32[8,8]{1,0:T(8,128)S(1)} %get-tuple-element.74.offset_ref, s32[8]{0:T(128)S(1)} %get-tuple-element.75.count_ref.first_ref, s32[8]{0:T(128)S(1)} %get-tuple-element.76.count_ref, s32[8,8]{1,0:T(8,128)S(1)} %get-tuple-element.77.kind_ref, ...), custom_call_target="tpu_custom_call" | custom-call | flops 4294967296 | bytes 16777216 | tf_op jit(solution)/shard_map/couple_middle/pallas_call | solution.py:214
  158.1 8.8 %collective-permute-done.17.refs_1_ = bf16[1024,256]{1,0:T(8,128)(2,1)S(1)} collective-permute-done((bf16[1024,256]{1,0:T(8,128)(2,1)S(1)}, bf16[1024,256]{1,0:T(8,128)(2,1)S(1)}, u32[]{:S(2)}, u32[]{:S(2)}) %collective-permute-start.17) | collective-permute-done | bytes 524320 | tf_op jit(solution)/shard_map/ppermute | solution.py:496
  167.0 4.9 %couple_late.1 = (bf16[4096,256]{1,0:T(8,128)(2,1)S(1)}, f32[256,512]{1,0:T(8,128)S(1)}) custom-call(s32[8,8]{1,0:T(8,128)S(1)} %get-tuple-element.73.origin_ref, s32[8,8]{1,0:T(8,128)S(1)} %get-tuple-element.74.offset_ref, s32[8]{0:T(128)S(1)} %add.86.first_ref, s32[8]{0:T(128)S(1)} %get-tuple-element.55.count_ref, s32[8,8]{1,0:T(8,128)S(1)} %get-tuple-element.77.kind_ref, ...), custom_call_target="tpu_custom_call" | custom-call | tf_op jit(solution)/shard_map/couple_late/pallas_call | solution.py:246
  173.6 3.5 %collective-permute-start.31 = (f32[64,512]{1,0:T(8,128)S(1)}, f32[64,512]{1,0:T(8,128)S(1)}, u32[]{:S(2)}, u32[]{:S(2)}) collective-permute-start(f32[64,512]{1,0:T(8,128)S(1)} %slice_select_fusion.1), channel_id=1, source_target_pairs={{0,16},{8,24},{16,0},{24,8},{1,17},{9,25},{17,1},{25,9},{2,18},{10... | collective-permute-start | bytes 393224 | tf_op jit(solution)/shard_map/ppermute | solution.py:546
  177.1 3.8 %collective-permute-done.31 = f32[64,512]{1,0:T(8,128)S(1)} collective-permute-done((f32[64,512]{1,0:T(8,128)S(1)}, f32[64,512]{1,0:T(8,128)S(1)}, u32[]{:S(2)}, u32[]{:S(2)}) %collective-permute-start.31) | collective-permute-done | bytes 131104 | tf_op jit(solution)/shard_map/ppermute | solution.py:546
  181.1 4.4 %collective-permute-done.32 = f32[32,640]{1,0:T(8,128)S(1)} collective-permute-done((f32[32,640]{1,0:T(8,128)S(1)}, f32[32,640]{1,0:T(8,128)S(1)}, u32[]{:S(2)}, u32[]{:S(2)}) %collective-permute-start.32) | collective-permute-done | bytes 81952 | tf_op jit(solution)/shard_map/ppermute | solution.py:546
  186.3 3.7 %collective-permute-done.33 = f32[32,640]{1,0:T(8,128)S(1)} collective-permute-done((f32[32,640]{1,0:T(8,128)S(1)}, f32[32,640]{1,0:T(8,128)S(1)}, u32[]{:S(2)}, u32[]{:S(2)}) %collective-permute-start.33) | collective-permute-done | bytes 81952 | tf_op jit(solution)/shard_map/ppermute | solution.py:546
  190.1 3.0 %collective-permute-start.34 = (f32[32,640]{1,0:T(8,128)S(1)}, f32[32,640]{1,0:T(8,128)S(1)}, u32[]{:S(2)}, u32[]{:S(2)}) collective-permute-start(f32[32,640]{1,0:T(8,128)S(1)} %add.93), channel_id=1, source_target_pairs={{0,4},{1,5},{2,6},{3,7},{4,0},{5,1},{6,2},{7,3},{8,12},{9,13},{10,... | collective-permute-start | bytes 245768 | tf_op jit(solution)/shard_map/ppermute | solution.py:546
  193.1 3.3 %collective-permute-done.34 = f32[32,640]{1,0:T(8,128)S(1)} collective-permute-done((f32[32,640]{1,0:T(8,128)S(1)}, f32[32,640]{1,0:T(8,128)S(1)}, u32[]{:S(2)}, u32[]{:S(2)}) %collective-permute-start.34) | collective-permute-done | bytes 81952 | tf_op jit(solution)/shard_map/ppermute | solution.py:546
  196.4 4.4 %collective-permute-done.35 = f32[32,640]{1,0:T(8,128)S(1)} collective-permute-done((f32[32,640]{1,0:T(8,128)S(1)}, f32[32,640]{1,0:T(8,128)S(1)}, u32[]{:S(2)}, u32[]{:S(2)}) %collective-permute-start.35) | collective-permute-done | bytes 81952 | tf_op jit(solution)/shard_map/ppermute | solution.py:546
  202.7 3.6 %collective-permute-done.36 = f32[64,640]{1,0:T(8,128)S(1)} collective-permute-done((f32[64,640]{1,0:T(8,128)S(1)}, f32[64,640]{1,0:T(8,128)S(1)}, u32[]{:S(2)}, u32[]{:S(2)}) %collective-permute-start.36) | collective-permute-done | bytes 163872 | tf_op jit(solution)/shard_map/ppermute | solution.py:546
  208.0 16.1 %finish.1 = bf16[4096,256]{1,0:T(8,128)(2,1)} custom-call(s32[8]{0:T(128)S(1)} %iota_xor_fusion.order_ref, f32[256,640]{1,0:T(8,128)S(1)} %pad_maximum_fusion.chunks_ref, bf16[4096,256]{1,0:T(8,128)(2,1)S(1)} %get-tuple-element.82.moved_hbm, bf16[4096,256]{1,0:T(8,128)(2,1)S(1)} %copy-done.4), custom_call_target="tpu_custom_call" | custom-call | tf_op jit(solution)/shard_map/finish/pallas_call | solution.py:427
  (103 shorter events, 42.4 us)
Async XLA Ops:
  3.0 15.9 %collective-permute-start = (bf16[1024,256]{1,0:T(8,128)(2,1)}, bf16[1024,256]{1,0:T(8,128)(2,1)S(1)}, u32[]{:S(2)}, u32[]{:S(2)}) collective-permute-start(bf16[1024,256]{1,0:T(8,128)(2,1)} %get-tuple-element.95), channel_id=1, source_target_pairs={{1,0},{3,1},{5,3},{7,5},{6,7},{4,6},{2,4},{0,2},{9,8},{11,9},{13,1... | collective-permute-start | bytes 1572872 | tf_op jit(solution)/shard_map/ppermute | solution.py:496
  6.1 16.2 %collective-permute-start.11 = (bf16[1024,256]{1,0:T(8,128)(2,1)}, bf16[1024,256]{1,0:T(8,128)(2,1)S(1)}, u32[]{:S(2)}, u32[]{:S(2)}) collective-permute-start(bf16[1024,256]{1,0:T(8,128)(2,1)} %get-tuple-element.93), channel_id=1, source_target_pairs={{0,1},{1,3},{3,5},{5,7},{7,6},{6,4},{4,2},{2,0},{8,9},{9,11},{11,1... | collective-permute-start | bytes 1572872 | tf_op jit(solution)/shard_map/ppermute | solution.py:496
  6.1 24.2 %collective-permute-start.18 = (bf16[1024,256]{1,0:T(8,128)(2,1)}, bf16[1024,256]{1,0:T(8,128)(2,1)}, u32[]{:S(2)}, u32[]{:S(2)}) collective-permute-start(bf16[1024,256]{1,0:T(8,128)(2,1)} %get-tuple-element.92), channel_id=1, source_target_pairs={{1,0},{3,1},{5,3},{7,5},{6,7},{4,6},{2,4},{0,2},{9,8},{11,9},{13,1... | collective-permute-start | bytes 1572872 | tf_op jit(solution)/shard_map/ppermute | solution.py:496
  8.1 24.4 %collective-permute-start.4 = (bf16[1024,256]{1,0:T(8,128)(2,1)}, bf16[1024,256]{1,0:T(8,128)(2,1)}, u32[]{:S(2)}, u32[]{:S(2)}) collective-permute-start(bf16[1024,256]{1,0:T(8,128)(2,1)} %get-tuple-element.94), channel_id=1, source_target_pairs={{0,1},{1,3},{3,5},{5,7},{7,6},{6,4},{4,2},{2,0},{8,9},{9,11},{11,1... | collective-permute-start | bytes 1572872 | tf_op jit(solution)/shard_map/ppermute | solution.py:496
  19.7 12.8 %collective-permute-start.2 = (f32[128,256]{1,0:T(8,128)}, f32[128,256]{1,0:T(8,128)}, u32[]{:S(2)}, u32[]{:S(2)}) collective-permute-start(f32[128,256]{1,0:T(8,128)} %slice_select_fusion.2), channel_id=1, source_target_pairs={{0,8},{8,0},{16,24},{24,16},{1,9},{9,1},{17,25},{25,17},{2,10},{10... | collective-permute-start | bytes 393224 | tf_op jit(solution)/shard_map/ppermute | solution.py:546
  20.1 21.3 %collective-permute-start.1 = (bf16[1024,256]{1,0:T(8,128)(2,1)S(1)}, bf16[1024,256]{1,0:T(8,128)(2,1)S(1)}, u32[]{:S(2)}, u32[]{:S(2)}) collective-permute-start(bf16[1024,256]{1,0:T(8,128)(2,1)S(1)} %collective-permute-done.refs_4_), channel_id=1, source_target_pairs={{1,0},{3,1},{5,3},{7,5},{6,7},{4,6},{2,4},{0,2},{9,8},{11,9},{13,1... | collective-permute-start | bytes 1572872 | tf_op jit(solution)/shard_map/ppermute | solution.py:496
  22.3 31.4 %collective-permute-start.12 = (bf16[1024,256]{1,0:T(8,128)(2,1)S(1)}, bf16[1024,256]{1,0:T(8,128)(2,1)S(1)}, u32[]{:S(2)}, u32[]{:S(2)}) collective-permute-start(bf16[1024,256]{1,0:T(8,128)(2,1)S(1)} %collective-permute-done.11.refs_2_), channel_id=1, source_target_pairs={{0,1},{1,3},{3,5},{5,7},{7,6},{6,4},{4,2},{2,0},{8,9},{9,11},{11,1... | collective-permute-start | bytes 1572872 | tf_op jit(solution)/shard_map/ppermute | solution.py:496
  30.3 25.0 %collective-permute-start.19 = (bf16[1024,256]{1,0:T(8,128)(2,1)}, bf16[1024,256]{1,0:T(8,128)(2,1)S(1)}, u32[]{:S(2)}, u32[]{:S(2)}) collective-permute-start(bf16[1024,256]{1,0:T(8,128)(2,1)} %collective-permute-done.18.refs_3_), channel_id=1, source_target_pairs={{1,0},{3,1},{5,3},{7,5},{6,7},{4,6},{2,4},{0,2},{9,8},{11,9},{13,1... | collective-permute-start | bytes 1572872 | tf_op jit(solution)/shard_map/ppermute | solution.py:496
  32.5 20.9 %collective-permute-start.5 = (bf16[1024,256]{1,0:T(8,128)(2,1)}, bf16[1024,256]{1,0:T(8,128)(2,1)S(1)}, u32[]{:S(2)}, u32[]{:S(2)}) collective-permute-start(bf16[1024,256]{1,0:T(8,128)(2,1)} %collective-permute-done.4.refs_1_), channel_id=1, source_target_pairs={{0,1},{1,3},{3,5},{5,7},{7,6},{6,4},{4,2},{2,0},{8,9},{9,11},{11,1... | collective-permute-start | bytes 1572872 | tf_op jit(solution)/shard_map/ppermute | solution.py:496
  41.5 22.5 %collective-permute-start.25 = (bf16[1024,256]{1,0:T(8,128)(2,1)S(1)}, bf16[1024,256]{1,0:T(8,128)(2,1)S(1)}, u32[]{:S(2)}, u32[]{:S(2)}) collective-permute-start(bf16[1024,256]{1,0:T(8,128)(2,1)S(1)} %collective-permute-done.1.refs_8_), channel_id=1, source_target_pairs={{1,0},{3,1},{5,3},{7,5},{6,7},{4,6},{2,4},{0,2},{9,8},{11,9},{13,1... | collective-permute-start | bytes 1572872 | tf_op jit(solution)/shard_map/ppermute | solution.py:496
  53.4 14.9 %collective-permute-start.6 = (bf16[1024,256]{1,0:T(8,128)(2,1)S(1)}, bf16[1024,256]{1,0:T(8,128)(2,1)S(1)}, u32[]{:S(2)}, u32[]{:S(2)}) collective-permute-start(bf16[1024,256]{1,0:T(8,128)(2,1)S(1)} %collective-permute-done.5.refs_5_), channel_id=1, source_target_pairs={{0,1},{1,3},{3,5},{5,7},{7,6},{6,4},{4,2},{2,0},{8,9},{9,11},{11,1... | collective-permute-start | bytes 1572872 | tf_op jit(solution)/shard_map/ppermute | solution.py:496
  53.7 25.8 %collective-permute-start.13 = (bf16[1024,256]{1,0:T(8,128)(2,1)S(1)}, bf16[1024,256]{1,0:T(8,128)(2,1)S(1)}, u32[]{:S(2)}, u32[]{:S(2)}) collective-permute-start(bf16[1024,256]{1,0:T(8,128)(2,1)S(1)} %collective-permute-done.12.refs_6_), channel_id=1, source_target_pairs={{0,1},{1,3},{3,5},{5,7},{7,6},{6,4},{4,2},{2,0},{8,9},{9,11},{11,1... | collective-permute-start | bytes 1572872 | tf_op jit(solution)/shard_map/ppermute | solution.py:496
  55.4 24.4 %collective-permute-start.20 = (bf16[1024,256]{1,0:T(8,128)(2,1)S(1)}, bf16[1024,256]{1,0:T(8,128)(2,1)S(1)}, u32[]{:S(2)}, u32[]{:S(2)}) collective-permute-start(bf16[1024,256]{1,0:T(8,128)(2,1)S(1)} %collective-permute-done.19.refs_7_), channel_id=1, source_target_pairs={{1,0},{3,1},{5,3},{7,5},{6,7},{4,6},{2,4},{0,2},{9,8},{11,9},{13,1... | collective-permute-start | bytes 1572872 | tf_op jit(solution)/shard_map/ppermute | solution.py:496
  63.9 22.5 %collective-permute-start.26 = (bf16[1024,256]{1,0:T(8,128)(2,1)S(1)}, bf16[1024,256]{1,0:T(8,128)(2,1)S(1)}, u32[]{:S(2)}, u32[]{:S(2)}) collective-permute-start(bf16[1024,256]{1,0:T(8,128)(2,1)S(1)} %collective-permute-done.25.refs_12_), channel_id=1, source_target_pairs={{1,0},{3,1},{5,3},{7,5},{6,7},{4,6},{2,4},{0,2},{9,8},{11,9},{13,1... | collective-permute-start | bytes 1572872 | tf_op jit(solution)/shard_map/ppermute | solution.py:496
  68.2 22.5 %collective-permute-start.7 = (bf16[1024,256]{1,0:T(8,128)(2,1)S(1)}, bf16[1024,256]{1,0:T(8,128)(2,1)S(1)}, u32[]{:S(2)}, u32[]{:S(2)}) collective-permute-start(bf16[1024,256]{1,0:T(8,128)(2,1)S(1)} %collective-permute-done.6.refs_9_), channel_id=1, source_target_pairs={{0,1},{1,3},{3,5},{5,7},{7,6},{6,4},{4,2},{2,0},{8,9},{9,11},{11,1... | collective-permute-start | bytes 1572872 | tf_op jit(solution)/shard_map/ppermute | solution.py:496
  79.5 22.5 %collective-permute-start.14 = (bf16[1024,256]{1,0:T(8,128)(2,1)S(1)}, bf16[1024,256]{1,0:T(8,128)(2,1)S(1)}, u32[]{:S(2)}, u32[]{:S(2)}) collective-permute-start(bf16[1024,256]{1,0:T(8,128)(2,1)S(1)} %collective-permute-done.13.refs_10_), channel_id=1, source_target_pairs={{0,1},{1,3},{3,5},{5,7},{7,6},{6,4},{4,2},{2,0},{8,9},{9,11},{11,1... | collective-permute-start | bytes 1572872 | tf_op jit(solution)/shard_map/ppermute | solution.py:496
  79.8 22.5 %collective-permute-start.21 = (bf16[1024,256]{1,0:T(8,128)(2,1)S(1)}, bf16[1024,256]{1,0:T(8,128)(2,1)S(1)}, u32[]{:S(2)}, u32[]{:S(2)}) collective-permute-start(bf16[1024,256]{1,0:T(8,128)(2,1)S(1)} %collective-permute-done.20.refs_11_), channel_id=1, source_target_pairs={{1,0},{3,1},{5,3},{7,5},{6,7},{4,6},{2,4},{0,2},{9,8},{11,9},{13,1... | collective-permute-start | bytes 1572872 | tf_op jit(solution)/shard_map/ppermute | solution.py:496
  86.4 29.8 %collective-permute-start.27 = (bf16[1024,256]{1,0:T(8,128)(2,1)S(1)}, bf16[1024,256]{1,0:T(8,128)(2,1)S(1)}, u32[]{:S(2)}, u32[]{:S(2)}) collective-permute-start(bf16[1024,256]{1,0:T(8,128)(2,1)S(1)} %collective-permute-done.26.refs_3_), channel_id=1, source_target_pairs={{1,0},{3,1},{5,3},{7,5},{6,7},{4,6},{2,4},{0,2},{9,8},{11,9},{13,1... | collective-permute-start | bytes 1572872 | tf_op jit(solution)/shard_map/ppermute | solution.py:496
  90.7 27.1 %collective-permute-start.8 = (bf16[1024,256]{1,0:T(8,128)(2,1)S(1)}, bf16[1024,256]{1,0:T(8,128)(2,1)S(1)}, u32[]{:S(2)}, u32[]{:S(2)}) collective-permute-start(bf16[1024,256]{1,0:T(8,128)(2,1)S(1)} %collective-permute-done.7.refs_0_), channel_id=1, source_target_pairs={{0,1},{1,3},{3,5},{5,7},{7,6},{6,4},{4,2},{2,0},{8,9},{9,11},{11,1... | collective-permute-start | bytes 1572872 | tf_op jit(solution)/shard_map/ppermute | solution.py:496
  102.0 22.5 %collective-permute-start.15 = (bf16[1024,256]{1,0:T(8,128)(2,1)S(1)}, bf16[1024,256]{1,0:T(8,128)(2,1)S(1)}, u32[]{:S(2)}, u32[]{:S(2)}) collective-permute-start(bf16[1024,256]{1,0:T(8,128)(2,1)S(1)} %collective-permute-done.14.refs_1_), channel_id=1, source_target_pairs={{0,1},{1,3},{3,5},{5,7},{7,6},{6,4},{4,2},{2,0},{8,9},{9,11},{11,1... | collective-permute-start | bytes 1572872 | tf_op jit(solution)/shard_map/ppermute | solution.py:496
  102.2 22.5 %collective-permute-start.22 = (bf16[1024,256]{1,0:T(8,128)(2,1)S(1)}, bf16[1024,256]{1,0:T(8,128)(2,1)S(1)}, u32[]{:S(2)}, u32[]{:S(2)}) collective-permute-start(bf16[1024,256]{1,0:T(8,128)(2,1)S(1)} %collective-permute-done.21.refs_2_), channel_id=1, source_target_pairs={{1,0},{3,1},{5,3},{7,5},{6,7},{4,6},{2,4},{0,2},{9,8},{11,9},{13,1... | collective-permute-start | bytes 1572872 | tf_op jit(solution)/shard_map/ppermute | solution.py:496
  116.2 15.1 %collective-permute-start.28 = (bf16[1024,256]{1,0:T(8,128)(2,1)S(1)}, bf16[1024,256]{1,0:T(8,128)(2,1)S(1)}, u32[]{:S(2)}, u32[]{:S(2)}) collective-permute-start(bf16[1024,256]{1,0:T(8,128)(2,1)S(1)} %collective-permute-done.27.refs_7_), channel_id=1, source_target_pairs={{1,0},{3,1},{5,3},{7,5},{6,7},{4,6},{2,4},{0,2},{9,8},{11,9},{13,1... | collective-permute-start | bytes 1572872 | tf_op jit(solution)/shard_map/ppermute | solution.py:496
  117.8 17.9 %collective-permute-start.9 = (bf16[1024,256]{1,0:T(8,128)(2,1)S(1)}, bf16[1024,256]{1,0:T(8,128)(2,1)S(1)}, u32[]{:S(2)}, u32[]{:S(2)}) collective-permute-start(bf16[1024,256]{1,0:T(8,128)(2,1)S(1)} %collective-permute-done.8.refs_4_), channel_id=1, source_target_pairs={{0,1},{1,3},{3,5},{5,7},{7,6},{6,4},{4,2},{2,0},{8,9},{9,11},{11,1... | collective-permute-start | bytes 1572872 | tf_op jit(solution)/shard_map/ppermute | solution.py:496
  124.4 22.5 %collective-permute-start.16 = (bf16[1024,256]{1,0:T(8,128)(2,1)S(1)}, bf16[1024,256]{1,0:T(8,128)(2,1)S(1)}, u32[]{:S(2)}, u32[]{:S(2)}) collective-permute-start(bf16[1024,256]{1,0:T(8,128)(2,1)S(1)} %collective-permute-done.15.refs_5_), channel_id=1, source_target_pairs={{0,1},{1,3},{3,5},{5,7},{7,6},{6,4},{4,2},{2,0},{8,9},{9,11},{11,1... | collective-permute-start | bytes 1572872 | tf_op jit(solution)/shard_map/ppermute | solution.py:496
  124.7 22.5 %collective-permute-start.23 = (bf16[1024,256]{1,0:T(8,128)(2,1)S(1)}, bf16[1024,256]{1,0:T(8,128)(2,1)S(1)}, u32[]{:S(2)}, u32[]{:S(2)}) collective-permute-start(bf16[1024,256]{1,0:T(8,128)(2,1)S(1)} %collective-permute-done.22.refs_6_), channel_id=1, source_target_pairs={{1,0},{3,1},{5,3},{7,5},{6,7},{4,6},{2,4},{0,2},{9,8},{11,9},{13,1... | collective-permute-start | bytes 1572872 | tf_op jit(solution)/shard_map/ppermute | solution.py:496
  131.3 25.6 %collective-permute-start.29 = (bf16[1024,256]{1,0:T(8,128)(2,1)S(1)}, bf16[1024,256]{1,0:T(8,128)(2,1)S(1)}, u32[]{:S(2)}, u32[]{:S(2)}) collective-permute-start(bf16[1024,256]{1,0:T(8,128)(2,1)S(1)} %collective-permute-done.28.refs_11_), channel_id=1, source_target_pairs={{1,0},{3,1},{5,3},{7,5},{6,7},{4,6},{2,4},{0,2},{9,8},{11,9},{13,1... | collective-permute-start | bytes 1572872 | tf_op jit(solution)/shard_map/ppermute | solution.py:496
  135.7 22.5 %collective-permute-start.10 = (bf16[1024,256]{1,0:T(8,128)(2,1)S(1)}, bf16[1024,256]{1,0:T(8,128)(2,1)S(1)}, u32[]{:S(2)}, u32[]{:S(2)}) collective-permute-start(bf16[1024,256]{1,0:T(8,128)(2,1)S(1)} %collective-permute-done.9.refs_8_), channel_id=1, source_target_pairs={{0,1},{1,3},{3,5},{5,7},{7,6},{6,4},{4,2},{2,0},{8,9},{9,11},{11,1... | collective-permute-start | bytes 1572872 | tf_op jit(solution)/shard_map/ppermute | solution.py:496
  146.9 20.1 %collective-permute-start.17 = (bf16[1024,256]{1,0:T(8,128)(2,1)S(1)}, bf16[1024,256]{1,0:T(8,128)(2,1)S(1)}, u32[]{:S(2)}, u32[]{:S(2)}) collective-permute-start(bf16[1024,256]{1,0:T(8,128)(2,1)S(1)} %collective-permute-done.16.refs_9_), channel_id=1, source_target_pairs={{0,1},{1,3},{3,5},{5,7},{7,6},{6,4},{4,2},{2,0},{8,9},{9,11},{11,1... | collective-permute-start | bytes 1572872 | tf_op jit(solution)/shard_map/ppermute | solution.py:496
  147.2 19.8 %collective-permute-start.24 = (bf16[1024,256]{1,0:T(8,128)(2,1)S(1)}, bf16[1024,256]{1,0:T(8,128)(2,1)S(1)}, u32[]{:S(2)}, u32[]{:S(2)}) collective-permute-start(bf16[1024,256]{1,0:T(8,128)(2,1)S(1)} %collective-permute-done.23.refs_10_), channel_id=1, source_target_pairs={{1,0},{3,1},{5,3},{7,5},{6,7},{4,6},{2,4},{0,2},{9,8},{11,9},{13,1... | collective-permute-start | bytes 1572872 | tf_op jit(solution)/shard_map/ppermute | solution.py:496
  173.6 7.3 %collective-permute-start.31 = (f32[64,512]{1,0:T(8,128)S(1)}, f32[64,512]{1,0:T(8,128)S(1)}, u32[]{:S(2)}, u32[]{:S(2)}) collective-permute-start(f32[64,512]{1,0:T(8,128)S(1)} %slice_select_fusion.1), channel_id=1, source_target_pairs={{0,16},{8,24},{16,0},{24,8},{1,17},{9,25},{17,1},{25,9},{2,18},{10... | collective-permute-start | bytes 393224 | tf_op jit(solution)/shard_map/ppermute | solution.py:546
  190.1 6.3 %collective-permute-start.34 = (f32[32,640]{1,0:T(8,128)S(1)}, f32[32,640]{1,0:T(8,128)S(1)}, u32[]{:S(2)}, u32[]{:S(2)}) collective-permute-start(f32[32,640]{1,0:T(8,128)S(1)} %add.93), channel_id=1, source_target_pairs={{0,4},{1,5},{2,6},{3,7},{4,0},{5,1},{6,2},{7,3},{8,12},{9,13},{10,... | collective-permute-start | bytes 245768 | tf_op jit(solution)/shard_map/ppermute | solution.py:546
  200.9 5.4 %collective-permute-start.36 = (f32[64,640]{1,0:T(8,128)S(1)}, f32[64,640]{1,0:T(8,128)S(1)}, u32[]{:S(2)}, u32[]{:S(2)}) collective-permute-start(f32[64,640]{1,0:T(8,128)S(1)} %pad_maximum_fusion.2), channel_id=1, source_target_pairs={{0,16},{8,24},{16,0},{24,8},{1,17},{9,25},{17,1},{25,9},{2,18},{10... | collective-permute-start | bytes 491528 | tf_op jit(solution)/shard_map/ppermute | solution.py:546
  (18 other events, 181.8 us)
where the time goes:
time: 225 us; the launch traced here: 224 us
  waiting for transfers between devices  124 us (55%)
  Pallas kernels  45 us (20%)
  starting transfers between devices  42.6 us (19%)
  local copies, waits for them, and re-layouts  7.58 us (3%)
  other arithmetic  4.16 us (2%)
    ppermute x28, waiting for transfers between devices, ring_gather(): lax.ppermute(piece, 'col', forward if i < PIECES // 2 else back)  95.7 us
    ppermute x28, starting transfers between devices, ring_gather(): lax.ppermute(piece, 'col', forward if i < PIECES // 2 else back)  31.2 us
    ppermute x10, waiting for transfers between devices, swap(): return lax.ppermute(value, axis, [(i, i ^ stride) for i in range(count)])  28.7 us
    pallas_call x1, Pallas kernels, finish_part(): pl.pallas_call(finish_kernel, in_specs=[pl.BlockSpec(memory_space=pltpu.S...  16.1 us
    ppermute x10, starting transfers between devices, swap(): return lax.ppermute(value, axis, [(i, i ^ stride) for i in range(count)])  11.4 us
    pallas_call x1, Pallas kernels, early_part(): pl.pallas_call(early_kernel, grid_spec=pltpu.PrefetchScalarGridSpec(num_s...  10.6 us
    pallas_call x1, Pallas kernels, middle_part(): pl.pallas_call(middle_kernel, grid_spec=pltpu.PrefetchScalarGridSpec(num_...  8 us
    pallas_call x1, Pallas kernels, bath_part(): pl.pallas_call(bath_kernel, grid_spec=pltpu.PrefetchScalarGridSpec(num_sc...  5.46 us
  transfers between devices with their start and end apart: 38, of which 25 were waited for; matrix products, arithmetic and copies ran while one was open for 2% of the time, Pallas kernels for 11%

commit v1 on v0

--- a/solution.py
+++ b/solution.py
@@ -338,10 +338,10 @@
 
 
 def finish_kernel(
-    order_ref, chunks_ref, moved_hbm, bathed_hbm, out_hbm,
+    order_ref, left_ref, right_ref, moved_hbm, bathed_hbm, out_hbm,
     gram, inner, image, start, lowest, moved, bathed, out, in_sems, out_sems,
 ):
-    rank = chunks_ref.shape[0]
+    rank = left_ref.shape[0]
     load_moved = pltpu.make_async_copy(moved_hbm, moved, in_sems.at[0])
     load_bathed = pltpu.make_async_copy(bathed_hbm, bathed, in_sems.at[1])
     load_moved.start()
@@ -353,7 +353,9 @@
     for i in range(chunks):
         rows = pl.ds(pl.multiple_of(order_ref[i] * size, size), size)
         below = pl.ds(pl.multiple_of(rank + order_ref[i] * size, size), size)
-        chunk = chunks_ref[i * size : (i + 1) * size, :]
+        chunk = jnp.concatenate(
+            [left_ref[i * size : (i + 1) * size, :], right_ref[i * size : (i + 1) * size, :]], axis=1
+        )
 
         @pl.when(order_ref[i] < chunks // 2)
         def _():
@@ -422,12 +424,13 @@
     lax.fori_loop(0, pieces, drain, 0)
 
 
-def finish_part(order, chunks, moved, bathed):
+def finish_part(order, left, right, moved, bathed):
     rows, rank = moved.shape
     return pl.pallas_call(
         finish_kernel,
         in_specs=[
             pl.BlockSpec(memory_space=pltpu.SMEM),
+            pl.BlockSpec(memory_space=pltpu.VMEM),
             pl.BlockSpec(memory_space=pltpu.VMEM),
             pl.BlockSpec(memory_space=pltpu.HBM),
             pl.BlockSpec(memory_space=pltpu.HBM),
@@ -448,7 +451,7 @@
         ],
         compiler_params=pltpu.CompilerParams(vmem_limit_bytes=14 * 2**20),
         name="finish",
-    )(order, chunks, moved, bathed)
+    )(order, left, right, moved, bathed)
 
 
 def ring_order(count):
@@ -550,10 +553,6 @@
     return [1 << i for i in range(lax.axis_size(axis).bit_length() - 1)]
 
 
-def halvings():
-    return [("row", stride) for stride in strides("row")] + [("col", 1)]
-
-
 def side_of(axis, stride):
     return (lax.axis_index(axis) >> (stride.bit_length() - 1)) & 1
 
@@ -565,30 +564,27 @@
     return keep + swap(give, *swapped)
 
 
-def sum_relative(value, lower):
-    value = halve(value, ("col", 1), lower)
-    for stride in strides("col")[1:]:
+def sum_relative(value, col_strides):
+    for stride in col_strides:
         value = value + swap(value, "col", stride)
-    for axis, stride in reversed(halvings()):
-        value = jnp.concatenate([value, swap(value, axis, stride)], axis=0)
+    for stride in reversed(strides("row")):
+        value = jnp.concatenate([value, swap(value, "row", stride)], axis=0)
     return value
 
 
 def pack(upper, corner, lower):
     half = corner.shape[1] // 2
-    return jnp.where(
-        lower,
-        jnp.concatenate([upper, corner[:, :half]], axis=1),
-        jnp.concatenate([upper[:, half:], corner], axis=1),
-    )
+    left = jnp.where(lower, upper[:, : 3 * half], upper[:, half:])
+    right = jnp.where(lower, jnp.concatenate([upper[:, 3 * half :], corner[:, :half]], axis=1), corner)
+    return left, right
 
 
 def chunk_order():
-    swaps = halvings()
+    swaps = strides("row")
     relative = jnp.arange(1 << len(swaps), dtype=jnp.int32)
     mine = jnp.zeros_like(relative)
-    for i, (axis, stride) in enumerate(swaps):
-        mine = mine + (side_of(axis, stride) << (len(swaps) - 1 - i))
+    for i, stride in enumerate(swaps):
+        mine = mine + (side_of("row", stride) << (len(swaps) - 1 - i))
     return relative ^ mine
 
 
@@ -608,12 +604,12 @@
     lists = slot_lists(in_group, neighbour_count, coupling_type)
     bathed, corner = bath_part(density_factor, bath_pattern, bath_blocks)
     energy = onsite.reshape(blocks, -1)
-    swaps = halvings()
-    lower = [side_of(axis, stride) == 0 for axis, stride in swaps]
+    swaps = strides("row")
+    lower = [side_of("row", stride) == 0 for stride in swaps]
 
     def over_row(value, lower):
-        for swapped, chosen in zip(swaps[:-1], lower):
-            value = halve(value, swapped, chosen)
+        for stride, chosen in zip(swaps, lower):
+            value = halve(value, ("row", stride), chosen)
         return value
 
     def early(small, pieces):
@@ -631,8 +627,11 @@
     between = [piece for step in steps[early_steps() : -1] for piece in step]
     total = middle_part(lists[1], between, coupling_blocks, total)
     moved, upper = late_part(lists[2], steps[-1], coupling_blocks, total, bathed)
-    gram = pack(over_row(upper, lower), corner, lower[0])
-    return finish_part(order, sum_relative(gram, lower[-1]), moved, bathed)
+    left, right = pack(over_row(upper, lower), corner, lower[0])
+    col_strides = strides("col")
+    left = sum_relative(left, col_strides)
+    right = sum_relative(right, col_strides[1:] + col_strides[:1])
+    return finish_part(order, left, right, moved, bathed)
 
 
 def solution(mesh):

time: 225 us -> 223 us (level)
  starting transfers between devices: 42.6 us -> 48.2 us
  waiting for transfers between devices: 124 us -> 120 us
  Pallas kernels: 45 us -> 42.1 us
    ppermute x10 -> x14, waiting for transfers between devices: 28.7 us -> 20.7 us  [swap(): return lax.ppermute(value, axis, [(i, i ^ stride) for i in range(count)])]
    ppermute x10 -> x14, starting transfers between devices: 11.4 us -> 17 us  [swap(): return lax.ppermute(value, axis, [(i, i ^ stride) for i in range(count)])]
    ppermute x28, waiting for transfers between devices: 95.7 us -> 99 us  [ring_gather(): lax.ppermute(piece, 'col', forward if i < PIECES // 2 else back)]
  transfers between devices with their start and end apart: 38 -> 42, of which waited for: 25 -> 26; matrix products, arithmetic and copies ran while one was open for 2% -> 2% of each run, Pallas kernels for 11% -> 9%
where the time goes in v1:
time: 223 us; the launch traced here: 222 us
  waiting for transfers between devices  120 us (54%)
  starting transfers between devices  48.2 us (22%)
  Pallas kernels  42.1 us (19%)
  local copies, waits for them, and re-layouts  7.58 us (3%)
  other arithmetic  4.17 us (2%)
    ppermute x28, waiting for transfers between devices, ring_gather(): lax.ppermute(piece, 'col', forward if i < PIECES // 2 else back)  99 us
    ppermute x28, starting transfers between devices, ring_gather(): lax.ppermute(piece, 'col', forward if i < PIECES // 2 else back)  31.2 us
    ppermute x14, waiting for transfers between devices, swap(): return lax.ppermute(value, axis, [(i, i ^ stride) for i in range(count)])  20.7 us
    ppermute x14, starting transfers between devices, swap(): return lax.ppermute(value, axis, [(i, i ^ stride) for i in range(count)])  17 us
    pallas_call x1, Pallas kernels, finish_part(): pl.pallas_call(finish_kernel, in_specs=[pl.BlockSpec(memory_space=pltpu.S...  16 us
    pallas_call x1, Pallas kernels, early_part(): pl.pallas_call(early_kernel, grid_spec=pltpu.PrefetchScalarGridSpec(num_s...  8.97 us
    pallas_call x1, Pallas kernels, middle_part(): pl.pallas_call(middle_kernel, grid_spec=pltpu.PrefetchScalarGridSpec(num_...  6.41 us
    pallas_call x1, Pallas kernels, bath_part(): pl.pallas_call(bath_kernel, grid_spec=pltpu.PrefetchScalarGridSpec(num_sc...  5.46 us
  transfers between devices with their start and end apart: 42, of which 26 were waited for; matrix products, arithmetic and copies ran while one was open for 2% of the time, Pallas kernels for 9%

profile of v1, /device:TPU:0, one launch (start us, length us, event | category | flops | bytes accessed | tf_op | source)
XLA Modules:
  0.0 222.2 jit_solution(10620664888338367792)
XLA Ops:
  0.0 3.0 %fusion.13 = (bf16[1024,256]{1,0:T(8,128)(2,1)}, bf16[1024,256]{1,0:T(8,128)(2,1)}, bf16[1024,256]{1,0:T(8,128)(2,1)}, bf16[1024,256]{1,0:T(8,128)(2,1)}) fusion(bf16[4096,256]{1,0:T(8,128)(2,1)} %refs_14_.1), kind=kLoop, calls=%fused_computation.62 | loop fusion | bytes 4194304 | tf_op jit(solution)/shard_map/slice | solution.py:486
  3.0 3.0 %collective-permute-start = (bf16[1024,256]{1,0:T(8,128)(2,1)}, bf16[1024,256]{1,0:T(8,128)(2,1)S(1)}, u32[]{:S(2)}, u32[]{:S(2)}) collective-permute-start(bf16[1024,256]{1,0:T(8,128)(2,1)} %get-tuple-element.93), channel_id=1, source_target_pairs={{1,0},{3,1},{5,3},{7,5},{6,7},{4,6},{2,4},{0,2},{9,8},{11,9},{13,1... | collective-permute-start | bytes 1572872 | tf_op jit(solution)/shard_map/ppermute | solution.py:499
  11.6 5.5 %bath.1 = (bf16[4096,256]{1,0:T(8,128)(2,1)S(1)}, f32[256,256]{1,0:T(8,128)S(1)}) custom-call(s32[8]{0:T(128)S(1)} %copy-done.6, bf16[4,512,512]{2,1,0:T(8,128)(2,1)S(1)} %copy-done.5, bf16[4096,256]{1,0:T(8,128)(2,1)S(1)} %copy-done), custom_call_target="tpu_custom_call" | custom-call | tf_op jit(solution)/shard_map/bath/pallas_call | solution.py:35
  20.1 2.2 collective-permute-start.1
  22.3 8.0 %collective-permute-done.18.refs_3_ = bf16[1024,256]{1,0:T(8,128)(2,1)} collective-permute-done((bf16[1024,256]{1,0:T(8,128)(2,1)}, bf16[1024,256]{1,0:T(8,128)(2,1)}, u32[]{:S(2)}, u32[]{:S(2)}) %collective-permute-start.18) | collective-permute-done | bytes 524320 | tf_op jit(solution)/shard_map/ppermute | solution.py:499
  35.4 2.3 %collective-permute-done.3 = f32[64,256]{1,0:T(8,128)S(1)} collective-permute-done((f32[64,256]{1,0:T(8,128)S(1)}, f32[64,256]{1,0:T(8,128)S(1)}, u32[]{:S(2)}, u32[]{:S(2)}) %collective-permute-start.3) | collective-permute-done | bytes 65568 | tf_op jit(solution)/shard_map/ppermute | solution.py:549
  37.8 3.7 %collective-permute-done.1.refs_8_ = bf16[1024,256]{1,0:T(8,128)(2,1)S(1)} collective-permute-done((bf16[1024,256]{1,0:T(8,128)(2,1)S(1)}, bf16[1024,256]{1,0:T(8,128)(2,1)S(1)}, u32[]{:S(2)}, u32[]{:S(2)}) %collective-permute-start.1) | collective-permute-done | bytes 524320 | tf_op jit(solution)/shard_map/ppermute | solution.py:499
  43.6 9.8 %collective-permute-done.5.refs_5_ = bf16[1024,256]{1,0:T(8,128)(2,1)S(1)} collective-permute-done((bf16[1024,256]{1,0:T(8,128)(2,1)}, bf16[1024,256]{1,0:T(8,128)(2,1)S(1)}, u32[]{:S(2)}, u32[]{:S(2)}) %collective-permute-start.5) | collective-permute-done | bytes 524320 | tf_op jit(solution)/shard_map/ppermute | solution.py:499
  55.7 8.2 %collective-permute-done.25.refs_12_ = bf16[1024,256]{1,0:T(8,128)(2,1)S(1)} collective-permute-done((bf16[1024,256]{1,0:T(8,128)(2,1)S(1)}, bf16[1024,256]{1,0:T(8,128)(2,1)S(1)}, u32[]{:S(2)}, u32[]{:S(2)}) %collective-permute-start.25) | collective-permute-done | bytes 524320 | tf_op jit(solution)/shard_map/ppermute | solution.py:499
  66.0 2.2 collective-permute-done.6.refs_9_
  68.5 11.0 %collective-permute-done.13.refs_10_ = bf16[1024,256]{1,0:T(8,128)(2,1)S(1)} collective-permute-done((bf16[1024,256]{1,0:T(8,128)(2,1)S(1)}, bf16[1024,256]{1,0:T(8,128)(2,1)S(1)}, u32[]{:S(2)}, u32[]{:S(2)}) %collective-permute-start.13) | collective-permute-done | bytes 524320 | tf_op jit(solution)/shard_map/ppermute | solution.py:499
  81.5 4.9 %collective-permute-done.26.refs_3_ = bf16[1024,256]{1,0:T(8,128)(2,1)S(1)} collective-permute-done((bf16[1024,256]{1,0:T(8,128)(2,1)S(1)}, bf16[1024,256]{1,0:T(8,128)(2,1)S(1)}, u32[]{:S(2)}, u32[]{:S(2)}) %collective-permute-start.26) | collective-permute-done | bytes 524320 | tf_op jit(solution)/shard_map/ppermute | solution.py:499
  88.5 2.2 collective-permute-done.7.refs_0_
  91.0 11.0 %collective-permute-done.14.refs_1_ = bf16[1024,256]{1,0:T(8,128)(2,1)S(1)} collective-permute-done((bf16[1024,256]{1,0:T(8,128)(2,1)S(1)}, bf16[1024,256]{1,0:T(8,128)(2,1)S(1)}, u32[]{:S(2)}, u32[]{:S(2)}) %collective-permute-start.14) | collective-permute-done | bytes 524320 | tf_op jit(solution)/shard_map/ppermute | solution.py:499
  105.6 9.0 %couple_early.1.refs_13_ = f32[4096,256]{1,0:T(8,128)S(1)} custom-call(s32[8,8]{1,0:T(8,128)S(1)} %get-tuple-element.71.origin_ref, s32[8,8]{1,0:T(8,128)S(1)} %get-tuple-element.72.offset_ref, s32[8]{0:T(128)S(1)} %broadcast_in_dim.52.first_ref, s32[8]{0:T(128)S(1)} %get-tuple-element.73.count_ref.first_ref, s32[8,8]{1,0:T(8,128)S(1)} %get-tuple-element.75.kind_ref, ...), custom_call_target="tpu_custom_call" | custom-call | flops 4294967296 | bytes 16777216 | tf_op jit(solution)/shard_map/couple_early/pallas_call | solution.py:179
  116.7 7.8 %collective-permute-done.15.refs_5_ = bf16[1024,256]{1,0:T(8,128)(2,1)S(1)} collective-permute-done((bf16[1024,256]{1,0:T(8,128)(2,1)S(1)}, bf16[1024,256]{1,0:T(8,128)(2,1)S(1)}, u32[]{:S(2)}, u32[]{:S(2)}) %collective-permute-start.15) | collective-permute-done | bytes 524320 | tf_op jit(solution)/shard_map/ppermute | solution.py:499
  126.5 4.9 %collective-permute-done.28.refs_11_ = bf16[1024,256]{1,0:T(8,128)(2,1)S(1)} collective-permute-done((bf16[1024,256]{1,0:T(8,128)(2,1)S(1)}, bf16[1024,256]{1,0:T(8,128)(2,1)S(1)}, u32[]{:S(2)}, u32[]{:S(2)}) %collective-permute-start.28) | collective-permute-done | bytes 524320 | tf_op jit(solution)/shard_map/ppermute | solution.py:499
  133.5 2.2 collective-permute-done.9.refs_8_
  135.9 11.0 %collective-permute-done.16.refs_9_ = bf16[1024,256]{1,0:T(8,128)(2,1)S(1)} collective-permute-done((bf16[1024,256]{1,0:T(8,128)(2,1)S(1)}, bf16[1024,256]{1,0:T(8,128)(2,1)S(1)}, u32[]{:S(2)}, u32[]{:S(2)}) %collective-permute-start.16) | collective-permute-done | bytes 524320 | tf_op jit(solution)/shard_map/ppermute | solution.py:499
  148.9 6.4 %couple_middle.1.refs_5_ = f32[4096,256]{1,0:T(8,128)S(1)} custom-call(s32[8,8]{1,0:T(8,128)S(1)} %get-tuple-element.71.origin_ref, s32[8,8]{1,0:T(8,128)S(1)} %get-tuple-element.72.offset_ref, s32[8]{0:T(128)S(1)} %get-tuple-element.73.count_ref.first_ref, s32[8]{0:T(128)S(1)} %get-tuple-element.74.count_ref, s32[8,8]{1,0:T(8,128)S(1)} %get-tuple-element.75.kind_ref, ...), custom_call_target="tpu_custom_call" | custom-call | flops 4294967296 | bytes 16777216 | tf_op jit(solution)/shard_map/couple_middle/pallas_call | solution.py:214
  155.4 2.8 %collective-permute-done.10.refs_0_ = bf16[1024,256]{1,0:T(8,128)(2,1)S(1)} collective-permute-done((bf16[1024,256]{1,0:T(8,128)(2,1)S(1)}, bf16[1024,256]{1,0:T(8,128)(2,1)S(1)}, u32[]{:S(2)}, u32[]{:S(2)}) %collective-permute-start.10) | collective-permute-done | bytes 524320 | tf_op jit(solution)/shard_map/ppermute | solution.py:499
  158.1 8.8 %collective-permute-done.17.refs_1_ = bf16[1024,256]{1,0:T(8,128)(2,1)S(1)} collective-permute-done((bf16[1024,256]{1,0:T(8,128)(2,1)S(1)}, bf16[1024,256]{1,0:T(8,128)(2,1)S(1)}, u32[]{:S(2)}, u32[]{:S(2)}) %collective-permute-start.17) | collective-permute-done | bytes 524320 | tf_op jit(solution)/shard_map/ppermute | solution.py:499
  167.0 5.2 %couple_late.1 = (bf16[4096,256]{1,0:T(8,128)(2,1)S(1)}, f32[256,512]{1,0:T(8,128)S(1)}) custom-call(s32[8,8]{1,0:T(8,128)S(1)} %get-tuple-element.71.origin_ref, s32[8,8]{1,0:T(8,128)S(1)} %get-tuple-element.72.offset_ref, s32[8]{0:T(128)S(1)} %add.90.first_ref, s32[8]{0:T(128)S(1)} %get-tuple-element.53.count_ref, s32[8,8]{1,0:T(8,128)S(1)} %get-tuple-element.75.kind_ref, ...), custom_call_target="tpu_custom_call" | custom-call | tf_op jit(solution)/shard_map/couple_late/pallas_call | solution.py:246
  173.9 2.4 %collective-permute-start.31 = (f32[64,512]{1,0:T(8,128)S(1)}, f32[64,512]{1,0:T(8,128)S(1)}, u32[]{:S(2)}, u32[]{:S(2)}) collective-permute-start(f32[64,512]{1,0:T(8,128)S(1)} %slice_select_fusion.1), channel_id=1, source_target_pairs={{0,16},{8,24},{16,0},{24,8},{1,17},{9,25},{17,1},{25,9},{2,18},{10... | collective-permute-start | bytes 393224 | tf_op jit(solution)/shard_map/ppermute | solution.py:549
  176.4 3.8 %collective-permute-done.31 = f32[64,512]{1,0:T(8,128)S(1)} collective-permute-done((f32[64,512]{1,0:T(8,128)S(1)}, f32[64,512]{1,0:T(8,128)S(1)}, u32[]{:S(2)}, u32[]{:S(2)}) %collective-permute-start.31) | collective-permute-done | bytes 131104 | tf_op jit(solution)/shard_map/ppermute | solution.py:549
  182.5 2.4 %collective-permute-done.32 = f32[64,384]{1,0:T(8,128)S(1)} collective-permute-done((f32[64,384]{1,0:T(8,128)S(1)}, f32[64,384]{1,0:T(8,128)S(1)}, u32[]{:S(2)}, u32[]{:S(2)}) %collective-permute-start.32) | collective-permute-done | bytes 98336 | tf_op jit(solution)/shard_map/ppermute | solution.py:549
  184.9 2.1 collective-permute-start.33
  187.1 4.1 %collective-permute-start.38 = (f32[64,256]{1,0:T(8,128)S(1)}, f32[64,256]{1,0:T(8,128)S(1)}, u32[]{:S(2)}, u32[]{:S(2)}) collective-permute-start(f32[64,256]{1,0:T(8,128)S(1)} %add.98), channel_id=1, source_target_pairs={{0,4},{1,5},{2,6},{3,7},{4,0},{5,1},{6,2},{7,3},{8,12},{9,13},{10,... | collective-permute-start | bytes 196616 | tf_op jit(solution)/shard_map/ppermute | solution.py:549
  191.1 2.9 %collective-permute-done.38 = f32[64,256]{1,0:T(8,128)S(1)} collective-permute-done((f32[64,256]{1,0:T(8,128)S(1)}, f32[64,256]{1,0:T(8,128)S(1)}, u32[]{:S(2)}, u32[]{:S(2)}) %collective-permute-start.38) | collective-permute-done | bytes 65568 | tf_op jit(solution)/shard_map/ppermute | solution.py:549
  194.2 2.3 %collective-permute-start.34 = (f32[64,384]{1,0:T(8,128)S(1)}, f32[64,384]{1,0:T(8,128)S(1)}, u32[]{:S(2)}, u32[]{:S(2)}) collective-permute-start(f32[64,384]{1,0:T(8,128)S(1)} %add.96), channel_id=1, source_target_pairs={{0,4},{1,5},{2,6},{3,7},{4,0},{5,1},{6,2},{7,3},{8,12},{9,13},{10,... | collective-permute-start | bytes 294920 | tf_op jit(solution)/shard_map/ppermute | solution.py:549
  200.6 2.2 collective-permute-done.40
  206.1 16.0 %finish.1 = bf16[4096,256]{1,0:T(8,128)(2,1)} custom-call(s32[4]{0:T(128)S(1)} %iota_xor_fusion.order_ref, f32[256,384]{1,0:T(8,128)S(1)} %pad_maximum_fusion.left_ref, f32[256,256]{1,0:T(8,128)S(1)} %pad_maximum_fusion.1.right_ref, bf16[4096,256]{1,0:T(8,128)(2,1)S(1)} %get-tuple-element.80.moved_hbm, bf16[4096,256]{1,0:T(8,128)(2,1)S(1)} %copy-done.4), custom_call_target="tpu_custom_call" | custom-call | tf_op jit(solution)/shard_map/finish/pallas_call | solution.py:429
  (115 shorter events, 48.5 us)
Async XLA Ops:
  3.0 15.9 %collective-permute-start = (bf16[1024,256]{1,0:T(8,128)(2,1)}, bf16[1024,256]{1,0:T(8,128)(2,1)S(1)}, u32[]{:S(2)}, u32[]{:S(2)}) collective-permute-start(bf16[1024,256]{1,0:T(8,128)(2,1)} %get-tuple-element.93), channel_id=1, source_target_pairs={{1,0},{3,1},{5,3},{7,5},{6,7},{4,6},{2,4},{0,2},{9,8},{11,9},{13,1... | collective-permute-start | bytes 1572872 | tf_op jit(solution)/shard_map/ppermute | solution.py:499
  6.1 16.2 %collective-permute-start.11 = (bf16[1024,256]{1,0:T(8,128)(2,1)}, bf16[1024,256]{1,0:T(8,128)(2,1)S(1)}, u32[]{:S(2)}, u32[]{:S(2)}) collective-permute-start(bf16[1024,256]{1,0:T(8,128)(2,1)} %get-tuple-element.91), channel_id=1, source_target_pairs={{0,1},{1,3},{3,5},{5,7},{7,6},{6,4},{4,2},{2,0},{8,9},{9,11},{11,1... | collective-permute-start | bytes 1572872 | tf_op jit(solution)/shard_map/ppermute | solution.py:499
  6.1 24.2 %collective-permute-start.18 = (bf16[1024,256]{1,0:T(8,128)(2,1)}, bf16[1024,256]{1,0:T(8,128)(2,1)}, u32[]{:S(2)}, u32[]{:S(2)}) collective-permute-start(bf16[1024,256]{1,0:T(8,128)(2,1)} %get-tuple-element.90), channel_id=1, source_target_pairs={{1,0},{3,1},{5,3},{7,5},{6,7},{4,6},{2,4},{0,2},{9,8},{11,9},{13,1... | collective-permute-start | bytes 1572872 | tf_op jit(solution)/shard_map/ppermute | solution.py:499
  8.1 24.4 %collective-permute-start.4 = (bf16[1024,256]{1,0:T(8,128)(2,1)}, bf16[1024,256]{1,0:T(8,128)(2,1)}, u32[]{:S(2)}, u32[]{:S(2)}) collective-permute-start(bf16[1024,256]{1,0:T(8,128)(2,1)} %get-tuple-element.92), channel_id=1, source_target_pairs={{0,1},{1,3},{3,5},{5,7},{7,6},{6,4},{4,2},{2,0},{8,9},{9,11},{11,1... | collective-permute-start | bytes 1572872 | tf_op jit(solution)/shard_map/ppermute | solution.py:499
  19.6 12.8 %collective-permute-start.2 = (f32[128,256]{1,0:T(8,128)}, f32[128,256]{1,0:T(8,128)}, u32[]{:S(2)}, u32[]{:S(2)}) collective-permute-start(f32[128,256]{1,0:T(8,128)} %slice_select_fusion.2), channel_id=1, source_target_pairs={{0,8},{8,0},{16,24},{24,16},{1,9},{9,1},{17,25},{25,17},{2,10},{10... | collective-permute-start | bytes 393224 | tf_op jit(solution)/shard_map/ppermute | solution.py:549
  20.1 21.4 %collective-permute-start.1 = (bf16[1024,256]{1,0:T(8,128)(2,1)S(1)}, bf16[1024,256]{1,0:T(8,128)(2,1)S(1)}, u32[]{:S(2)}, u32[]{:S(2)}) collective-permute-start(bf16[1024,256]{1,0:T(8,128)(2,1)S(1)} %collective-permute-done.refs_4_), channel_id=1, source_target_pairs={{1,0},{3,1},{5,3},{7,5},{6,7},{4,6},{2,4},{0,2},{9,8},{11,9},{13,1... | collective-permute-start | bytes 1572872 | tf_op jit(solution)/shard_map/ppermute | solution.py:499
  22.3 31.4 %collective-permute-start.12 = (bf16[1024,256]{1,0:T(8,128)(2,1)S(1)}, bf16[1024,256]{1,0:T(8,128)(2,1)S(1)}, u32[]{:S(2)}, u32[]{:S(2)}) collective-permute-start(bf16[1024,256]{1,0:T(8,128)(2,1)S(1)} %collective-permute-done.11.refs_2_), channel_id=1, source_target_pairs={{0,1},{1,3},{3,5},{5,7},{7,6},{6,4},{4,2},{2,0},{8,9},{9,11},{11,1... | collective-permute-start | bytes 1572872 | tf_op jit(solution)/shard_map/ppermute | solution.py:499
  30.3 25.0 %collective-permute-start.19 = (bf16[1024,256]{1,0:T(8,128)(2,1)}, bf16[1024,256]{1,0:T(8,128)(2,1)S(1)}, u32[]{:S(2)}, u32[]{:S(2)}) collective-permute-start(bf16[1024,256]{1,0:T(8,128)(2,1)} %collective-permute-done.18.refs_3_), channel_id=1, source_target_pairs={{1,0},{3,1},{5,3},{7,5},{6,7},{4,6},{2,4},{0,2},{9,8},{11,9},{13,1... | collective-permute-start | bytes 1572872 | tf_op jit(solution)/shard_map/ppermute | solution.py:499
  32.5 20.9 %collective-permute-start.5 = (bf16[1024,256]{1,0:T(8,128)(2,1)}, bf16[1024,256]{1,0:T(8,128)(2,1)S(1)}, u32[]{:S(2)}, u32[]{:S(2)}) collective-permute-start(bf16[1024,256]{1,0:T(8,128)(2,1)} %collective-permute-done.4.refs_1_), channel_id=1, source_target_pairs={{0,1},{1,3},{3,5},{5,7},{7,6},{6,4},{4,2},{2,0},{8,9},{9,11},{11,1... | collective-permute-start | bytes 1572872 | tf_op jit(solution)/shard_map/ppermute | solution.py:499
  41.5 22.5 %collective-permute-start.25 = (bf16[1024,256]{1,0:T(8,128)(2,1)S(1)}, bf16[1024,256]{1,0:T(8,128)(2,1)S(1)}, u32[]{:S(2)}, u32[]{:S(2)}) collective-permute-start(bf16[1024,256]{1,0:T(8,128)(2,1)S(1)} %collective-permute-done.1.refs_8_), channel_id=1, source_target_pairs={{1,0},{3,1},{5,3},{7,5},{6,7},{4,6},{2,4},{0,2},{9,8},{11,9},{13,1... | collective-permute-start | bytes 1572872 | tf_op jit(solution)/shard_map/ppermute | solution.py:499
  53.4 14.9 %collective-permute-start.6 = (bf16[1024,256]{1,0:T(8,128)(2,1)S(1)}, bf16[1024,256]{1,0:T(8,128)(2,1)S(1)}, u32[]{:S(2)}, u32[]{:S(2)}) collective-permute-start(bf16[1024,256]{1,0:T(8,128)(2,1)S(1)} %collective-permute-done.5.refs_5_), channel_id=1, source_target_pairs={{0,1},{1,3},{3,5},{5,7},{7,6},{6,4},{4,2},{2,0},{8,9},{9,11},{11,1... | collective-permute-start | bytes 1572872 | tf_op jit(solution)/shard_map/ppermute | solution.py:499
  53.7 25.8 %collective-permute-start.13 = (bf16[1024,256]{1,0:T(8,128)(2,1)S(1)}, bf16[1024,256]{1,0:T(8,128)(2,1)S(1)}, u32[]{:S(2)}, u32[]{:S(2)}) collective-permute-start(bf16[1024,256]{1,0:T(8,128)(2,1)S(1)} %collective-permute-done.12.refs_6_), channel_id=1, source_target_pairs={{0,1},{1,3},{3,5},{5,7},{7,6},{6,4},{4,2},{2,0},{8,9},{9,11},{11,1... | collective-permute-start | bytes 1572872 | tf_op jit(solution)/shard_map/ppermute | solution.py:499
  55.4 24.4 %collective-permute-start.20 = (bf16[1024,256]{1,0:T(8,128)(2,1)S(1)}, bf16[1024,256]{1,0:T(8,128)(2,1)S(1)}, u32[]{:S(2)}, u32[]{:S(2)}) collective-permute-start(bf16[1024,256]{1,0:T(8,128)(2,1)S(1)} %collective-permute-done.19.refs_7_), channel_id=1, source_target_pairs={{1,0},{3,1},{5,3},{7,5},{6,7},{4,6},{2,4},{0,2},{9,8},{11,9},{13,1... | collective-permute-start | bytes 1572872 | tf_op jit(solution)/shard_map/ppermute | solution.py:499
  63.9 22.5 %collective-permute-start.26 = (bf16[1024,256]{1,0:T(8,128)(2,1)S(1)}, bf16[1024,256]{1,0:T(8,128)(2,1)S(1)}, u32[]{:S(2)}, u32[]{:S(2)}) collective-permute-start(bf16[1024,256]{1,0:T(8,128)(2,1)S(1)} %collective-permute-done.25.refs_12_), channel_id=1, source_target_pairs={{1,0},{3,1},{5,3},{7,5},{6,7},{4,6},{2,4},{0,2},{9,8},{11,9},{13,1... | collective-permute-start | bytes 1572872 | tf_op jit(solution)/shard_map/ppermute | solution.py:499
  68.2 22.5 %collective-permute-start.7 = (bf16[1024,256]{1,0:T(8,128)(2,1)S(1)}, bf16[1024,256]{1,0:T(8,128)(2,1)S(1)}, u32[]{:S(2)}, u32[]{:S(2)}) collective-permute-start(bf16[1024,256]{1,0:T(8,128)(2,1)S(1)} %collective-permute-done.6.refs_9_), channel_id=1, source_target_pairs={{0,1},{1,3},{3,5},{5,7},{7,6},{6,4},{4,2},{2,0},{8,9},{9,11},{11,1... | collective-permute-start | bytes 1572872 | tf_op jit(solution)/shard_map/ppermute | solution.py:499
  79.5 22.5 %collective-permute-start.14 = (bf16[1024,256]{1,0:T(8,128)(2,1)S(1)}, bf16[1024,256]{1,0:T(8,128)(2,1)S(1)}, u32[]{:S(2)}, u32[]{:S(2)}) collective-permute-start(bf16[1024,256]{1,0:T(8,128)(2,1)S(1)} %collective-permute-done.13.refs_10_), channel_id=1, source_target_pairs={{0,1},{1,3},{3,5},{5,7},{7,6},{6,4},{4,2},{2,0},{8,9},{9,11},{11,1... | collective-permute-start | bytes 1572872 | tf_op jit(solution)/shard_map/ppermute | solution.py:499
  79.8 22.5 %collective-permute-start.21 = (bf16[1024,256]{1,0:T(8,128)(2,1)S(1)}, bf16[1024,256]{1,0:T(8,128)(2,1)S(1)}, u32[]{:S(2)}, u32[]{:S(2)}) collective-permute-start(bf16[1024,256]{1,0:T(8,128)(2,1)S(1)} %collective-permute-done.20.refs_11_), channel_id=1, source_target_pairs={{1,0},{3,1},{5,3},{7,5},{6,7},{4,6},{2,4},{0,2},{9,8},{11,9},{13,1... | collective-permute-start | bytes 1572872 | tf_op jit(solution)/shard_map/ppermute | solution.py:499
  86.4 28.2 %collective-permute-start.27 = (bf16[1024,256]{1,0:T(8,128)(2,1)S(1)}, bf16[1024,256]{1,0:T(8,128)(2,1)S(1)}, u32[]{:S(2)}, u32[]{:S(2)}) collective-permute-start(bf16[1024,256]{1,0:T(8,128)(2,1)S(1)} %collective-permute-done.26.refs_3_), channel_id=1, source_target_pairs={{1,0},{3,1},{5,3},{7,5},{6,7},{4,6},{2,4},{0,2},{9,8},{11,9},{13,1... | collective-permute-start | bytes 1572872 | tf_op jit(solution)/shard_map/ppermute | solution.py:499
  90.7 24.8 %collective-permute-start.8 = (bf16[1024,256]{1,0:T(8,128)(2,1)S(1)}, bf16[1024,256]{1,0:T(8,128)(2,1)S(1)}, u32[]{:S(2)}, u32[]{:S(2)}) collective-permute-start(bf16[1024,256]{1,0:T(8,128)(2,1)S(1)} %collective-permute-done.7.refs_0_), channel_id=1, source_target_pairs={{0,1},{1,3},{3,5},{5,7},{7,6},{6,4},{4,2},{2,0},{8,9},{9,11},{11,1... | collective-permute-start | bytes 1572872 | tf_op jit(solution)/shard_map/ppermute | solution.py:499
  102.0 22.5 %collective-permute-start.15 = (bf16[1024,256]{1,0:T(8,128)(2,1)S(1)}, bf16[1024,256]{1,0:T(8,128)(2,1)S(1)}, u32[]{:S(2)}, u32[]{:S(2)}) collective-permute-start(bf16[1024,256]{1,0:T(8,128)(2,1)S(1)} %collective-permute-done.14.refs_1_), channel_id=1, source_target_pairs={{0,1},{1,3},{3,5},{5,7},{7,6},{6,4},{4,2},{2,0},{8,9},{9,11},{11,1... | collective-permute-start | bytes 1572872 | tf_op jit(solution)/shard_map/ppermute | solution.py:499
  102.2 22.5 %collective-permute-start.22 = (bf16[1024,256]{1,0:T(8,128)(2,1)S(1)}, bf16[1024,256]{1,0:T(8,128)(2,1)S(1)}, u32[]{:S(2)}, u32[]{:S(2)}) collective-permute-start(bf16[1024,256]{1,0:T(8,128)(2,1)S(1)} %collective-permute-done.21.refs_2_), channel_id=1, source_target_pairs={{1,0},{3,1},{5,3},{7,5},{6,7},{4,6},{2,4},{0,2},{9,8},{11,9},{13,1... | collective-permute-start | bytes 1572872 | tf_op jit(solution)/shard_map/ppermute | solution.py:499
  114.6 16.8 %collective-permute-start.28 = (bf16[1024,256]{1,0:T(8,128)(2,1)S(1)}, bf16[1024,256]{1,0:T(8,128)(2,1)S(1)}, u32[]{:S(2)}, u32[]{:S(2)}) collective-permute-start(bf16[1024,256]{1,0:T(8,128)(2,1)S(1)} %collective-permute-done.27.refs_7_), channel_id=1, source_target_pairs={{1,0},{3,1},{5,3},{7,5},{6,7},{4,6},{2,4},{0,2},{9,8},{11,9},{13,1... | collective-permute-start | bytes 1572872 | tf_op jit(solution)/shard_map/ppermute | solution.py:499
  115.5 20.1 %collective-permute-start.9 = (bf16[1024,256]{1,0:T(8,128)(2,1)S(1)}, bf16[1024,256]{1,0:T(8,128)(2,1)S(1)}, u32[]{:S(2)}, u32[]{:S(2)}) collective-permute-start(bf16[1024,256]{1,0:T(8,128)(2,1)S(1)} %collective-permute-done.8.refs_4_), channel_id=1, source_target_pairs={{0,1},{1,3},{3,5},{5,7},{7,6},{6,4},{4,2},{2,0},{8,9},{9,11},{11,1... | collective-permute-start | bytes 1572872 | tf_op jit(solution)/shard_map/ppermute | solution.py:499
  124.4 22.5 %collective-permute-start.16 = (bf16[1024,256]{1,0:T(8,128)(2,1)S(1)}, bf16[1024,256]{1,0:T(8,128)(2,1)S(1)}, u32[]{:S(2)}, u32[]{:S(2)}) collective-permute-start(bf16[1024,256]{1,0:T(8,128)(2,1)S(1)} %collective-permute-done.15.refs_5_), channel_id=1, source_target_pairs={{0,1},{1,3},{3,5},{5,7},{7,6},{6,4},{4,2},{2,0},{8,9},{9,11},{11,1... | collective-permute-start | bytes 1572872 | tf_op jit(solution)/shard_map/ppermute | solution.py:499
  124.7 22.5 %collective-permute-start.23 = (bf16[1024,256]{1,0:T(8,128)(2,1)S(1)}, bf16[1024,256]{1,0:T(8,128)(2,1)S(1)}, u32[]{:S(2)}, u32[]{:S(2)}) collective-permute-start(bf16[1024,256]{1,0:T(8,128)(2,1)S(1)} %collective-permute-done.22.refs_6_), channel_id=1, source_target_pairs={{1,0},{3,1},{5,3},{7,5},{6,7},{4,6},{2,4},{0,2},{9,8},{11,9},{13,1... | collective-permute-start | bytes 1572872 | tf_op jit(solution)/shard_map/ppermute | solution.py:499
  131.3 24.0 %collective-permute-start.29 = (bf16[1024,256]{1,0:T(8,128)(2,1)S(1)}, bf16[1024,256]{1,0:T(8,128)(2,1)S(1)}, u32[]{:S(2)}, u32[]{:S(2)}) collective-permute-start(bf16[1024,256]{1,0:T(8,128)(2,1)S(1)} %collective-permute-done.28.refs_11_), channel_id=1, source_target_pairs={{1,0},{3,1},{5,3},{7,5},{6,7},{4,6},{2,4},{0,2},{9,8},{11,9},{13,1... | collective-permute-start | bytes 1572872 | tf_op jit(solution)/shard_map/ppermute | solution.py:499
  135.7 22.5 %collective-permute-start.10 = (bf16[1024,256]{1,0:T(8,128)(2,1)S(1)}, bf16[1024,256]{1,0:T(8,128)(2,1)S(1)}, u32[]{:S(2)}, u32[]{:S(2)}) collective-permute-start(bf16[1024,256]{1,0:T(8,128)(2,1)S(1)} %collective-permute-done.9.refs_8_), channel_id=1, source_target_pairs={{0,1},{1,3},{3,5},{5,7},{7,6},{6,4},{4,2},{2,0},{8,9},{9,11},{11,1... | collective-permute-start | bytes 1572872 | tf_op jit(solution)/shard_map/ppermute | solution.py:499
  146.9 20.1 %collective-permute-start.17 = (bf16[1024,256]{1,0:T(8,128)(2,1)S(1)}, bf16[1024,256]{1,0:T(8,128)(2,1)S(1)}, u32[]{:S(2)}, u32[]{:S(2)}) collective-permute-start(bf16[1024,256]{1,0:T(8,128)(2,1)S(1)} %collective-permute-done.16.refs_9_), channel_id=1, source_target_pairs={{0,1},{1,3},{3,5},{5,7},{7,6},{6,4},{4,2},{2,0},{8,9},{9,11},{11,1... | collective-permute-start | bytes 1572872 | tf_op jit(solution)/shard_map/ppermute | solution.py:499
  147.2 19.8 %collective-permute-start.24 = (bf16[1024,256]{1,0:T(8,128)(2,1)S(1)}, bf16[1024,256]{1,0:T(8,128)(2,1)S(1)}, u32[]{:S(2)}, u32[]{:S(2)}) collective-permute-start(bf16[1024,256]{1,0:T(8,128)(2,1)S(1)} %collective-permute-done.23.refs_10_), channel_id=1, source_target_pairs={{1,0},{3,1},{5,3},{7,5},{6,7},{4,6},{2,4},{0,2},{9,8},{11,9},{13,1... | collective-permute-start | bytes 1572872 | tf_op jit(solution)/shard_map/ppermute | solution.py:499
  173.9 6.2 %collective-permute-start.31 = (f32[64,512]{1,0:T(8,128)S(1)}, f32[64,512]{1,0:T(8,128)S(1)}, u32[]{:S(2)}, u32[]{:S(2)}) collective-permute-start(f32[64,512]{1,0:T(8,128)S(1)} %slice_select_fusion.1), channel_id=1, source_target_pairs={{0,16},{8,24},{16,0},{24,8},{1,17},{9,25},{17,1},{25,9},{2,18},{10... | collective-permute-start | bytes 393224 | tf_op jit(solution)/shard_map/ppermute | solution.py:549
  184.9 9.3 %collective-permute-start.33 = (f32[64,384]{1,0:T(8,128)S(1)}, f32[64,384]{1,0:T(8,128)S(1)}, u32[]{:S(2)}, u32[]{:S(2)}) collective-permute-start(f32[64,384]{1,0:T(8,128)S(1)} %fusion.14), channel_id=1, source_target_pairs={{0,2},{1,3},{2,0},{3,1},{4,6},{5,7},{6,4},{7,5},{8,10},{9,11},{10,... | collective-permute-start | bytes 294920 | tf_op jit(solution)/shard_map/ppermute | solution.py:549
  187.1 7.0 %collective-permute-start.38 = (f32[64,256]{1,0:T(8,128)S(1)}, f32[64,256]{1,0:T(8,128)S(1)}, u32[]{:S(2)}, u32[]{:S(2)}) collective-permute-start(f32[64,256]{1,0:T(8,128)S(1)} %add.98), channel_id=1, source_target_pairs={{0,4},{1,5},{2,6},{3,7},{4,0},{5,1},{6,2},{7,3},{8,12},{9,13},{10,... | collective-permute-start | bytes 196616 | tf_op jit(solution)/shard_map/ppermute | solution.py:549
  (22 other events, 201.3 us)

commit v2 on v1

--- a/solution.py
+++ b/solution.py
@@ -52,23 +52,31 @@
     )(bath_pattern, bath_blocks, own)
 
 
-def gather_products(origin_ref, offset_ref, first_ref, count_ref, kind_ref, sources, coupling_ref, held, sems, total):
+def gather_products(
+    origin_ref, offset_ref, first_ref, count_ref, kind_ref, sources, coupling_ref, held, sems, total, visits=None
+):
     blocks, slots = origin_ref.shape
     block_rows = held.shape[2]
-    b = pl.program_id(0)
+    here = pl.program_id(0)
+    last = blocks if visits is None else visits[1][0]
     group = 1
     while group * group < len(sources):
         group += 1
 
-    def copy(source, block, slot):
-        start = pl.multiple_of(offset_ref[block, slot] * block_rows, block_rows)
+    def block_of(step):
+        return step if visits is None else visits[0][step]
+
+    def copy(source, step, slot):
+        start = pl.multiple_of(offset_ref[block_of(step), slot] * block_rows, block_rows)
         return pltpu.make_async_copy(
             source.at[pl.ds(start, block_rows), :],
-            held.at[lax.rem(block, 2), slot],
-            sems.at[lax.rem(block, 2), slot],
+            held.at[lax.rem(step, 2), slot],
+            sems.at[lax.rem(step, 2), slot],
         )
 
-    def fetch(block):
+    def fetch(step):
+        block = block_of(step)
+
         def one(slot, carry):
             origin = origin_ref[block, slot]
             for low in range(0, len(sources), group):
@@ -79,24 +87,26 @@
                     for place in range(low, high):
                         @pl.when(origin == place)
                         def _():
-                            copy(sources[place], block, slot).start()
+                            copy(sources[place], step, slot).start()
             return carry
 
         lax.fori_loop(first_ref[block], first_ref[block] + count_ref[block], one, 0)
 
-    @pl.when(b == 0)
+    @pl.when(here == 0)
     def _():
         fetch(0)
 
-    @pl.when(b + 1 < blocks)
-    def _():
-        fetch(b + 1)
+    @pl.when(here + 1 < last)
+    def _():
+        fetch(here + 1)
+
+    b = block_of(here)
 
     def product(slot):
-        copy(sources[0], b, slot).wait()
+        copy(sources[0], here, slot).wait()
         return jnp.dot(
             coupling_ref[kind_ref[b, slot]],
-            held[lax.rem(b, 2), slot],
+            held[lax.rem(here, 2), slot],
             preferred_element_type=jnp.float32,
         )
 
@@ -147,28 +157,50 @@
     )
 
 
-def late_kernel(origin_ref, offset_ref, first_ref, count_ref, kind_ref, *refs):
+def gram_part(moved, bathed):
+    both = jnp.concatenate([moved, bathed], axis=1)
+    return lax.dot_general(moved, both, (((0,), (0,)), ((), ())), preferred_element_type=jnp.float32)
+
+
+def settle_kernel(origin_ref, offset_ref, first_ref, count_ref, kind_ref, settled_ref, *refs):
     sources = refs[:-8]
-    coupling_ref, base_ref, bathed_ref, moved_ref, gram_ref, total, held, sems = refs[-8:]
+    coupling_ref, base_ref, bathed_ref, total_ref, moved_ref, gram_ref, held, sems = refs[-8:]
     b = pl.program_id(0)
-    total[...] = base_ref[...]
+    total_ref[...] = base_ref[...]
     gather_products(
-        origin_ref, offset_ref, first_ref, count_ref, kind_ref, sources, coupling_ref, held, sems, total
-    )
-    moved = total[...].astype(jnp.bfloat16)
+        origin_ref, offset_ref, first_ref, count_ref, kind_ref, sources, coupling_ref, held, sems, total_ref
+    )
+    moved = total_ref[...].astype(jnp.bfloat16)
     moved_ref[...] = moved
-    both = jnp.concatenate([moved, bathed_ref[...]], axis=1)
-    part = lax.dot_general(
-        moved, both, (((0,), (0,)), ((), ())), preferred_element_type=jnp.float32
-    )
 
     @pl.when(b == 0)
     def _():
-        gram_ref[...] = part
-
-    @pl.when(b > 0)
-    def _():
-        gram_ref[...] += part
+        gram_ref[...] = jnp.zeros_like(gram_ref)
+
+    @pl.when(settled_ref[b] == 1)
+    def _():
+        gram_ref[...] += gram_part(moved, bathed_ref[...])
+
+
+def late_kernel(origin_ref, offset_ref, first_ref, count_ref, kind_ref, visit_ref, number_ref, *refs):
+    sources = refs[:-10]
+    coupling_ref, base_ref, bathed_ref, _, before_ref, moved_ref, gram_ref, total, held, sems = refs[-10:]
+    b = pl.program_id(0)
+
+    @pl.when(b == 0)
+    def _():
+        gram_ref[...] = before_ref[...]
+
+    @pl.when(b < number_ref[0])
+    def _():
+        total[...] = base_ref[...]
+        gather_products(
+            origin_ref, offset_ref, first_ref, count_ref, kind_ref, sources, coupling_ref, held, sems, total,
+            visits=(visit_ref, number_ref),
+        )
+        moved = total[...].astype(jnp.bfloat16)
+        moved_ref[...] = moved
+        gram_ref[...] += gram_part(moved, bathed_ref[...])
 
 
 def early_part(lists, sources, coupling_blocks, own, energy):
@@ -238,15 +270,15 @@
     )(*lists, *sources, coupling_blocks, base)
 
 
-def late_part(lists, sources, coupling_blocks, base, bathed):
+def settle_part(lists, settled, sources, coupling_blocks, base, bathed):
     blocks, slots = lists[0].shape
     kinds, block_rows, _ = coupling_blocks.shape
     rows, rank = base.shape
     tile = pl.BlockSpec((block_rows, rank), lambda b, *_: (b, 0))
     return pl.pallas_call(
-        late_kernel,
+        settle_kernel,
         grid_spec=pltpu.PrefetchScalarGridSpec(
-            num_scalar_prefetch=5,
+            num_scalar_prefetch=6,
             grid=(blocks,),
             in_specs=[
                 *[pl.BlockSpec(memory_space=pl.ANY) for _ in sources],
@@ -254,7 +286,51 @@
                 tile,
                 tile,
             ],
-            out_specs=[tile, pl.BlockSpec((rank, 2 * rank), lambda b, *_: (0, 0))],
+            out_specs=[tile, tile, pl.BlockSpec((rank, 2 * rank), lambda b, *_: (0, 0))],
+            scratch_shapes=[
+                pltpu.VMEM((2, slots, block_rows, rank), jnp.bfloat16),
+                pltpu.SemaphoreType.DMA((2, slots)),
+            ],
+        ),
+        out_shape=[
+            jax.ShapeDtypeStruct((rows, rank), jnp.float32),
+            jax.ShapeDtypeStruct((rows, rank), jnp.bfloat16),
+            jax.ShapeDtypeStruct((rank, 2 * rank), jnp.float32),
+        ],
+        compiler_params=pltpu.CompilerParams(vmem_limit_bytes=16 * 2**20),
+        cost_estimate=pl.CostEstimate(
+            flops=blocks * slots * block_rows * block_rows * rank,
+            bytes_accessed=blocks * slots * block_rows * rank * 2,
+            transcendentals=0,
+        ),
+        name="couple_settle",
+    )(*lists, settled, *sources, coupling_blocks, base, bathed)
+
+
+def late_part(lists, visits, number, sources, coupling_blocks, base, bathed, moved, gram):
+    blocks, slots = lists[0].shape
+    kinds, block_rows, _ = coupling_blocks.shape
+    rows, rank = base.shape
+
+    def visited(b, *scalars):
+        return scalars[5][jnp.minimum(b, scalars[6][0] - 1)], 0
+
+    tile = pl.BlockSpec((block_rows, rank), visited)
+    whole = pl.BlockSpec((rank, 2 * rank), lambda b, *_: (0, 0))
+    return pl.pallas_call(
+        late_kernel,
+        grid_spec=pltpu.PrefetchScalarGridSpec(
+            num_scalar_prefetch=7,
+            grid=(blocks,),
+            in_specs=[
+                *[pl.BlockSpec(memory_space=pl.ANY) for _ in sources],
+                pl.BlockSpec((kinds, block_rows, block_rows), lambda b, *_: (0, 0, 0)),
+                tile,
+                tile,
+                pl.BlockSpec(memory_space=pl.ANY),
+                whole,
+            ],
+            out_specs=[tile, whole],
             scratch_shapes=[
                 pltpu.VMEM((block_rows, rank), jnp.float32),
                 pltpu.VMEM((2, slots, block_rows, rank), jnp.bfloat16),
@@ -265,9 +341,10 @@
             jax.ShapeDtypeStruct((rows, rank), jnp.bfloat16),
             jax.ShapeDtypeStruct((rank, 2 * rank), jnp.float32),
         ],
-        compiler_params=pltpu.CompilerParams(vmem_limit_bytes=14 * 2**20),
+        input_output_aliases={7 + len(sources) + 3: 0},
+        compiler_params=pltpu.CompilerParams(vmem_limit_bytes=16 * 2**20),
         name="couple_late",
-    )(*lists, *sources, coupling_blocks, base, bathed)
+    )(*lists, visits, number, *sources, coupling_blocks, base, bathed, moved, gram)
 
 
 def inverse_factor(square, start, lowest):
@@ -518,16 +595,18 @@
     piece = within // in_piece
     step = jnp.where(piece >= PIECES // 2, theirs - mine, mine - theirs) % count
     before = early_steps()
-    part = (step > before).astype(jnp.int32) + (step == count - 1).astype(jnp.int32)
+    last = step == count - 1
+    outer = (piece == 0) | (piece == PIECES - 1)
+    part = (step > before).astype(jnp.int32) + last.astype(jnp.int32) + (last & ~outer).astype(jnp.int32)
     origin = jnp.where(
         part == 0,
         jnp.where(step == 0, 0, 1 + (step - 1) * PIECES + piece),
-        jnp.where(part == 1, (step - before - 1) * PIECES + piece, piece),
+        jnp.where(part == 1, (step - before - 1) * PIECES + piece, jnp.where(outer, piece // (PIECES - 1), piece - 1)),
     )
     offset = jnp.where(step == 0, within, within % in_piece)
     slot = jnp.arange(slots, dtype=jnp.int32)
     used = slot[None, :] < counts[:, None]
-    key = jnp.where(used, part, 3) * slots + slot
+    key = jnp.where(used, part, 4) * slots + slot
     rank = jnp.sum((key[:, None, :] < key[:, :, None]).astype(jnp.int32), axis=-1)
     at = rank[:, :, None] == slot
 
@@ -537,11 +616,17 @@
     origin, offset, kinds = arrange(origin), arrange(offset), arrange(kinds)
     parts = []
     first = jnp.zeros_like(counts)
-    for i in range(3):
+    for i in range(4):
         number = jnp.sum((used & (part == i)).astype(jnp.int32), axis=1)
         parts.append((origin, offset, first, number, kinds))
         first = first + number
-    return parts
+    block = jnp.arange(blocks, dtype=jnp.int32)
+    key = jnp.where(parts[3][3] > 0, 0, blocks) + block
+    turn = jnp.sum((key[None, :] < key[:, None]).astype(jnp.int32), axis=1)
+    number = jnp.maximum(jnp.sum((parts[3][3] > 0).astype(jnp.int32), keepdims=True), 1)
+    visits = jnp.sum(jnp.where(turn[:, None] == block, block[:, None], 0), axis=0)
+    settled = (turn >= number).astype(jnp.int32)
+    return parts, settled, visits, number
 
 
 def swap(value, axis, stride):
@@ -613,7 +698,7 @@
         return value
 
     def early(small, pieces):
-        lists, energy, _, _ = small
+        (lists, _, _, _), energy, _, _ = small
         return early_part(lists[0], [density_factor] + pieces, coupling_blocks, density_factor, energy)
 
     steps, corner, small, total = ring_gather(
@@ -623,10 +708,12 @@
         (lists, energy, chunk_order(), lower),
         early,
     )
-    lists, _, order, lower = small
+    (lists, settled, visits, number), _, order, lower = small
     between = [piece for step in steps[early_steps() : -1] for piece in step]
     total = middle_part(lists[1], between, coupling_blocks, total)
-    moved, upper = late_part(lists[2], steps[-1], coupling_blocks, total, bathed)
+    outer, inner = [steps[-1][0], steps[-1][-1]], steps[-1][1:-1]
+    total, moved, upper = settle_part(lists[2], settled, outer, coupling_blocks, total, bathed)
+    moved, upper = late_part(lists[3], visits, number, inner, coupling_blocks, total, bathed, moved, upper)
     left, right = pack(over_row(upper, lower), corner, lower[0])
     col_strides = strides("col")
     left = sum_relative(left, col_strides)

time: 223 us -> 220 us (0.987)
  waiting for transfers between devices: 120 us -> 111 us
  Pallas kernels: 42.1 us -> 47.7 us
    ppermute x28, waiting for transfers between devices: 99 us -> 88.5 us  [ring_gather(): lax.ppermute(piece, 'col', forward if i < PIECES // 2 else back)]
    pallas_call x0 -> x1, Pallas kernels: none -> 5.21 us  [settle_part(): pl.pallas_call(settle_kernel, grid_spec=pltpu.PrefetchScalarGridSpec(num_...]
    ppermute x14, starting transfers between devices: 17 us -> 14.6 us  [swap(): return lax.ppermute(value, axis, [(i, i ^ stride) for i in range(count)])]
  transfers between devices with their start and end apart: 42 -> 42, of which waited for: 26 -> 29; matrix products, arithmetic and copies ran while one was open for 2% -> 2% of each run, Pallas kernels for 9% -> 13%
where the time goes in v2:
time: 220 us
  waiting for transfers between devices  111 us (50%)
  starting transfers between devices  47.8 us (22%)
  Pallas kernels  47.7 us (22%)
  local copies, waits for them, and re-layouts  7.55 us (3%)
  other arithmetic  5.09 us (2%)
    ppermute x28, waiting for transfers between devices, ring_gather(): lax.ppermute(piece, 'col', forward if i < PIECES // 2 else back)  88.5 us
    ppermute x28, starting transfers between devices, ring_gather(): lax.ppermute(piece, 'col', forward if i < PIECES // 2 else back)  33.2 us
    ppermute x14, waiting for transfers between devices, swap(): return lax.ppermute(value, axis, [(i, i ^ stride) for i in range(count)])  22.6 us
    pallas_call x1, Pallas kernels, finish_part(): pl.pallas_call(finish_kernel, in_specs=[pl.BlockSpec(memory_space=pltpu.S...  16 us
    ppermute x14, starting transfers between devices, swap(): return lax.ppermute(value, axis, [(i, i ^ stride) for i in range(count)])  14.6 us
    pallas_call x1, Pallas kernels, early_part(): pl.pallas_call(early_kernel, grid_spec=pltpu.PrefetchScalarGridSpec(num_s...  10.2 us
    pallas_call x1, Pallas kernels, middle_part(): pl.pallas_call(middle_kernel, grid_spec=pltpu.PrefetchScalarGridSpec(num_...  7.46 us
    pallas_call x1, Pallas kernels, bath_part(): pl.pallas_call(bath_kernel, grid_spec=pltpu.PrefetchScalarGridSpec(num_sc...  5.46 us
  transfers between devices with their start and end apart: 42, of which 29 were waited for; matrix products, arithmetic and copies ran while one was open for 2% of the time, Pallas kernels for 13%

profile of v2, /device:TPU:0, one launch (start us, length us, event | category | flops | bytes accessed | tf_op | source)
XLA Modules:
  0.0 220.4 jit_solution(9438522369321037407)
XLA Ops:
  0.0 3.0 %fusion.21 = (bf16[1024,256]{1,0:T(8,128)(2,1)}, bf16[1024,256]{1,0:T(8,128)(2,1)}, bf16[1024,256]{1,0:T(8,128)(2,1)}, bf16[1024,256]{1,0:T(8,128)(2,1)}) fusion(bf16[4096,256]{1,0:T(8,128)(2,1)} %refs_14_.1), kind=kLoop, calls=%fused_computation.81 | loop fusion | bytes 4194304 | tf_op jit(solution)/shard_map/slice | solution.py:563
  3.0 3.0 %collective-permute-start = (bf16[1024,256]{1,0:T(8,128)(2,1)}, bf16[1024,256]{1,0:T(8,128)(2,1)S(1)}, u32[]{:S(2)}, u32[]{:S(2)}) collective-permute-start(bf16[1024,256]{1,0:T(8,128)(2,1)} %get-tuple-element.119), channel_id=1, source_target_pairs={{1,0},{3,1},{5,3},{7,5},{6,7},{4,6},{2,4},{0,2},{9,8},{11,9},{13,1... | collective-permute-start | bytes 1572872 | tf_op jit(solution)/shard_map/ppermute | solution.py:576
  13.0 5.5 %bath.1 = (bf16[4096,256]{1,0:T(8,128)(2,1)S(1)}, f32[256,256]{1,0:T(8,128)S(1)}) custom-call(s32[8]{0:T(128)S(1)} %copy-done.6, bf16[4,512,512]{2,1,0:T(8,128)(2,1)S(1)} %copy-done.5, bf16[4096,256]{1,0:T(8,128)(2,1)S(1)} %copy-done), custom_call_target="tpu_custom_call" | custom-call | tf_op jit(solution)/shard_map/bath/pallas_call | solution.py:35
  23.1 7.1 %collective-permute-done.11.refs_3_ = bf16[1024,256]{1,0:T(8,128)(2,1)S(1)} collective-permute-done((bf16[1024,256]{1,0:T(8,128)(2,1)}, bf16[1024,256]{1,0:T(8,128)(2,1)S(1)}, u32[]{:S(2)}, u32[]{:S(2)}) %collective-permute-start.11) | collective-permute-done | bytes 524320 | tf_op jit(solution)/shard_map/ppermute | solution.py:576
  36.8 2.8 %collective-permute-done.3 = f32[64,256]{1,0:T(8,128)S(1)} collective-permute-done((f32[64,256]{1,0:T(8,128)S(1)}, f32[64,256]{1,0:T(8,128)S(1)}, u32[]{:S(2)}, u32[]{:S(2)}) %collective-permute-start.3) | collective-permute-done | bytes 65568 | tf_op jit(solution)/shard_map/ppermute | solution.py:634
  43.6 3.8 %collective-permute-done.19.refs_5_ = bf16[1024,256]{1,0:T(8,128)(2,1)S(1)} collective-permute-done((bf16[1024,256]{1,0:T(8,128)(2,1)}, bf16[1024,256]{1,0:T(8,128)(2,1)S(1)}, u32[]{:S(2)}, u32[]{:S(2)}) %collective-permute-start.19) | collective-permute-done | bytes 524320 | tf_op jit(solution)/shard_map/ppermute | solution.py:576
  47.4 5.3 %collective-permute-done.12.refs_7_ = bf16[1024,256]{1,0:T(8,128)(2,1)S(1)} collective-permute-done((bf16[1024,256]{1,0:T(8,128)(2,1)S(1)}, bf16[1024,256]{1,0:T(8,128)(2,1)S(1)}, u32[]{:S(2)}, u32[]{:S(2)}) %collective-permute-start.12) | collective-permute-done | bytes 524320 | tf_op jit(solution)/shard_map/ppermute | solution.py:576
  54.8 3.8 %collective-permute-done.5.refs_6_ = bf16[1024,256]{1,0:T(8,128)(2,1)S(1)} collective-permute-done((bf16[1024,256]{1,0:T(8,128)(2,1)}, bf16[1024,256]{1,0:T(8,128)(2,1)S(1)}, u32[]{:S(2)}, u32[]{:S(2)}) %collective-permute-start.5) | collective-permute-done | bytes 524320 | tf_op jit(solution)/shard_map/ppermute | solution.py:576
  58.6 5.3 %collective-permute-done.25.refs_12_ = bf16[1024,256]{1,0:T(8,128)(2,1)S(1)} collective-permute-done((bf16[1024,256]{1,0:T(8,128)(2,1)S(1)}, bf16[1024,256]{1,0:T(8,128)(2,1)S(1)}, u32[]{:S(2)}, u32[]{:S(2)}) %collective-permute-start.25) | collective-permute-done | bytes 524320 | tf_op jit(solution)/shard_map/ppermute | solution.py:576
  66.0 3.8 %collective-permute-done.20.refs_9_ = bf16[1024,256]{1,0:T(8,128)(2,1)S(1)} collective-permute-done((bf16[1024,256]{1,0:T(8,128)(2,1)S(1)}, bf16[1024,256]{1,0:T(8,128)(2,1)S(1)}, u32[]{:S(2)}, u32[]{:S(2)}) %collective-permute-start.20) | collective-permute-done | bytes 524320 | tf_op jit(solution)/shard_map/ppermute | solution.py:576
  69.9 5.3 %collective-permute-done.13.refs_11_ = bf16[1024,256]{1,0:T(8,128)(2,1)S(1)} collective-permute-done((bf16[1024,256]{1,0:T(8,128)(2,1)S(1)}, bf16[1024,256]{1,0:T(8,128)(2,1)S(1)}, u32[]{:S(2)}, u32[]{:S(2)}) %collective-permute-start.13) | collective-permute-done | bytes 524320 | tf_op jit(solution)/shard_map/ppermute | solution.py:576
  77.3 3.8 %collective-permute-done.6.refs_10_ = bf16[1024,256]{1,0:T(8,128)(2,1)S(1)} collective-permute-done((bf16[1024,256]{1,0:T(8,128)(2,1)S(1)}, bf16[1024,256]{1,0:T(8,128)(2,1)S(1)}, u32[]{:S(2)}, u32[]{:S(2)}) %collective-permute-start.6) | collective-permute-done | bytes 524320 | tf_op jit(solution)/shard_map/ppermute | solution.py:576
  81.1 5.3 %collective-permute-done.26.refs_3_ = bf16[1024,256]{1,0:T(8,128)(2,1)S(1)} collective-permute-done((bf16[1024,256]{1,0:T(8,128)(2,1)S(1)}, bf16[1024,256]{1,0:T(8,128)(2,1)S(1)}, u32[]{:S(2)}, u32[]{:S(2)}) %collective-permute-start.26) | collective-permute-done | bytes 524320 | tf_op jit(solution)/shard_map/ppermute | solution.py:576
  88.5 3.8 %collective-permute-done.21.refs_0_ = bf16[1024,256]{1,0:T(8,128)(2,1)S(1)} collective-permute-done((bf16[1024,256]{1,0:T(8,128)(2,1)S(1)}, bf16[1024,256]{1,0:T(8,128)(2,1)S(1)}, u32[]{:S(2)}, u32[]{:S(2)}) %collective-permute-start.21) | collective-permute-done | bytes 524320 | tf_op jit(solution)/shard_map/ppermute | solution.py:576
  92.3 5.3 %collective-permute-done.14.refs_2_ = bf16[1024,256]{1,0:T(8,128)(2,1)S(1)} collective-permute-done((bf16[1024,256]{1,0:T(8,128)(2,1)S(1)}, bf16[1024,256]{1,0:T(8,128)(2,1)S(1)}, u32[]{:S(2)}, u32[]{:S(2)}) %collective-permute-start.14) | collective-permute-done | bytes 524320 | tf_op jit(solution)/shard_map/ppermute | solution.py:576
  99.7 3.8 %collective-permute-done.7.refs_1_ = bf16[1024,256]{1,0:T(8,128)(2,1)S(1)} collective-permute-done((bf16[1024,256]{1,0:T(8,128)(2,1)S(1)}, bf16[1024,256]{1,0:T(8,128)(2,1)S(1)}, u32[]{:S(2)}, u32[]{:S(2)}) %collective-permute-start.7) | collective-permute-done | bytes 524320 | tf_op jit(solution)/shard_map/ppermute | solution.py:576
  105.2 10.2 %couple_early.1.refs_13_ = f32[4096,256]{1,0:T(8,128)S(1)} custom-call(s32[8,8]{1,0:T(8,128)S(1)} %get-tuple-element.90.origin_ref, s32[8,8]{1,0:T(8,128)S(1)} %get-tuple-element.91.offset_ref, s32[8]{0:T(128)S(1)} %broadcast_in_dim.76.first_ref, s32[8]{0:T(128)S(1)} %get-tuple-element.92.count_ref.first_ref, s32[8,8]{1,0:T(8,128)S(1)} %get-tuple-element.94.kind_ref, ...), custom_call_target="tpu_custom_call" | custom-call | flops 4294967296 | bytes 16777216 | tf_op jit(solution)/shard_map/couple_early/pallas_call | solution.py:211
  116.4 3.5 %collective-permute-start.23 = (bf16[1024,256]{1,0:T(8,128)(2,1)S(1)}, bf16[1024,256]{1,0:T(8,128)(2,1)S(1)}, u32[]{:S(2)}, u32[]{:S(2)}) collective-permute-start(bf16[1024,256]{1,0:T(8,128)(2,1)S(1)} %collective-permute-done.22.refs_4_), channel_id=1, source_target_pairs={{0,1},{1,3},{3,5},{5,7},{7,6},{6,4},{4,2},{2,0},{8,9},{9,11},{11,1... | collective-permute-start | bytes 1572872 | tf_op jit(solution)/shard_map/ppermute | solution.py:576
  120.0 6.1 %collective-permute-done.8.refs_5_ = bf16[1024,256]{1,0:T(8,128)(2,1)S(1)} collective-permute-done((bf16[1024,256]{1,0:T(8,128)(2,1)S(1)}, bf16[1024,256]{1,0:T(8,128)(2,1)S(1)}, u32[]{:S(2)}, u32[]{:S(2)}) %collective-permute-start.8) | collective-permute-done | bytes 524320 | tf_op jit(solution)/shard_map/ppermute | solution.py:576
  128.1 4.7 %collective-permute-done.28.refs_11_ = bf16[1024,256]{1,0:T(8,128)(2,1)S(1)} collective-permute-done((bf16[1024,256]{1,0:T(8,128)(2,1)S(1)}, bf16[1024,256]{1,0:T(8,128)(2,1)S(1)}, u32[]{:S(2)}, u32[]{:S(2)}) %collective-permute-start.28) | collective-permute-done | bytes 524320 | tf_op jit(solution)/shard_map/ppermute | solution.py:576
  133.4 3.8 %collective-permute-done.23.refs_8_ = bf16[1024,256]{1,0:T(8,128)(2,1)S(1)} collective-permute-done((bf16[1024,256]{1,0:T(8,128)(2,1)S(1)}, bf16[1024,256]{1,0:T(8,128)(2,1)S(1)}, u32[]{:S(2)}, u32[]{:S(2)}) %collective-permute-start.23) | collective-permute-done | bytes 524320 | tf_op jit(solution)/shard_map/ppermute | solution.py:576
  137.3 11.2 %collective-permute-done.9.refs_9_ = bf16[1024,256]{1,0:T(8,128)(2,1)S(1)} collective-permute-done((bf16[1024,256]{1,0:T(8,128)(2,1)S(1)}, bf16[1024,256]{1,0:T(8,128)(2,1)S(1)}, u32[]{:S(2)}, u32[]{:S(2)}) %collective-permute-start.9) | collective-permute-done | bytes 524320 | tf_op jit(solution)/shard_map/ppermute | solution.py:576
  150.5 7.5 %couple_middle.1.refs_3_ = f32[4096,256]{1,0:T(8,128)S(1)} custom-call(s32[8,8]{1,0:T(8,128)S(1)} %get-tuple-element.90.origin_ref, s32[8,8]{1,0:T(8,128)S(1)} %get-tuple-element.91.offset_ref, s32[8]{0:T(128)S(1)} %get-tuple-element.92.count_ref.first_ref, s32[8]{0:T(128)S(1)} %get-tuple-element.93.count_ref, s32[8,8]{1,0:T(8,128)S(1)} %get-tuple-element.94.kind_ref, ...), custom_call_target="tpu_custom_call" | custom-call | flops 4294967296 | bytes 16777216 | tf_op jit(solution)/shard_map/couple_middle/pallas_call | solution.py:246
  159.7 5.2 %couple_settle.1 = (f32[4096,256]{1,0:T(8,128)S(1)}, bf16[4096,256]{1,0:T(8,128)(2,1)S(1)}, f32[256,512]{1,0:T(8,128)S(1)}) custom-call(s32[8,8]{1,0:T(8,128)S(1)} %get-tuple-element.90.origin_ref, s32[8,8]{1,0:T(8,128)S(1)} %get-tuple-element.91.offset_ref, s32[8]{0:T(128)S(1)} %get-tuple-element.70.first_ref, s32[8]{0:T(128)S(1)} %get-tuple-element.71.count_ref, ...), custom_call_target="tpu_custom_call" | custom-call | flops 4294967296 | bytes 16777216 | tf_op jit(solution)/shard_map/couple_settle/pallas_call | solution.py:278
  165.0 2.6 %collective-permute-done.10.refs_0_ = bf16[1024,256]{1,0:T(8,128)(2,1)S(1)} collective-permute-done((bf16[1024,256]{1,0:T(8,128)(2,1)S(1)}, bf16[1024,256]{1,0:T(8,128)(2,1)S(1)}, u32[]{:S(2)}, u32[]{:S(2)}) %collective-permute-start.10) | collective-permute-done | bytes 524320 | tf_op jit(solution)/shard_map/ppermute | solution.py:576
  167.6 3.4 %couple_late.1 = (bf16[4096,256]{1,0:T(8,128)(2,1)S(1)}, f32[256,512]{1,0:T(8,128)S(1)}) custom-call(s32[8,8]{1,0:T(8,128)S(1)} %get-tuple-element.90.origin_ref, s32[8,8]{1,0:T(8,128)S(1)} %get-tuple-element.91.offset_ref, s32[8]{0:T(128)S(1)} %get-tuple-element.63.first_ref, s32[8]{0:T(128)S(1)} %get-tuple-element.64.count_ref, ...), custom_call_target="tpu_custom_call", output_to_operand_aliasing={{0}: (12, {})} | custom-call | tf_op jit(solution)/shard_map/couple_late/pallas_call | solution.py:320
  173.6 4.7 %collective-permute-done.31 = f32[64,512]{1,0:T(8,128)S(1)} collective-permute-done((f32[64,512]{1,0:T(8,128)S(1)}, f32[64,512]{1,0:T(8,128)S(1)}, u32[]{:S(2)}, u32[]{:S(2)}) %collective-permute-start.31) | collective-permute-done | bytes 131104 | tf_op jit(solution)/shard_map/ppermute | solution.py:634
  180.6 2.4 %collective-permute-done.32 = f32[64,384]{1,0:T(8,128)S(1)} collective-permute-done((f32[64,384]{1,0:T(8,128)S(1)}, f32[64,384]{1,0:T(8,128)S(1)}, u32[]{:S(2)}, u32[]{:S(2)}) %collective-permute-start.32) | collective-permute-done | bytes 98336 | tf_op jit(solution)/shard_map/ppermute | solution.py:634
  186.7 3.7 %collective-permute-done.38 = f32[64,256]{1,0:T(8,128)S(1)} collective-permute-done((f32[64,256]{1,0:T(8,128)S(1)}, f32[64,256]{1,0:T(8,128)S(1)}, u32[]{:S(2)}, u32[]{:S(2)}) %collective-permute-start.38) | collective-permute-done | bytes 65568 | tf_op jit(solution)/shard_map/ppermute | solution.py:634
  191.4 3.0 %collective-permute-start.34 = (f32[64,384]{1,0:T(8,128)S(1)}, f32[64,384]{1,0:T(8,128)S(1)}, u32[]{:S(2)}, u32[]{:S(2)}) collective-permute-start(f32[64,384]{1,0:T(8,128)S(1)} %add.118), channel_id=1, source_target_pairs={{0,4},{1,5},{2,6},{3,7},{4,0},{5,1},{6,2},{7,3},{8,12},{9,13},{10,... | collective-permute-start | bytes 294920 | tf_op jit(solution)/shard_map/ppermute | solution.py:634
  199.3 3.4 %collective-permute-done.35 = f32[64,384]{1,0:T(8,128)S(1)} collective-permute-done((f32[64,384]{1,0:T(8,128)S(1)}, f32[64,384]{1,0:T(8,128)S(1)}, u32[]{:S(2)}, u32[]{:S(2)}) %collective-permute-start.35) | collective-permute-done | bytes 98336 | tf_op jit(solution)/shard_map/ppermute | solution.py:634
  204.2 16.0 %finish.1 = bf16[4096,256]{1,0:T(8,128)(2,1)} custom-call(s32[4]{0:T(128)S(1)} %iota_xor_fusion.order_ref, f32[256,384]{1,0:T(8,128)S(1)} %pad_maximum_fusion.left_ref, f32[256,256]{1,0:T(8,128)S(1)} %pad_maximum_fusion.1.right_ref, bf16[4096,256]{1,0:T(8,128)(2,1)S(1)} %get-tuple-element.102.moved_hbm, bf16[4096,256]{1,0:T(8,128)(2,1)S(1)} %copy-done.4), custom_call_target="tpu_custom_call" | custom-call | tf_op jit(solution)/shard_map/finish/pallas_call | solution.py:506
  (120 shorter events, 57.1 us)
Async XLA Ops:
  3.0 17.2 %collective-permute-start = (bf16[1024,256]{1,0:T(8,128)(2,1)}, bf16[1024,256]{1,0:T(8,128)(2,1)S(1)}, u32[]{:S(2)}, u32[]{:S(2)}) collective-permute-start(bf16[1024,256]{1,0:T(8,128)(2,1)} %get-tuple-element.119), channel_id=1, source_target_pairs={{1,0},{3,1},{5,3},{7,5},{6,7},{4,6},{2,4},{0,2},{9,8},{11,9},{13,1... | collective-permute-start | bytes 1572872 | tf_op jit(solution)/shard_map/ppermute | solution.py:576
  6.1 24.1 %collective-permute-start.11 = (bf16[1024,256]{1,0:T(8,128)(2,1)}, bf16[1024,256]{1,0:T(8,128)(2,1)S(1)}, u32[]{:S(2)}, u32[]{:S(2)}) collective-permute-start(bf16[1024,256]{1,0:T(8,128)(2,1)} %get-tuple-element.117), channel_id=1, source_target_pairs={{1,0},{3,1},{5,3},{7,5},{6,7},{4,6},{2,4},{0,2},{9,8},{11,9},{13,1... | collective-permute-start | bytes 1572872 | tf_op jit(solution)/shard_map/ppermute | solution.py:576
  7.6 24.7 %collective-permute-start.18 = (bf16[1024,256]{1,0:T(8,128)(2,1)}, bf16[1024,256]{1,0:T(8,128)(2,1)}, u32[]{:S(2)}, u32[]{:S(2)}) collective-permute-start(bf16[1024,256]{1,0:T(8,128)(2,1)} %get-tuple-element.116), channel_id=1, source_target_pairs={{0,1},{1,3},{3,5},{5,7},{7,6},{6,4},{4,2},{2,0},{8,9},{9,11},{11,1... | collective-permute-start | bytes 1572872 | tf_op jit(solution)/shard_map/ppermute | solution.py:576
  8.1 24.2 %collective-permute-start.4 = (bf16[1024,256]{1,0:T(8,128)(2,1)}, bf16[1024,256]{1,0:T(8,128)(2,1)}, u32[]{:S(2)}, u32[]{:S(2)}) collective-permute-start(bf16[1024,256]{1,0:T(8,128)(2,1)} %get-tuple-element.118), channel_id=1, source_target_pairs={{0,1},{1,3},{3,5},{5,7},{7,6},{6,4},{4,2},{2,0},{8,9},{9,11},{11,1... | collective-permute-start | bytes 1572872 | tf_op jit(solution)/shard_map/ppermute | solution.py:576
  20.9 13.4 %collective-permute-start.2 = (f32[128,256]{1,0:T(8,128)}, f32[128,256]{1,0:T(8,128)}, u32[]{:S(2)}, u32[]{:S(2)}) collective-permute-start(f32[128,256]{1,0:T(8,128)} %slice_select_fusion.2), channel_id=1, source_target_pairs={{0,8},{8,0},{16,24},{24,16},{1,9},{9,1},{17,25},{25,17},{2,10},{10... | collective-permute-start | bytes 393224 | tf_op jit(solution)/shard_map/ppermute | solution.py:634
  21.1 20.3 %collective-permute-start.1 = (bf16[1024,256]{1,0:T(8,128)(2,1)S(1)}, bf16[1024,256]{1,0:T(8,128)(2,1)S(1)}, u32[]{:S(2)}, u32[]{:S(2)}) collective-permute-start(bf16[1024,256]{1,0:T(8,128)(2,1)S(1)} %collective-permute-done.refs_4_), channel_id=1, source_target_pairs={{1,0},{3,1},{5,3},{7,5},{6,7},{4,6},{2,4},{0,2},{9,8},{11,9},{13,1... | collective-permute-start | bytes 1572872 | tf_op jit(solution)/shard_map/ppermute | solution.py:576
  30.2 22.5 %collective-permute-start.12 = (bf16[1024,256]{1,0:T(8,128)(2,1)S(1)}, bf16[1024,256]{1,0:T(8,128)(2,1)S(1)}, u32[]{:S(2)}, u32[]{:S(2)}) collective-permute-start(bf16[1024,256]{1,0:T(8,128)(2,1)S(1)} %collective-permute-done.11.refs_3_), channel_id=1, source_target_pairs={{1,0},{3,1},{5,3},{7,5},{6,7},{4,6},{2,4},{0,2},{9,8},{11,9},{13,1... | collective-permute-start | bytes 1572872 | tf_op jit(solution)/shard_map/ppermute | solution.py:576
  32.3 15.1 %collective-permute-start.19 = (bf16[1024,256]{1,0:T(8,128)(2,1)}, bf16[1024,256]{1,0:T(8,128)(2,1)S(1)}, u32[]{:S(2)}, u32[]{:S(2)}) collective-permute-start(bf16[1024,256]{1,0:T(8,128)(2,1)} %collective-permute-done.18.refs_1_), channel_id=1, source_target_pairs={{0,1},{1,3},{3,5},{5,7},{7,6},{6,4},{4,2},{2,0},{8,9},{9,11},{11,1... | collective-permute-start | bytes 1572872 | tf_op jit(solution)/shard_map/ppermute | solution.py:576
  32.3 26.3 %collective-permute-start.5 = (bf16[1024,256]{1,0:T(8,128)(2,1)}, bf16[1024,256]{1,0:T(8,128)(2,1)S(1)}, u32[]{:S(2)}, u32[]{:S(2)}) collective-permute-start(bf16[1024,256]{1,0:T(8,128)(2,1)} %collective-permute-done.4.refs_2_), channel_id=1, source_target_pairs={{0,1},{1,3},{3,5},{5,7},{7,6},{6,4},{4,2},{2,0},{8,9},{9,11},{11,1... | collective-permute-start | bytes 1572872 | tf_op jit(solution)/shard_map/ppermute | solution.py:576
  41.4 22.5 %collective-permute-start.25 = (bf16[1024,256]{1,0:T(8,128)(2,1)S(1)}, bf16[1024,256]{1,0:T(8,128)(2,1)S(1)}, u32[]{:S(2)}, u32[]{:S(2)}) collective-permute-start(bf16[1024,256]{1,0:T(8,128)(2,1)S(1)} %collective-permute-done.1.refs_8_), channel_id=1, source_target_pairs={{1,0},{3,1},{5,3},{7,5},{6,7},{4,6},{2,4},{0,2},{9,8},{11,9},{13,1... | collective-permute-start | bytes 1572872 | tf_op jit(solution)/shard_map/ppermute | solution.py:576
  47.4 22.5 %collective-permute-start.20 = (bf16[1024,256]{1,0:T(8,128)(2,1)S(1)}, bf16[1024,256]{1,0:T(8,128)(2,1)S(1)}, u32[]{:S(2)}, u32[]{:S(2)}) collective-permute-start(bf16[1024,256]{1,0:T(8,128)(2,1)S(1)} %collective-permute-done.19.refs_5_), channel_id=1, source_target_pairs={{0,1},{1,3},{3,5},{5,7},{7,6},{6,4},{4,2},{2,0},{8,9},{9,11},{11,1... | collective-permute-start | bytes 1572872 | tf_op jit(solution)/shard_map/ppermute | solution.py:576
  52.7 22.5 %collective-permute-start.13 = (bf16[1024,256]{1,0:T(8,128)(2,1)S(1)}, bf16[1024,256]{1,0:T(8,128)(2,1)S(1)}, u32[]{:S(2)}, u32[]{:S(2)}) collective-permute-start(bf16[1024,256]{1,0:T(8,128)(2,1)S(1)} %collective-permute-done.12.refs_7_), channel_id=1, source_target_pairs={{1,0},{3,1},{5,3},{7,5},{6,7},{4,6},{2,4},{0,2},{9,8},{11,9},{13,1... | collective-permute-start | bytes 1572872 | tf_op jit(solution)/shard_map/ppermute | solution.py:576
  58.6 22.5 %collective-permute-start.6 = (bf16[1024,256]{1,0:T(8,128)(2,1)S(1)}, bf16[1024,256]{1,0:T(8,128)(2,1)S(1)}, u32[]{:S(2)}, u32[]{:S(2)}) collective-permute-start(bf16[1024,256]{1,0:T(8,128)(2,1)S(1)} %collective-permute-done.5.refs_6_), channel_id=1, source_target_pairs={{0,1},{1,3},{3,5},{5,7},{7,6},{6,4},{4,2},{2,0},{8,9},{9,11},{11,1... | collective-permute-start | bytes 1572872 | tf_op jit(solution)/shard_map/ppermute | solution.py:576
  63.9 22.5 %collective-permute-start.26 = (bf16[1024,256]{1,0:T(8,128)(2,1)S(1)}, bf16[1024,256]{1,0:T(8,128)(2,1)S(1)}, u32[]{:S(2)}, u32[]{:S(2)}) collective-permute-start(bf16[1024,256]{1,0:T(8,128)(2,1)S(1)} %collective-permute-done.25.refs_12_), channel_id=1, source_target_pairs={{1,0},{3,1},{5,3},{7,5},{6,7},{4,6},{2,4},{0,2},{9,8},{11,9},{13,1... | collective-permute-start | bytes 1572872 | tf_op jit(solution)/shard_map/ppermute | solution.py:576
  69.9 22.5 %collective-permute-start.21 = (bf16[1024,256]{1,0:T(8,128)(2,1)S(1)}, bf16[1024,256]{1,0:T(8,128)(2,1)S(1)}, u32[]{:S(2)}, u32[]{:S(2)}) collective-permute-start(bf16[1024,256]{1,0:T(8,128)(2,1)S(1)} %collective-permute-done.20.refs_9_), channel_id=1, source_target_pairs={{0,1},{1,3},{3,5},{5,7},{7,6},{6,4},{4,2},{2,0},{8,9},{9,11},{11,1... | collective-permute-start | bytes 1572872 | tf_op jit(solution)/shard_map/ppermute | solution.py:576
  75.1 22.5 %collective-permute-start.14 = (bf16[1024,256]{1,0:T(8,128)(2,1)S(1)}, bf16[1024,256]{1,0:T(8,128)(2,1)S(1)}, u32[]{:S(2)}, u32[]{:S(2)}) collective-permute-start(bf16[1024,256]{1,0:T(8,128)(2,1)S(1)} %collective-permute-done.13.refs_11_), channel_id=1, source_target_pairs={{1,0},{3,1},{5,3},{7,5},{6,7},{4,6},{2,4},{0,2},{9,8},{11,9},{13,1... | collective-permute-start | bytes 1572872 | tf_op jit(solution)/shard_map/ppermute | solution.py:576
  81.1 22.5 %collective-permute-start.7 = (bf16[1024,256]{1,0:T(8,128)(2,1)S(1)}, bf16[1024,256]{1,0:T(8,128)(2,1)S(1)}, u32[]{:S(2)}, u32[]{:S(2)}) collective-permute-start(bf16[1024,256]{1,0:T(8,128)(2,1)S(1)} %collective-permute-done.6.refs_10_), channel_id=1, source_target_pairs={{0,1},{1,3},{3,5},{5,7},{7,6},{6,4},{4,2},{2,0},{8,9},{9,11},{11,1... | collective-permute-start | bytes 1572872 | tf_op jit(solution)/shard_map/ppermute | solution.py:576
  86.4 29.1 %collective-permute-start.27 = (bf16[1024,256]{1,0:T(8,128)(2,1)S(1)}, bf16[1024,256]{1,0:T(8,128)(2,1)S(1)}, u32[]{:S(2)}, u32[]{:S(2)}) collective-permute-start(bf16[1024,256]{1,0:T(8,128)(2,1)S(1)} %collective-permute-done.26.refs_3_), channel_id=1, source_target_pairs={{1,0},{3,1},{5,3},{7,5},{6,7},{4,6},{2,4},{0,2},{9,8},{11,9},{13,1... | collective-permute-start | bytes 1572872 | tf_op jit(solution)/shard_map/ppermute | solution.py:576
  92.3 24.1 %collective-permute-start.22 = (bf16[1024,256]{1,0:T(8,128)(2,1)S(1)}, bf16[1024,256]{1,0:T(8,128)(2,1)S(1)}, u32[]{:S(2)}, u32[]{:S(2)}) collective-permute-start(bf16[1024,256]{1,0:T(8,128)(2,1)S(1)} %collective-permute-done.21.refs_0_), channel_id=1, source_target_pairs={{0,1},{1,3},{3,5},{5,7},{7,6},{6,4},{4,2},{2,0},{8,9},{9,11},{11,1... | collective-permute-start | bytes 1572872 | tf_op jit(solution)/shard_map/ppermute | solution.py:576
  97.6 28.4 %collective-permute-start.15 = (bf16[1024,256]{1,0:T(8,128)(2,1)S(1)}, bf16[1024,256]{1,0:T(8,128)(2,1)S(1)}, u32[]{:S(2)}, u32[]{:S(2)}) collective-permute-start(bf16[1024,256]{1,0:T(8,128)(2,1)S(1)} %collective-permute-done.14.refs_2_), channel_id=1, source_target_pairs={{1,0},{3,1},{5,3},{7,5},{6,7},{4,6},{2,4},{0,2},{9,8},{11,9},{13,1... | collective-permute-start | bytes 1572872 | tf_op jit(solution)/shard_map/ppermute | solution.py:576
  103.6 22.5 %collective-permute-start.8 = (bf16[1024,256]{1,0:T(8,128)(2,1)S(1)}, bf16[1024,256]{1,0:T(8,128)(2,1)S(1)}, u32[]{:S(2)}, u32[]{:S(2)}) collective-permute-start(bf16[1024,256]{1,0:T(8,128)(2,1)S(1)} %collective-permute-done.7.refs_1_), channel_id=1, source_target_pairs={{0,1},{1,3},{3,5},{5,7},{7,6},{6,4},{4,2},{2,0},{8,9},{9,11},{11,1... | collective-permute-start | bytes 1572872 | tf_op jit(solution)/shard_map/ppermute | solution.py:576
  115.4 17.3 %collective-permute-start.28 = (bf16[1024,256]{1,0:T(8,128)(2,1)S(1)}, bf16[1024,256]{1,0:T(8,128)(2,1)S(1)}, u32[]{:S(2)}, u32[]{:S(2)}) collective-permute-start(bf16[1024,256]{1,0:T(8,128)(2,1)S(1)} %collective-permute-done.27.refs_7_), channel_id=1, source_target_pairs={{1,0},{3,1},{5,3},{7,5},{6,7},{4,6},{2,4},{0,2},{9,8},{11,9},{13,1... | collective-permute-start | bytes 1572872 | tf_op jit(solution)/shard_map/ppermute | solution.py:576
  116.4 20.8 %collective-permute-start.23 = (bf16[1024,256]{1,0:T(8,128)(2,1)S(1)}, bf16[1024,256]{1,0:T(8,128)(2,1)S(1)}, u32[]{:S(2)}, u32[]{:S(2)}) collective-permute-start(bf16[1024,256]{1,0:T(8,128)(2,1)S(1)} %collective-permute-done.22.refs_4_), channel_id=1, source_target_pairs={{0,1},{1,3},{3,5},{5,7},{7,6},{6,4},{4,2},{2,0},{8,9},{9,11},{11,1... | collective-permute-start | bytes 1572872 | tf_op jit(solution)/shard_map/ppermute | solution.py:576
  126.0 22.5 %collective-permute-start.9 = (bf16[1024,256]{1,0:T(8,128)(2,1)S(1)}, bf16[1024,256]{1,0:T(8,128)(2,1)S(1)}, u32[]{:S(2)}, u32[]{:S(2)}) collective-permute-start(bf16[1024,256]{1,0:T(8,128)(2,1)S(1)} %collective-permute-done.8.refs_5_), channel_id=1, source_target_pairs={{0,1},{1,3},{3,5},{5,7},{7,6},{6,4},{4,2},{2,0},{8,9},{9,11},{11,1... | collective-permute-start | bytes 1572872 | tf_op jit(solution)/shard_map/ppermute | solution.py:576
  126.0 22.5 %collective-permute-start.16 = (bf16[1024,256]{1,0:T(8,128)(2,1)S(1)}, bf16[1024,256]{1,0:T(8,128)(2,1)S(1)}, u32[]{:S(2)}, u32[]{:S(2)}) collective-permute-start(bf16[1024,256]{1,0:T(8,128)(2,1)S(1)} %collective-permute-done.15.refs_6_), channel_id=1, source_target_pairs={{1,0},{3,1},{5,3},{7,5},{6,7},{4,6},{2,4},{0,2},{9,8},{11,9},{13,1... | collective-permute-start | bytes 1572872 | tf_op jit(solution)/shard_map/ppermute | solution.py:576
  132.7 25.3 %collective-permute-start.29 = (bf16[1024,256]{1,0:T(8,128)(2,1)S(1)}, bf16[1024,256]{1,0:T(8,128)(2,1)S(1)}, u32[]{:S(2)}, u32[]{:S(2)}) collective-permute-start(bf16[1024,256]{1,0:T(8,128)(2,1)S(1)} %collective-permute-done.28.refs_11_), channel_id=1, source_target_pairs={{1,0},{3,1},{5,3},{7,5},{6,7},{4,6},{2,4},{0,2},{9,8},{11,9},{13,1... | collective-permute-start | bytes 1572872 | tf_op jit(solution)/shard_map/ppermute | solution.py:576
  137.3 22.5 %collective-permute-start.24 = (bf16[1024,256]{1,0:T(8,128)(2,1)S(1)}, bf16[1024,256]{1,0:T(8,128)(2,1)S(1)}, u32[]{:S(2)}, u32[]{:S(2)}) collective-permute-start(bf16[1024,256]{1,0:T(8,128)(2,1)S(1)} %collective-permute-done.23.refs_8_), channel_id=1, source_target_pairs={{0,1},{1,3},{3,5},{5,7},{7,6},{6,4},{4,2},{2,0},{8,9},{9,11},{11,1... | collective-permute-start | bytes 1572872 | tf_op jit(solution)/shard_map/ppermute | solution.py:576
  148.5 19.1 %collective-permute-start.10 = (bf16[1024,256]{1,0:T(8,128)(2,1)S(1)}, bf16[1024,256]{1,0:T(8,128)(2,1)S(1)}, u32[]{:S(2)}, u32[]{:S(2)}) collective-permute-start(bf16[1024,256]{1,0:T(8,128)(2,1)S(1)} %collective-permute-done.9.refs_9_), channel_id=1, source_target_pairs={{0,1},{1,3},{3,5},{5,7},{7,6},{6,4},{4,2},{2,0},{8,9},{9,11},{11,1... | collective-permute-start | bytes 1572872 | tf_op jit(solution)/shard_map/ppermute | solution.py:576
  148.5 19.1 %collective-permute-start.17 = (bf16[1024,256]{1,0:T(8,128)(2,1)S(1)}, bf16[1024,256]{1,0:T(8,128)(2,1)S(1)}, u32[]{:S(2)}, u32[]{:S(2)}) collective-permute-start(bf16[1024,256]{1,0:T(8,128)(2,1)S(1)} %collective-permute-done.16.refs_10_), channel_id=1, source_target_pairs={{1,0},{3,1},{5,3},{7,5},{6,7},{4,6},{2,4},{0,2},{9,8},{11,9},{13,1... | collective-permute-start | bytes 1572872 | tf_op jit(solution)/shard_map/ppermute | solution.py:576
  179.6 5.7 %collective-permute-start.37 = (f32[64,256]{1,0:T(8,128)S(1)}, f32[64,256]{1,0:T(8,128)S(1)}, u32[]{:S(2)}, u32[]{:S(2)}) collective-permute-start(f32[64,256]{1,0:T(8,128)S(1)} %maximum_select_fusion), channel_id=1, source_target_pairs={{0,2},{1,3},{2,0},{3,1},{4,6},{5,7},{6,4},{7,5},{8,10},{9,11},{10,... | collective-permute-start | bytes 196616 | tf_op jit(solution)/shard_map/ppermute | solution.py:634
  183.1 8.3 %collective-permute-start.33 = (f32[64,384]{1,0:T(8,128)S(1)}, f32[64,384]{1,0:T(8,128)S(1)}, u32[]{:S(2)}, u32[]{:S(2)}) collective-permute-start(f32[64,384]{1,0:T(8,128)S(1)} %fusion.22), channel_id=1, source_target_pairs={{0,2},{1,3},{2,0},{3,1},{4,6},{5,7},{6,4},{7,5},{8,10},{9,11},{10,... | collective-permute-start | bytes 294920 | tf_op jit(solution)/shard_map/ppermute | solution.py:634
  191.4 6.6 %collective-permute-start.34 = (f32[64,384]{1,0:T(8,128)S(1)}, f32[64,384]{1,0:T(8,128)S(1)}, u32[]{:S(2)}, u32[]{:S(2)}) collective-permute-start(f32[64,384]{1,0:T(8,128)S(1)} %add.118), channel_id=1, source_target_pairs={{0,4},{1,5},{2,6},{3,7},{4,0},{5,1},{6,2},{7,3},{8,12},{9,13},{10,... | collective-permute-start | bytes 294920 | tf_op jit(solution)/shard_map/ppermute | solution.py:634
  (22 other events, 198.1 us)

commit v3 on v2

--- a/solution.py
+++ b/solution.py
@@ -408,10 +408,10 @@
         share = panel[:, high - here :]
         if high < rank:
             inner[high:, first:] -= product(share, panel[:, first - here :], (0,))
-        side = product(inverse, image[low:high, :], (1,))
-        image[low:high, :] = side
-        if high < rank:
-            image[high:, :] -= product(share, side, (0,))
+        side = image[low:high, :]
+        if low > 0:
+            side = side - product(inner[:low, low:high], image[:low, :], (0,))
+        image[low:high, :] = product(inverse, side, (1,))
 
 
 def finish_kernel(

time: 220 us -> 222 us (level)
  waiting for transfers between devices: 111 us -> 116 us
  starting transfers between devices: 47.8 us -> 45.5 us
    ppermute x14, waiting for transfers between devices: 22.6 us -> 25.7 us  [swap(): return lax.ppermute(value, axis, [(i, i ^ stride) for i in range(count)])]
    ppermute x14, starting transfers between devices: 14.6 us -> 12.1 us  [swap(): return lax.ppermute(value, axis, [(i, i ^ stride) for i in range(count)])]
  transfers between devices with their start and end apart: 42 -> 42, of which waited for: 29 -> 29; matrix products, arithmetic and copies ran while one was open for 2% -> 2% of each run, Pallas kernels for 13% -> 12%
where the time goes in v3:
time: 222 us
  waiting for transfers between devices  116 us (52%)
  Pallas kernels  46.3 us (21%)
  starting transfers between devices  45.5 us (20%)
  local copies, waits for them, and re-layouts  7.55 us (3%)
  other arithmetic  5.1 us (2%)
    ppermute x28, waiting for transfers between devices, ring_gather(): lax.ppermute(piece, 'col', forward if i < PIECES // 2 else back)  90.3 us
    ppermute x28, starting transfers between devices, ring_gather(): lax.ppermute(piece, 'col', forward if i < PIECES // 2 else back)  33.4 us
    ppermute x14, waiting for transfers between devices, swap(): return lax.ppermute(value, axis, [(i, i ^ stride) for i in range(count)])  25.7 us
    pallas_call x1, Pallas kernels, finish_part(): pl.pallas_call(finish_kernel, in_specs=[pl.BlockSpec(memory_space=pltpu.S...  16.4 us
    ppermute x14, starting transfers between devices, swap(): return lax.ppermute(value, axis, [(i, i ^ stride) for i in range(count)])  12.1 us
    pallas_call x1, Pallas kernels, early_part(): pl.pallas_call(early_kernel, grid_spec=pltpu.PrefetchScalarGridSpec(num_s...  9.28 us
    pallas_call x1, Pallas kernels, middle_part(): pl.pallas_call(middle_kernel, grid_spec=pltpu.PrefetchScalarGridSpec(num_...  7.2 us
    pallas_call x1, Pallas kernels, bath_part(): pl.pallas_call(bath_kernel, grid_spec=pltpu.PrefetchScalarGridSpec(num_sc...  5.46 us
  transfers between devices with their start and end apart: 42, of which 29 were waited for; matrix products, arithmetic and copies ran while one was open for 2% of the time, Pallas kernels for 12%

profile of v3, /device:TPU:0, one launch (start us, length us, event | category | flops | bytes accessed | tf_op | source)
XLA Modules:
  0.0 221.7 jit_solution(8140859241113134036)
XLA Ops:
  0.0 3.0 %fusion.21 = (bf16[1024,256]{1,0:T(8,128)(2,1)}, bf16[1024,256]{1,0:T(8,128)(2,1)}, bf16[1024,256]{1,0:T(8,128)(2,1)}, bf16[1024,256]{1,0:T(8,128)(2,1)}) fusion(bf16[4096,256]{1,0:T(8,128)(2,1)} %refs_14_.1), kind=kLoop, calls=%fused_computation.81 | loop fusion | bytes 4194304 | tf_op jit(solution)/shard_map/slice | solution.py:563
  3.0 3.0 %collective-permute-start = (bf16[1024,256]{1,0:T(8,128)(2,1)}, bf16[1024,256]{1,0:T(8,128)(2,1)S(1)}, u32[]{:S(2)}, u32[]{:S(2)}) collective-permute-start(bf16[1024,256]{1,0:T(8,128)(2,1)} %get-tuple-element.119), channel_id=1, source_target_pairs={{1,0},{3,1},{5,3},{7,5},{6,7},{4,6},{2,4},{0,2},{9,8},{11,9},{13,1... | collective-permute-start | bytes 1572872 | tf_op jit(solution)/shard_map/ppermute | solution.py:576
  13.0 5.5 %bath.1 = (bf16[4096,256]{1,0:T(8,128)(2,1)S(1)}, f32[256,256]{1,0:T(8,128)S(1)}) custom-call(s32[8]{0:T(128)S(1)} %copy-done.6, bf16[4,512,512]{2,1,0:T(8,128)(2,1)S(1)} %copy-done.5, bf16[4096,256]{1,0:T(8,128)(2,1)S(1)} %copy-done), custom_call_target="tpu_custom_call" | custom-call | tf_op jit(solution)/shard_map/bath/pallas_call | solution.py:35
  23.1 7.1 %collective-permute-done.11.refs_3_ = bf16[1024,256]{1,0:T(8,128)(2,1)S(1)} collective-permute-done((bf16[1024,256]{1,0:T(8,128)(2,1)}, bf16[1024,256]{1,0:T(8,128)(2,1)S(1)}, u32[]{:S(2)}, u32[]{:S(2)}) %collective-permute-start.11) | collective-permute-done | bytes 524320 | tf_op jit(solution)/shard_map/ppermute | solution.py:576
  36.8 2.8 %collective-permute-done.3 = f32[64,256]{1,0:T(8,128)S(1)} collective-permute-done((f32[64,256]{1,0:T(8,128)S(1)}, f32[64,256]{1,0:T(8,128)S(1)}, u32[]{:S(2)}, u32[]{:S(2)}) %collective-permute-start.3) | collective-permute-done | bytes 65568 | tf_op jit(solution)/shard_map/ppermute | solution.py:634
  43.6 3.8 %collective-permute-done.19.refs_5_ = bf16[1024,256]{1,0:T(8,128)(2,1)S(1)} collective-permute-done((bf16[1024,256]{1,0:T(8,128)(2,1)}, bf16[1024,256]{1,0:T(8,128)(2,1)S(1)}, u32[]{:S(2)}, u32[]{:S(2)}) %collective-permute-start.19) | collective-permute-done | bytes 524320 | tf_op jit(solution)/shard_map/ppermute | solution.py:576
  47.4 5.3 %collective-permute-done.12.refs_7_ = bf16[1024,256]{1,0:T(8,128)(2,1)S(1)} collective-permute-done((bf16[1024,256]{1,0:T(8,128)(2,1)S(1)}, bf16[1024,256]{1,0:T(8,128)(2,1)S(1)}, u32[]{:S(2)}, u32[]{:S(2)}) %collective-permute-start.12) | collective-permute-done | bytes 524320 | tf_op jit(solution)/shard_map/ppermute | solution.py:576
  54.8 3.8 %collective-permute-done.5.refs_6_ = bf16[1024,256]{1,0:T(8,128)(2,1)S(1)} collective-permute-done((bf16[1024,256]{1,0:T(8,128)(2,1)}, bf16[1024,256]{1,0:T(8,128)(2,1)S(1)}, u32[]{:S(2)}, u32[]{:S(2)}) %collective-permute-start.5) | collective-permute-done | bytes 524320 | tf_op jit(solution)/shard_map/ppermute | solution.py:576
  58.6 5.3 %collective-permute-done.25.refs_12_ = bf16[1024,256]{1,0:T(8,128)(2,1)S(1)} collective-permute-done((bf16[1024,256]{1,0:T(8,128)(2,1)S(1)}, bf16[1024,256]{1,0:T(8,128)(2,1)S(1)}, u32[]{:S(2)}, u32[]{:S(2)}) %collective-permute-start.25) | collective-permute-done | bytes 524320 | tf_op jit(solution)/shard_map/ppermute | solution.py:576
  66.0 3.8 %collective-permute-done.20.refs_9_ = bf16[1024,256]{1,0:T(8,128)(2,1)S(1)} collective-permute-done((bf16[1024,256]{1,0:T(8,128)(2,1)S(1)}, bf16[1024,256]{1,0:T(8,128)(2,1)S(1)}, u32[]{:S(2)}, u32[]{:S(2)}) %collective-permute-start.20) | collective-permute-done | bytes 524320 | tf_op jit(solution)/shard_map/ppermute | solution.py:576
  69.9 5.3 %collective-permute-done.13.refs_11_ = bf16[1024,256]{1,0:T(8,128)(2,1)S(1)} collective-permute-done((bf16[1024,256]{1,0:T(8,128)(2,1)S(1)}, bf16[1024,256]{1,0:T(8,128)(2,1)S(1)}, u32[]{:S(2)}, u32[]{:S(2)}) %collective-permute-start.13) | collective-permute-done | bytes 524320 | tf_op jit(solution)/shard_map/ppermute | solution.py:576
  77.3 3.8 %collective-permute-done.6.refs_10_ = bf16[1024,256]{1,0:T(8,128)(2,1)S(1)} collective-permute-done((bf16[1024,256]{1,0:T(8,128)(2,1)S(1)}, bf16[1024,256]{1,0:T(8,128)(2,1)S(1)}, u32[]{:S(2)}, u32[]{:S(2)}) %collective-permute-start.6) | collective-permute-done | bytes 524320 | tf_op jit(solution)/shard_map/ppermute | solution.py:576
  81.1 5.3 %collective-permute-done.26.refs_3_ = bf16[1024,256]{1,0:T(8,128)(2,1)S(1)} collective-permute-done((bf16[1024,256]{1,0:T(8,128)(2,1)S(1)}, bf16[1024,256]{1,0:T(8,128)(2,1)S(1)}, u32[]{:S(2)}, u32[]{:S(2)}) %collective-permute-start.26) | collective-permute-done | bytes 524320 | tf_op jit(solution)/shard_map/ppermute | solution.py:576
  88.5 3.8 %collective-permute-done.21.refs_0_ = bf16[1024,256]{1,0:T(8,128)(2,1)S(1)} collective-permute-done((bf16[1024,256]{1,0:T(8,128)(2,1)S(1)}, bf16[1024,256]{1,0:T(8,128)(2,1)S(1)}, u32[]{:S(2)}, u32[]{:S(2)}) %collective-permute-start.21) | collective-permute-done | bytes 524320 | tf_op jit(solution)/shard_map/ppermute | solution.py:576
  92.3 5.3 %collective-permute-done.14.refs_2_ = bf16[1024,256]{1,0:T(8,128)(2,1)S(1)} collective-permute-done((bf16[1024,256]{1,0:T(8,128)(2,1)S(1)}, bf16[1024,256]{1,0:T(8,128)(2,1)S(1)}, u32[]{:S(2)}, u32[]{:S(2)}) %collective-permute-start.14) | collective-permute-done | bytes 524320 | tf_op jit(solution)/shard_map/ppermute | solution.py:576
  99.7 3.8 %collective-permute-done.7.refs_1_ = bf16[1024,256]{1,0:T(8,128)(2,1)S(1)} collective-permute-done((bf16[1024,256]{1,0:T(8,128)(2,1)S(1)}, bf16[1024,256]{1,0:T(8,128)(2,1)S(1)}, u32[]{:S(2)}, u32[]{:S(2)}) %collective-permute-start.7) | collective-permute-done | bytes 524320 | tf_op jit(solution)/shard_map/ppermute | solution.py:576
  105.2 9.3 %couple_early.1.refs_13_ = f32[4096,256]{1,0:T(8,128)S(1)} custom-call(s32[8,8]{1,0:T(8,128)S(1)} %get-tuple-element.90.origin_ref, s32[8,8]{1,0:T(8,128)S(1)} %get-tuple-element.91.offset_ref, s32[8]{0:T(128)S(1)} %broadcast_in_dim.76.first_ref, s32[8]{0:T(128)S(1)} %get-tuple-element.92.count_ref.first_ref, s32[8,8]{1,0:T(8,128)S(1)} %get-tuple-element.94.kind_ref, ...), custom_call_target="tpu_custom_call" | custom-call | flops 4294967296 | bytes 16777216 | tf_op jit(solution)/shard_map/couple_early/pallas_call | solution.py:211
  117.7 8.3 %collective-permute-done.8.refs_5_ = bf16[1024,256]{1,0:T(8,128)(2,1)S(1)} collective-permute-done((bf16[1024,256]{1,0:T(8,128)(2,1)S(1)}, bf16[1024,256]{1,0:T(8,128)(2,1)S(1)}, u32[]{:S(2)}, u32[]{:S(2)}) %collective-permute-start.8) | collective-permute-done | bytes 524320 | tf_op jit(solution)/shard_map/ppermute | solution.py:576
  128.1 3.2 %collective-permute-done.28.refs_11_ = bf16[1024,256]{1,0:T(8,128)(2,1)S(1)} collective-permute-done((bf16[1024,256]{1,0:T(8,128)(2,1)S(1)}, bf16[1024,256]{1,0:T(8,128)(2,1)S(1)}, u32[]{:S(2)}, u32[]{:S(2)}) %collective-permute-start.28) | collective-permute-done | bytes 524320 | tf_op jit(solution)/shard_map/ppermute | solution.py:576
  133.4 3.8 %collective-permute-done.23.refs_8_ = bf16[1024,256]{1,0:T(8,128)(2,1)S(1)} collective-permute-done((bf16[1024,256]{1,0:T(8,128)(2,1)S(1)}, bf16[1024,256]{1,0:T(8,128)(2,1)S(1)}, u32[]{:S(2)}, u32[]{:S(2)}) %collective-permute-start.23) | collective-permute-done | bytes 524320 | tf_op jit(solution)/shard_map/ppermute | solution.py:576
  137.3 11.2 %collective-permute-done.9.refs_9_ = bf16[1024,256]{1,0:T(8,128)(2,1)S(1)} collective-permute-done((bf16[1024,256]{1,0:T(8,128)(2,1)S(1)}, bf16[1024,256]{1,0:T(8,128)(2,1)S(1)}, u32[]{:S(2)}, u32[]{:S(2)}) %collective-permute-start.9) | collective-permute-done | bytes 524320 | tf_op jit(solution)/shard_map/ppermute | solution.py:576
  150.5 7.2 %couple_middle.1.refs_3_ = f32[4096,256]{1,0:T(8,128)S(1)} custom-call(s32[8,8]{1,0:T(8,128)S(1)} %get-tuple-element.90.origin_ref, s32[8,8]{1,0:T(8,128)S(1)} %get-tuple-element.91.offset_ref, s32[8]{0:T(128)S(1)} %get-tuple-element.92.count_ref.first_ref, s32[8]{0:T(128)S(1)} %get-tuple-element.93.count_ref, s32[8,8]{1,0:T(8,128)S(1)} %get-tuple-element.94.kind_ref, ...), custom_call_target="tpu_custom_call" | custom-call | flops 4294967296 | bytes 16777216 | tf_op jit(solution)/shard_map/couple_middle/pallas_call | solution.py:246
  159.7 4.4 %couple_settle.1 = (f32[4096,256]{1,0:T(8,128)S(1)}, bf16[4096,256]{1,0:T(8,128)(2,1)S(1)}, f32[256,512]{1,0:T(8,128)S(1)}) custom-call(s32[8,8]{1,0:T(8,128)S(1)} %get-tuple-element.90.origin_ref, s32[8,8]{1,0:T(8,128)S(1)} %get-tuple-element.91.offset_ref, s32[8]{0:T(128)S(1)} %get-tuple-element.70.first_ref, s32[8]{0:T(128)S(1)} %get-tuple-element.71.count_ref, ...), custom_call_target="tpu_custom_call" | custom-call | flops 4294967296 | bytes 16777216 | tf_op jit(solution)/shard_map/couple_settle/pallas_call | solution.py:278
  164.2 3.4 %collective-permute-done.10.refs_0_ = bf16[1024,256]{1,0:T(8,128)(2,1)S(1)} collective-permute-done((bf16[1024,256]{1,0:T(8,128)(2,1)S(1)}, bf16[1024,256]{1,0:T(8,128)(2,1)S(1)}, u32[]{:S(2)}, u32[]{:S(2)}) %collective-permute-start.10) | collective-permute-done | bytes 524320 | tf_op jit(solution)/shard_map/ppermute | solution.py:576
  167.6 3.5 %couple_late.1 = (bf16[4096,256]{1,0:T(8,128)(2,1)S(1)}, f32[256,512]{1,0:T(8,128)S(1)}) custom-call(s32[8,8]{1,0:T(8,128)S(1)} %get-tuple-element.90.origin_ref, s32[8,8]{1,0:T(8,128)S(1)} %get-tuple-element.91.offset_ref, s32[8]{0:T(128)S(1)} %get-tuple-element.63.first_ref, s32[8]{0:T(128)S(1)} %get-tuple-element.64.count_ref, ...), custom_call_target="tpu_custom_call", output_to_operand_aliasing={{0}: (12, {})} | custom-call | tf_op jit(solution)/shard_map/couple_late/pallas_call | solution.py:320
  173.6 4.8 %collective-permute-done.31 = f32[64,512]{1,0:T(8,128)S(1)} collective-permute-done((f32[64,512]{1,0:T(8,128)S(1)}, f32[64,512]{1,0:T(8,128)S(1)}, u32[]{:S(2)}, u32[]{:S(2)}) %collective-permute-start.31) | collective-permute-done | bytes 131104 | tf_op jit(solution)/shard_map/ppermute | solution.py:634
  178.6 3.3 %collective-permute-start.37 = (f32[64,256]{1,0:T(8,128)S(1)}, f32[64,256]{1,0:T(8,128)S(1)}, u32[]{:S(2)}, u32[]{:S(2)}) collective-permute-start(f32[64,256]{1,0:T(8,128)S(1)} %maximum_select_fusion), channel_id=1, source_target_pairs={{0,2},{1,3},{2,0},{3,1},{4,6},{5,7},{6,4},{7,5},{8,10},{9,11},{10,... | collective-permute-start | bytes 196616 | tf_op jit(solution)/shard_map/ppermute | solution.py:634
  186.5 5.1 %collective-permute-done.38 = f32[64,256]{1,0:T(8,128)S(1)} collective-permute-done((f32[64,256]{1,0:T(8,128)S(1)}, f32[64,256]{1,0:T(8,128)S(1)}, u32[]{:S(2)}, u32[]{:S(2)}) %collective-permute-start.38) | collective-permute-done | bytes 65568 | tf_op jit(solution)/shard_map/ppermute | solution.py:634
  193.0 2.9 %collective-permute-done.39 = f32[64,256]{1,0:T(8,128)S(1)} collective-permute-done((f32[64,256]{1,0:T(8,128)S(1)}, f32[64,256]{1,0:T(8,128)S(1)}, u32[]{:S(2)}, u32[]{:S(2)}) %collective-permute-start.39) | collective-permute-done | bytes 65568 | tf_op jit(solution)/shard_map/ppermute | solution.py:634
  196.3 2.5 %collective-permute-done.34 = f32[64,384]{1,0:T(8,128)S(1)} collective-permute-done((f32[64,384]{1,0:T(8,128)S(1)}, f32[64,384]{1,0:T(8,128)S(1)}, u32[]{:S(2)}, u32[]{:S(2)}) %collective-permute-start.34) | collective-permute-done | bytes 98336 | tf_op jit(solution)/shard_map/ppermute | solution.py:634
  200.3 3.2 %collective-permute-done.35 = f32[64,384]{1,0:T(8,128)S(1)} collective-permute-done((f32[64,384]{1,0:T(8,128)S(1)}, f32[64,384]{1,0:T(8,128)S(1)}, u32[]{:S(2)}, u32[]{:S(2)}) %collective-permute-start.35) | collective-permute-done | bytes 98336 | tf_op jit(solution)/shard_map/ppermute | solution.py:634
  205.1 16.4 %finish.1 = bf16[4096,256]{1,0:T(8,128)(2,1)} custom-call(s32[4]{0:T(128)S(1)} %iota_xor_fusion.order_ref, f32[256,384]{1,0:T(8,128)S(1)} %pad_maximum_fusion.left_ref, f32[256,256]{1,0:T(8,128)S(1)} %pad_maximum_fusion.1.right_ref, bf16[4096,256]{1,0:T(8,128)(2,1)S(1)} %get-tuple-element.102.moved_hbm, bf16[4096,256]{1,0:T(8,128)(2,1)S(1)} %copy-done.4), custom_call_target="tpu_custom_call" | custom-call | tf_op jit(solution)/shard_map/finish/pallas_call | solution.py:506
  (120 shorter events, 57.1 us)
Async XLA Ops:
  3.0 17.2 %collective-permute-start = (bf16[1024,256]{1,0:T(8,128)(2,1)}, bf16[1024,256]{1,0:T(8,128)(2,1)S(1)}, u32[]{:S(2)}, u32[]{:S(2)}) collective-permute-start(bf16[1024,256]{1,0:T(8,128)(2,1)} %get-tuple-element.119), channel_id=1, source_target_pairs={{1,0},{3,1},{5,3},{7,5},{6,7},{4,6},{2,4},{0,2},{9,8},{11,9},{13,1... | collective-permute-start | bytes 1572872 | tf_op jit(solution)/shard_map/ppermute | solution.py:576
  6.1 24.1 %collective-permute-start.11 = (bf16[1024,256]{1,0:T(8,128)(2,1)}, bf16[1024,256]{1,0:T(8,128)(2,1)S(1)}, u32[]{:S(2)}, u32[]{:S(2)}) collective-permute-start(bf16[1024,256]{1,0:T(8,128)(2,1)} %get-tuple-element.117), channel_id=1, source_target_pairs={{1,0},{3,1},{5,3},{7,5},{6,7},{4,6},{2,4},{0,2},{9,8},{11,9},{13,1... | collective-permute-start | bytes 1572872 | tf_op jit(solution)/shard_map/ppermute | solution.py:576
  7.6 24.7 %collective-permute-start.18 = (bf16[1024,256]{1,0:T(8,128)(2,1)}, bf16[1024,256]{1,0:T(8,128)(2,1)}, u32[]{:S(2)}, u32[]{:S(2)}) collective-permute-start(bf16[1024,256]{1,0:T(8,128)(2,1)} %get-tuple-element.116), channel_id=1, source_target_pairs={{0,1},{1,3},{3,5},{5,7},{7,6},{6,4},{4,2},{2,0},{8,9},{9,11},{11,1... | collective-permute-start | bytes 1572872 | tf_op jit(solution)/shard_map/ppermute | solution.py:576
  8.1 24.2 %collective-permute-start.4 = (bf16[1024,256]{1,0:T(8,128)(2,1)}, bf16[1024,256]{1,0:T(8,128)(2,1)}, u32[]{:S(2)}, u32[]{:S(2)}) collective-permute-start(bf16[1024,256]{1,0:T(8,128)(2,1)} %get-tuple-element.118), channel_id=1, source_target_pairs={{0,1},{1,3},{3,5},{5,7},{7,6},{6,4},{4,2},{2,0},{8,9},{9,11},{11,1... | collective-permute-start | bytes 1572872 | tf_op jit(solution)/shard_map/ppermute | solution.py:576
  20.9 13.4 %collective-permute-start.2 = (f32[128,256]{1,0:T(8,128)}, f32[128,256]{1,0:T(8,128)}, u32[]{:S(2)}, u32[]{:S(2)}) collective-permute-start(f32[128,256]{1,0:T(8,128)} %slice_select_fusion.2), channel_id=1, source_target_pairs={{0,8},{8,0},{16,24},{24,16},{1,9},{9,1},{17,25},{25,17},{2,10},{10... | collective-permute-start | bytes 393224 | tf_op jit(solution)/shard_map/ppermute | solution.py:634
  21.1 20.3 %collective-permute-start.1 = (bf16[1024,256]{1,0:T(8,128)(2,1)S(1)}, bf16[1024,256]{1,0:T(8,128)(2,1)S(1)}, u32[]{:S(2)}, u32[]{:S(2)}) collective-permute-start(bf16[1024,256]{1,0:T(8,128)(2,1)S(1)} %collective-permute-done.refs_4_), channel_id=1, source_target_pairs={{1,0},{3,1},{5,3},{7,5},{6,7},{4,6},{2,4},{0,2},{9,8},{11,9},{13,1... | collective-permute-start | bytes 1572872 | tf_op jit(solution)/shard_map/ppermute | solution.py:576
  30.2 22.5 %collective-permute-start.12 = (bf16[1024,256]{1,0:T(8,128)(2,1)S(1)}, bf16[1024,256]{1,0:T(8,128)(2,1)S(1)}, u32[]{:S(2)}, u32[]{:S(2)}) collective-permute-start(bf16[1024,256]{1,0:T(8,128)(2,1)S(1)} %collective-permute-done.11.refs_3_), channel_id=1, source_target_pairs={{1,0},{3,1},{5,3},{7,5},{6,7},{4,6},{2,4},{0,2},{9,8},{11,9},{13,1... | collective-permute-start | bytes 1572872 | tf_op jit(solution)/shard_map/ppermute | solution.py:576
  32.3 15.1 %collective-permute-start.19 = (bf16[1024,256]{1,0:T(8,128)(2,1)}, bf16[1024,256]{1,0:T(8,128)(2,1)S(1)}, u32[]{:S(2)}, u32[]{:S(2)}) collective-permute-start(bf16[1024,256]{1,0:T(8,128)(2,1)} %collective-permute-done.18.refs_1_), channel_id=1, source_target_pairs={{0,1},{1,3},{3,5},{5,7},{7,6},{6,4},{4,2},{2,0},{8,9},{9,11},{11,1... | collective-permute-start | bytes 1572872 | tf_op jit(solution)/shard_map/ppermute | solution.py:576
  32.3 26.3 %collective-permute-start.5 = (bf16[1024,256]{1,0:T(8,128)(2,1)}, bf16[1024,256]{1,0:T(8,128)(2,1)S(1)}, u32[]{:S(2)}, u32[]{:S(2)}) collective-permute-start(bf16[1024,256]{1,0:T(8,128)(2,1)} %collective-permute-done.4.refs_2_), channel_id=1, source_target_pairs={{0,1},{1,3},{3,5},{5,7},{7,6},{6,4},{4,2},{2,0},{8,9},{9,11},{11,1... | collective-permute-start | bytes 1572872 | tf_op jit(solution)/shard_map/ppermute | solution.py:576
  41.4 22.5 %collective-permute-start.25 = (bf16[1024,256]{1,0:T(8,128)(2,1)S(1)}, bf16[1024,256]{1,0:T(8,128)(2,1)S(1)}, u32[]{:S(2)}, u32[]{:S(2)}) collective-permute-start(bf16[1024,256]{1,0:T(8,128)(2,1)S(1)} %collective-permute-done.1.refs_8_), channel_id=1, source_target_pairs={{1,0},{3,1},{5,3},{7,5},{6,7},{4,6},{2,4},{0,2},{9,8},{11,9},{13,1... | collective-permute-start | bytes 1572872 | tf_op jit(solution)/shard_map/ppermute | solution.py:576
  47.4 22.5 %collective-permute-start.20 = (bf16[1024,256]{1,0:T(8,128)(2,1)S(1)}, bf16[1024,256]{1,0:T(8,128)(2,1)S(1)}, u32[]{:S(2)}, u32[]{:S(2)}) collective-permute-start(bf16[1024,256]{1,0:T(8,128)(2,1)S(1)} %collective-permute-done.19.refs_5_), channel_id=1, source_target_pairs={{0,1},{1,3},{3,5},{5,7},{7,6},{6,4},{4,2},{2,0},{8,9},{9,11},{11,1... | collective-permute-start | bytes 1572872 | tf_op jit(solution)/shard_map/ppermute | solution.py:576
  52.7 22.5 %collective-permute-start.13 = (bf16[1024,256]{1,0:T(8,128)(2,1)S(1)}, bf16[1024,256]{1,0:T(8,128)(2,1)S(1)}, u32[]{:S(2)}, u32[]{:S(2)}) collective-permute-start(bf16[1024,256]{1,0:T(8,128)(2,1)S(1)} %collective-permute-done.12.refs_7_), channel_id=1, source_target_pairs={{1,0},{3,1},{5,3},{7,5},{6,7},{4,6},{2,4},{0,2},{9,8},{11,9},{13,1... | collective-permute-start | bytes 1572872 | tf_op jit(solution)/shard_map/ppermute | solution.py:576
  58.6 22.5 %collective-permute-start.6 = (bf16[1024,256]{1,0:T(8,128)(2,1)S(1)}, bf16[1024,256]{1,0:T(8,128)(2,1)S(1)}, u32[]{:S(2)}, u32[]{:S(2)}) collective-permute-start(bf16[1024,256]{1,0:T(8,128)(2,1)S(1)} %collective-permute-done.5.refs_6_), channel_id=1, source_target_pairs={{0,1},{1,3},{3,5},{5,7},{7,6},{6,4},{4,2},{2,0},{8,9},{9,11},{11,1... | collective-permute-start | bytes 1572872 | tf_op jit(solution)/shard_map/ppermute | solution.py:576
  63.9 22.5 %collective-permute-start.26 = (bf16[1024,256]{1,0:T(8,128)(2,1)S(1)}, bf16[1024,256]{1,0:T(8,128)(2,1)S(1)}, u32[]{:S(2)}, u32[]{:S(2)}) collective-permute-start(bf16[1024,256]{1,0:T(8,128)(2,1)S(1)} %collective-permute-done.25.refs_12_), channel_id=1, source_target_pairs={{1,0},{3,1},{5,3},{7,5},{6,7},{4,6},{2,4},{0,2},{9,8},{11,9},{13,1... | collective-permute-start | bytes 1572872 | tf_op jit(solution)/shard_map/ppermute | solution.py:576
  69.9 22.5 %collective-permute-start.21 = (bf16[1024,256]{1,0:T(8,128)(2,1)S(1)}, bf16[1024,256]{1,0:T(8,128)(2,1)S(1)}, u32[]{:S(2)}, u32[]{:S(2)}) collective-permute-start(bf16[1024,256]{1,0:T(8,128)(2,1)S(1)} %collective-permute-done.20.refs_9_), channel_id=1, source_target_pairs={{0,1},{1,3},{3,5},{5,7},{7,6},{6,4},{4,2},{2,0},{8,9},{9,11},{11,1... | collective-permute-start | bytes 1572872 | tf_op jit(solution)/shard_map/ppermute | solution.py:576
  75.1 22.5 %collective-permute-start.14 = (bf16[1024,256]{1,0:T(8,128)(2,1)S(1)}, bf16[1024,256]{1,0:T(8,128)(2,1)S(1)}, u32[]{:S(2)}, u32[]{:S(2)}) collective-permute-start(bf16[1024,256]{1,0:T(8,128)(2,1)S(1)} %collective-permute-done.13.refs_11_), channel_id=1, source_target_pairs={{1,0},{3,1},{5,3},{7,5},{6,7},{4,6},{2,4},{0,2},{9,8},{11,9},{13,1... | collective-permute-start | bytes 1572872 | tf_op jit(solution)/shard_map/ppermute | solution.py:576
  81.1 22.5 %collective-permute-start.7 = (bf16[1024,256]{1,0:T(8,128)(2,1)S(1)}, bf16[1024,256]{1,0:T(8,128)(2,1)S(1)}, u32[]{:S(2)}, u32[]{:S(2)}) collective-permute-start(bf16[1024,256]{1,0:T(8,128)(2,1)S(1)} %collective-permute-done.6.refs_10_), channel_id=1, source_target_pairs={{0,1},{1,3},{3,5},{5,7},{7,6},{6,4},{4,2},{2,0},{8,9},{9,11},{11,1... | collective-permute-start | bytes 1572872 | tf_op jit(solution)/shard_map/ppermute | solution.py:576
  86.4 28.1 %collective-permute-start.27 = (bf16[1024,256]{1,0:T(8,128)(2,1)S(1)}, bf16[1024,256]{1,0:T(8,128)(2,1)S(1)}, u32[]{:S(2)}, u32[]{:S(2)}) collective-permute-start(bf16[1024,256]{1,0:T(8,128)(2,1)S(1)} %collective-permute-done.26.refs_3_), channel_id=1, source_target_pairs={{1,0},{3,1},{5,3},{7,5},{6,7},{4,6},{2,4},{0,2},{9,8},{11,9},{13,1... | collective-permute-start | bytes 1572872 | tf_op jit(solution)/shard_map/ppermute | solution.py:576
  92.3 23.0 %collective-permute-start.22 = (bf16[1024,256]{1,0:T(8,128)(2,1)S(1)}, bf16[1024,256]{1,0:T(8,128)(2,1)S(1)}, u32[]{:S(2)}, u32[]{:S(2)}) collective-permute-start(bf16[1024,256]{1,0:T(8,128)(2,1)S(1)} %collective-permute-done.21.refs_0_), channel_id=1, source_target_pairs={{0,1},{1,3},{3,5},{5,7},{7,6},{6,4},{4,2},{2,0},{8,9},{9,11},{11,1... | collective-permute-start | bytes 1572872 | tf_op jit(solution)/shard_map/ppermute | solution.py:576
  97.6 28.4 %collective-permute-start.15 = (bf16[1024,256]{1,0:T(8,128)(2,1)S(1)}, bf16[1024,256]{1,0:T(8,128)(2,1)S(1)}, u32[]{:S(2)}, u32[]{:S(2)}) collective-permute-start(bf16[1024,256]{1,0:T(8,128)(2,1)S(1)} %collective-permute-done.14.refs_2_), channel_id=1, source_target_pairs={{1,0},{3,1},{5,3},{7,5},{6,7},{4,6},{2,4},{0,2},{9,8},{11,9},{13,1... | collective-permute-start | bytes 1572872 | tf_op jit(solution)/shard_map/ppermute | solution.py:576
  103.6 22.5 %collective-permute-start.8 = (bf16[1024,256]{1,0:T(8,128)(2,1)S(1)}, bf16[1024,256]{1,0:T(8,128)(2,1)S(1)}, u32[]{:S(2)}, u32[]{:S(2)}) collective-permute-start(bf16[1024,256]{1,0:T(8,128)(2,1)S(1)} %collective-permute-done.7.refs_1_), channel_id=1, source_target_pairs={{0,1},{1,3},{3,5},{5,7},{7,6},{6,4},{4,2},{2,0},{8,9},{9,11},{11,1... | collective-permute-start | bytes 1572872 | tf_op jit(solution)/shard_map/ppermute | solution.py:576
  114.5 16.8 %collective-permute-start.28 = (bf16[1024,256]{1,0:T(8,128)(2,1)S(1)}, bf16[1024,256]{1,0:T(8,128)(2,1)S(1)}, u32[]{:S(2)}, u32[]{:S(2)}) collective-permute-start(bf16[1024,256]{1,0:T(8,128)(2,1)S(1)} %collective-permute-done.27.refs_7_), channel_id=1, source_target_pairs={{1,0},{3,1},{5,3},{7,5},{6,7},{4,6},{2,4},{0,2},{9,8},{11,9},{13,1... | collective-permute-start | bytes 1572872 | tf_op jit(solution)/shard_map/ppermute | solution.py:576
  115.3 22.0 %collective-permute-start.23 = (bf16[1024,256]{1,0:T(8,128)(2,1)S(1)}, bf16[1024,256]{1,0:T(8,128)(2,1)S(1)}, u32[]{:S(2)}, u32[]{:S(2)}) collective-permute-start(bf16[1024,256]{1,0:T(8,128)(2,1)S(1)} %collective-permute-done.22.refs_4_), channel_id=1, source_target_pairs={{0,1},{1,3},{3,5},{5,7},{7,6},{6,4},{4,2},{2,0},{8,9},{9,11},{11,1... | collective-permute-start | bytes 1572872 | tf_op jit(solution)/shard_map/ppermute | solution.py:576
  126.0 22.5 %collective-permute-start.9 = (bf16[1024,256]{1,0:T(8,128)(2,1)S(1)}, bf16[1024,256]{1,0:T(8,128)(2,1)S(1)}, u32[]{:S(2)}, u32[]{:S(2)}) collective-permute-start(bf16[1024,256]{1,0:T(8,128)(2,1)S(1)} %collective-permute-done.8.refs_5_), channel_id=1, source_target_pairs={{0,1},{1,3},{3,5},{5,7},{7,6},{6,4},{4,2},{2,0},{8,9},{9,11},{11,1... | collective-permute-start | bytes 1572872 | tf_op jit(solution)/shard_map/ppermute | solution.py:576
  126.0 22.5 %collective-permute-start.16 = (bf16[1024,256]{1,0:T(8,128)(2,1)S(1)}, bf16[1024,256]{1,0:T(8,128)(2,1)S(1)}, u32[]{:S(2)}, u32[]{:S(2)}) collective-permute-start(bf16[1024,256]{1,0:T(8,128)(2,1)S(1)} %collective-permute-done.15.refs_6_), channel_id=1, source_target_pairs={{1,0},{3,1},{5,3},{7,5},{6,7},{4,6},{2,4},{0,2},{9,8},{11,9},{13,1... | collective-permute-start | bytes 1572872 | tf_op jit(solution)/shard_map/ppermute | solution.py:576
  131.3 26.4 %collective-permute-start.29 = (bf16[1024,256]{1,0:T(8,128)(2,1)S(1)}, bf16[1024,256]{1,0:T(8,128)(2,1)S(1)}, u32[]{:S(2)}, u32[]{:S(2)}) collective-permute-start(bf16[1024,256]{1,0:T(8,128)(2,1)S(1)} %collective-permute-done.28.refs_11_), channel_id=1, source_target_pairs={{1,0},{3,1},{5,3},{7,5},{6,7},{4,6},{2,4},{0,2},{9,8},{11,9},{13,1... | collective-permute-start | bytes 1572872 | tf_op jit(solution)/shard_map/ppermute | solution.py:576
  137.3 22.5 %collective-permute-start.24 = (bf16[1024,256]{1,0:T(8,128)(2,1)S(1)}, bf16[1024,256]{1,0:T(8,128)(2,1)S(1)}, u32[]{:S(2)}, u32[]{:S(2)}) collective-permute-start(bf16[1024,256]{1,0:T(8,128)(2,1)S(1)} %collective-permute-done.23.refs_8_), channel_id=1, source_target_pairs={{0,1},{1,3},{3,5},{5,7},{7,6},{6,4},{4,2},{2,0},{8,9},{9,11},{11,1... | collective-permute-start | bytes 1572872 | tf_op jit(solution)/shard_map/ppermute | solution.py:576
  148.5 19.1 %collective-permute-start.10 = (bf16[1024,256]{1,0:T(8,128)(2,1)S(1)}, bf16[1024,256]{1,0:T(8,128)(2,1)S(1)}, u32[]{:S(2)}, u32[]{:S(2)}) collective-permute-start(bf16[1024,256]{1,0:T(8,128)(2,1)S(1)} %collective-permute-done.9.refs_9_), channel_id=1, source_target_pairs={{0,1},{1,3},{3,5},{5,7},{7,6},{6,4},{4,2},{2,0},{8,9},{9,11},{11,1... | collective-permute-start | bytes 1572872 | tf_op jit(solution)/shard_map/ppermute | solution.py:576
  148.5 19.1 %collective-permute-start.17 = (bf16[1024,256]{1,0:T(8,128)(2,1)S(1)}, bf16[1024,256]{1,0:T(8,128)(2,1)S(1)}, u32[]{:S(2)}, u32[]{:S(2)}) collective-permute-start(bf16[1024,256]{1,0:T(8,128)(2,1)S(1)} %collective-permute-done.16.refs_10_), channel_id=1, source_target_pairs={{1,0},{3,1},{5,3},{7,5},{6,7},{4,6},{2,4},{0,2},{9,8},{11,9},{13,1... | collective-permute-start | bytes 1572872 | tf_op jit(solution)/shard_map/ppermute | solution.py:576
  178.6 7.0 %collective-permute-start.37 = (f32[64,256]{1,0:T(8,128)S(1)}, f32[64,256]{1,0:T(8,128)S(1)}, u32[]{:S(2)}, u32[]{:S(2)}) collective-permute-start(f32[64,256]{1,0:T(8,128)S(1)} %maximum_select_fusion), channel_id=1, source_target_pairs={{0,2},{1,3},{2,0},{3,1},{4,6},{5,7},{6,4},{7,5},{8,10},{9,11},{10,... | collective-permute-start | bytes 196616 | tf_op jit(solution)/shard_map/ppermute | solution.py:634
  183.2 9.3 %collective-permute-start.33 = (f32[64,384]{1,0:T(8,128)S(1)}, f32[64,384]{1,0:T(8,128)S(1)}, u32[]{:S(2)}, u32[]{:S(2)}) collective-permute-start(f32[64,384]{1,0:T(8,128)S(1)} %fusion.22), channel_id=1, source_target_pairs={{0,2},{1,3},{2,0},{3,1},{4,6},{5,7},{6,4},{7,5},{8,10},{9,11},{10,... | collective-permute-start | bytes 294920 | tf_op jit(solution)/shard_map/ppermute | solution.py:634
  192.6 6.2 %collective-permute-start.34 = (f32[64,384]{1,0:T(8,128)S(1)}, f32[64,384]{1,0:T(8,128)S(1)}, u32[]{:S(2)}, u32[]{:S(2)}) collective-permute-start(f32[64,384]{1,0:T(8,128)S(1)} %add.118), channel_id=1, source_target_pairs={{0,4},{1,5},{2,6},{3,7},{4,0},{5,1},{6,2},{7,3},{8,12},{9,13},{10,... | collective-permute-start | bytes 294920 | tf_op jit(solution)/shard_map/ppermute | solution.py:634
  (22 other events, 199.5 us)
